TPU v7x, 128 devices: a whole 4x4x4 slice. The times are simulated.
128 devices in a mesh: gy: 16 (over z, y_lo, core), gx: 8 (over y_hi, x).
Axes of the slice: x: 4, y: 4 (y_hi: 2, y_lo: 2; y = y_hi * 2 + y_lo), z: 4, core: 2. Of those that a mesh axis runs over, the one named last changes fastest.
Arguments:
- fine: bfloat16 [128, 96, 768], P('gy', 'gx'), may hold values from -6 to 6
- class_table: bfloat16 [1000, 768], replicated, may hold values from -3 to 3
- label: int32 [1], replicated, may hold values from 0 to 999
- timestep: int32 [1], replicated, may hold values from 0 to 999
- windows: int32 [12], replicated, may hold values from 3 to 7, as said below
- fine_scale: float32 [12], replicated, may hold values from 4 to 400
- fine_qkv: bfloat16 [768, 2304], replicated, may hold values from -0.21875 to 0.21875
- fine_out: bfloat16 [768, 768], replicated, may hold values from -0.21875 to 0.21875
- merge_weight: bfloat16 [3072, 1536], P(('gy', 'gx')), may hold values from -0.109375 to 0.109375
- bottom_scale: float32 [12], replicated, may hold values from 4 to 400
- bottom_qkv: bfloat16 [1536, 2304], replicated, may hold values from -0.15625 to 0.15625
- bottom_out: bfloat16 [768, 1536], replicated, may hold values from -0.21875 to 0.21875
- split_weight: bfloat16 [1536, 3072], P(None, ('gy', 'gx')), may hold values from -0.15625 to 0.15625
- skip_mix: float32 [768], replicated, may hold values from 0.2 to 0.8
Outputs:
- mixed: bfloat16 [128, 96, 768], P('gy', 'gx')
Inputs may be any that keep to these rules, and one draw needn't show every extreme that they name: `windows`: odd window sizes; some head has window 7.
All inputs are finite; a program needn't handle non-finite values.
Results may differ from a plain program's by a relative error of at most 0.034.
Values may be sent and summed in bfloat16 or wider, within the bound.
No kernel may reach another device: no remote copies, remote signals or barrier semaphores. Data moves between devices by JAX's collectives and lax.ppermute only.
A program may use at most 192 MiB of HBM per device.

v0:
```python
import math

import jax
import jax.numpy as jnp
from jax import lax
from jax.sharding import PartitionSpec as P

HEAD_DIM = 64
WIN = 7


EPS = 1e-06


def padded_2(x, sides, width):
    for axis, dim in sides:
        size, length = (lax.axis_size(axis), x.shape[dim])
        up = [(i, (i + 1) % size) for i in range(size - 1)]
        down = [(j, i) for i, j in up]
        last = lax.slice_in_dim(x, length - width, length, axis=dim)
        initial = lax.slice_in_dim(x, 0, width, axis=dim)
        before = lax.ppermute(last, axis, up)
        after = lax.ppermute(initial, axis, down)
        x = jnp.concatenate([before, x, after], axis=dim)
    return x


def time_features(step, width):
    half = width // 2
    freqs = jnp.exp(-math.log(10000.0) * jnp.arange(half, dtype=jnp.float32) / half)
    angles = step[0].astype(jnp.float32) * freqs
    return jnp.concatenate([jnp.cos(angles), jnp.sin(angles)])


def rms_scale(values, gain):
    return values * lax.rsqrt(jnp.mean(values * values, axis=-1, keepdims=True) + EPS) * gain


def unit_heads(values):
    return values * lax.rsqrt(jnp.sum(values * values, axis=-1, keepdims=True) + EPS)


def neighbour_attention(queries, padded, row_start, col_start, rows_all, cols_all, windows, scales):
    height, width, heads, depth = queries.shape
    reach = WIN // 2
    radius = (windows - 1) // 2
    row_pos = row_start + jnp.arange(height, dtype=jnp.int32)
    col_pos = col_start + jnp.arange(width, dtype=jnp.int32)
    scored = []
    for row_off in range(WIN):
        for col_off in range(WIN):
            window = padded[row_off : row_off + height, col_off : col_off + width, : heads * depth]
            keys = window.reshape(height, width, heads, depth).astype(jnp.float32)
            score = scales * jnp.sum(queries * keys, axis=-1)
            shift_row = row_off - reach
            shift_col = col_off - reach
            rows_in = (row_pos + shift_row >= 0) & (row_pos + shift_row < rows_all)
            cols_in = (col_pos + shift_col >= 0) & (col_pos + shift_col < cols_all)
            allowed = (abs(shift_row) <= radius) & (abs(shift_col) <= radius)
            valid = rows_in[:, None, None] & cols_in[None, :, None] & allowed[None, None, :]
            scored.append(jnp.where(valid, score, -jnp.inf))
    stacked = jnp.stack(scored, axis=-1)
    highest = jnp.max(stacked, axis=-1, keepdims=True)
    expd = jnp.exp(stacked - highest)
    weights = expd / jnp.sum(expd, axis=-1, keepdims=True)
    output = jnp.zeros((height, width, heads, depth), jnp.float32)
    for row_off in range(WIN):
        for col_off in range(WIN):
            window = padded[row_off : row_off + height, col_off : col_off + width, heads * depth :]
            values = window.reshape(height, width, heads, depth).astype(jnp.float32)
            output = output + weights[..., row_off * WIN + col_off, None] * values
    return output.reshape(height, width, heads * depth)


def merge_tokens(stream):
    height, width, depth = stream.shape
    blocks = stream.reshape(height // 2, 2, width // 2, 2, depth).transpose(0, 2, 1, 3, 4)
    return blocks.reshape(height // 2 * (width // 2), 4 * depth)


def split_tokens(split, height, width):
    depth = split.shape[1] // 4
    blocks = split.reshape(height // 2, width // 2, 2, 2, depth).transpose(0, 2, 1, 3, 4)
    return blocks.reshape(height, width, depth)


def shards(
    fine,
    class_table,
    label,
    timestep,
    windows,
    fine_scale,
    fine_qkv,
    fine_out,
    merge_weight,
    bottom_scale,
    bottom_qkv,
    bottom_out,
    split_weight,
    skip_mix,
):
    height, width, depth = fine.shape
    heads = depth // HEAD_DIM
    row = lax.dynamic_slice_in_dim(class_table, label[0], 1, 0)[0].astype(jnp.float32)
    gain = 1.0 + 0.5 * (row + time_features(timestep, depth))
    xfull = fine.astype(jnp.float32)
    normed = rms_scale(xfull, gain).astype(jnp.bfloat16)
    proj = jnp.dot(normed.reshape(-1, depth), fine_qkv, preferred_element_type=jnp.float32)
    queries = unit_heads(proj[:, :depth].reshape(height, width, heads, HEAD_DIM))
    keys = unit_heads(proj[:, depth : 2 * depth].reshape(height, width, heads, HEAD_DIM))
    keys = keys.astype(jnp.bfloat16).reshape(height, width, depth)
    values = proj[:, 2 * depth :].astype(jnp.bfloat16).reshape(height, width, depth)
    packed = jnp.concatenate([keys, values], axis=-1)
    padded = padded_2(packed, (("gy", 0), ("gx", 1)), WIN // 2)
    row_start = lax.axis_index("gy") * height
    col_start = lax.axis_index("gx") * width
    rows_all = height * lax.axis_size("gy")
    cols_all = width * lax.axis_size("gx")
    attended = neighbour_attention(
        queries, padded, row_start, col_start, rows_all, cols_all, windows, fine_scale
    ).astype(jnp.bfloat16)
    update = jnp.dot(attended.reshape(-1, depth), fine_out, preferred_element_type=jnp.float32)
    stream = (xfull + update.reshape(height, width, depth)).astype(jnp.bfloat16)
    merged = merge_tokens(stream)
    bottom_sum = jnp.dot(
        merged,
        lax.all_gather(merge_weight, ("gy", "gx"), axis=0, tiled=True),
        preferred_element_type=jnp.float32,
    )
    bottom = bottom_sum.astype(jnp.bfloat16)
    bfull = bottom.astype(jnp.float32)
    bnormed = rms_scale(bfull, 1.0).astype(jnp.bfloat16)
    bproj = jnp.dot(bnormed, bottom_qkv, preferred_element_type=jnp.float32)
    count = bproj.shape[0]
    bheads = bottom_scale.shape[0]
    battn = bheads * HEAD_DIM
    bquery = unit_heads(bproj[:, :battn].reshape(count, bheads, HEAD_DIM))
    bkey = (
        unit_heads(bproj[:, battn : 2 * battn].reshape(count, bheads, HEAD_DIM))
        .astype(jnp.bfloat16)
        .reshape(count, battn)
    )
    bvalue = bproj[:, 2 * battn :].astype(jnp.bfloat16)
    highest = jnp.full((count, bheads), -jnp.inf, jnp.float32)
    total = jnp.zeros((count, bheads), jnp.float32)
    accum = jnp.zeros((count, bheads, HEAD_DIM), jnp.float32)
    key_piece = lax.all_gather(bkey, ("gy", "gx"), axis=0, tiled=True)
    value_piece = lax.all_gather(bvalue, ("gy", "gx"), axis=0, tiled=True)
    rows = key_piece.shape[0]
    key_heads = key_piece.reshape(rows, bheads, HEAD_DIM).astype(jnp.float32)
    value_heads = value_piece.reshape(rows, bheads, HEAD_DIM).astype(jnp.float32)
    score = bottom_scale[None, :, None] * jnp.einsum(
        "qhe,khe->qhk", bquery, key_heads, precision=lax.Precision.HIGHEST
    )
    new_high = jnp.max(score, axis=-1)
    fade = jnp.exp(highest - new_high)
    expd = jnp.exp(score - new_high[..., None])
    total = total * fade + jnp.sum(expd, axis=-1)
    accum = accum * fade[..., None] + jnp.einsum(
        "qhk,khe->qhe", expd, value_heads, precision=lax.Precision.HIGH
    )
    highest, total, accum = (new_high, total, accum)
    batt = (accum / total[..., None]).reshape(count, battn).astype(jnp.bfloat16)
    bstream = (bfull + jnp.dot(batt, bottom_out, preferred_element_type=jnp.float32)).astype(
        jnp.bfloat16
    )
    split = jnp.dot(
        bstream,
        lax.all_gather(split_weight, ("gy", "gx"), axis=1, tiled=True),
        preferred_element_type=jnp.float32,
    )
    upward = split_tokens(split, height, width)
    sfull = stream.astype(jnp.float32)
    return (sfull + skip_mix * (upward - sfull)).astype(jnp.bfloat16)


def solution(mesh):
    placed = (
        P("gy", "gx", None),
        P(),
        P(),
        P(),
        P(),
        P(),
        P(),
        P(),
        P(("gy", "gx"), None),
        P(),
        P(),
        P(),
        P(None, ("gy", "gx")),
        P(),
    )
    return jax.shard_map(
        shards, mesh=mesh, in_specs=placed, out_specs=P("gy", "gx", None), check_vma=False
    )
```

profile of v0, /device:TPU:0, one launch (start us, length us, event | category | flops | bytes accessed | tf_op | source)
XLA Modules:
  0.0 1329.3 jit_solution(17495931956270703775)
XLA Ops:
  10.0 1.7 fusion.70
  27.4 4.6 collective-permute-start.2
  34.7 2.0 reshape.2789
  36.8 2.1 reshape.2796
  38.8 2.0 reshape.2803
  41.7 2.0 reshape.2776
  43.8 2.1 reshape.2762
  48.5 2.4 slice_convert_fusion.30
  50.9 2.0 reshape.2790
  52.9 2.0 reshape.2791
  55.0 2.1 reshape.2792
  57.0 2.5 slice_convert_fusion.34
  59.5 2.1 reshape.2793
  61.5 2.0 reshape.2794
  63.6 2.1 reshape.2795
  65.7 2.1 reshape.2797
  67.7 2.0 reshape.2798
  69.8 2.0 reshape.2799
  71.8 2.0 reshape.2800
  73.8 2.1 reshape.2801
  75.9 2.0 reshape.2802
  77.9 2.0 reshape.2804
  80.0 2.0 reshape.2805
  82.0 2.0 reshape.2806
  84.1 2.1 reshape.2773
  86.1 2.0 reshape.2774
  88.2 2.0 reshape.2775
  90.2 2.0 reshape.2777
  92.2 2.1 reshape.2778
  94.3 2.1 reshape.2779
  96.4 2.0 reshape.2780
  98.4 2.0 reshape.2781
  100.4 2.0 reshape.2782
  102.5 2.1 reshape.2783
  104.6 2.0 reshape.2784
  106.6 2.0 reshape.2785
  108.6 2.0 reshape.2786
  110.7 2.0 reshape.2787
  112.7 2.1 reshape.2788
  114.9 11.6 fusion.17
  126.7 5.0 fusion.35
  137.8 1.7 copy.1197
  146.7 1.7 copy.1204
  154.1 2.1 reshape.2761
  157.3 2.0 reshape.2766
  169.3 7.9 fusion.52
  187.5 1.7 copy.1192
  257.3 3.1 select_maximum_fusion
  264.5 2.3 fusion.142
  326.1 1.8 fusion.143
  342.1 6.9 add_convert_fusion
  349.7 5.1 multiply_reduce_fusion.4
  354.8 4.1 fusion.75
  362.4 312.7 %all-gather.7.cloned.1.call-done = bf16[3072,768]{1,0:T(8,128)(2,1)} async-done(((bf16[24,768]{1,0:T(8,128)(2,1)}), bf16[3072,768]{1,0:T(8,128)(2,1)}) %all-gather.7.cloned.1.call-update) | async-done | bytes 4718608 | tf_op jit(solution)/shard_map/all_gather | solution.py:148
  675.1 6.6 copy.1170
  681.7 304.7 %all-gather.9.cloned.1.call-done = bf16[3072,768]{1,0:T(8,128)(2,1)} async-done(((bf16[24,768]{1,0:T(8,128)(2,1)}), bf16[3072,768]{1,0:T(8,128)(2,1)}) %all-gather.9.cloned.1.call-update) | async-done | bytes 4718608 | tf_op jit(solution)/shard_map/all_gather | solution.py:149
  986.4 6.7 copy.1172
  993.1 4.1 fusion.146
  997.9 2.7 fusion.15
  1001.3 305.4 %all-gather.11.cloned.1.call-done = bf16[1536,3072]{0,1:T(8,128)(2,1)} async-done(((bf16[1536,24]{0,1:T(8,128)(2,1)}), bf16[1536,3072]{0,1:T(8,128)(2,1)}) %all-gather.11.cloned.1.call-update) | async-done | bytes 9437200 | tf_op jit(solution)/shard_map/all_gather | solution.py:170
  1306.7 8.2 fusion.16
  1314.9 1.9 reshape.2756
  1316.8 1.8 copy.1445
  1318.6 1.9 reshape.2757
  (555 shorter events, 215.4 us)
Async XLA Ops:
  6.5 343.1 %all-gather.5.cloned.1.call-start = ((), (), s32[]{:S(2)}) async-start(), calls=%async_computation | async-start | bytes 9510912 | tf_op jit(solution)/shard_map/all_gather | solution.py:128
  18.5 8.0 collective-permute-start
  19.8 6.7 collective-permute-start.1
  21.1 654.0 %all-gather.7.cloned.1.call-start = ((), (), s32[]{:S(2)}) async-start(), calls=%async_computation.1 | async-start | bytes 4755456 | tf_op jit(solution)/shard_map/all_gather | solution.py:148
  27.4 19.6 %collective-permute-start.2 = (bf16[14,3,1536]{2,0,1:T(8,128)(2,1)}, bf16[14,3,1536]{2,0,1:T(8,128)(2,1)}, u32[]{:S(2)}, u32[]{:S(2)}) collective-permute-start(bf16[14,3,1536]{2,0,1:T(8,128)(2,1)} %get-tuple-element.158), channel_id=1, source_target_pairs={{0,1},{1,2},{2,3},{3,4},{4,5},{5,6},{6,7},{8,9},{9,10},{10,11},{11... | collective-permute-start | bytes 387080 | tf_op jit(solution)/shard_map/ppermute | solution.py:22
  32.0 15.0 %collective-permute-start.3 = (bf16[14,3,1536]{2,0,1:T(8,128)(2,1)}, bf16[14,3,1536]{2,0,1:T(8,128)(2,1)}, u32[]{:S(2)}, u32[]{:S(2)}) collective-permute-start(bf16[14,3,1536]{2,0,1:T(8,128)(2,1)} %get-tuple-element.159), channel_id=1, source_target_pairs={{1,0},{2,1},{3,2},{4,3},{5,4},{6,5},{7,6},{9,8},{10,9},{11,10},{12... | collective-permute-start | bytes 387080 | tf_op jit(solution)/shard_map/ppermute | solution.py:23
  131.7 24.5 %copy-start.37 = (f32[8,12,768]{2,0,1:T(8,128)S(1)}, f32[8,12,768]{2,0,1:T(8,128)}, u32[]{:S(2)}) copy-start(f32[8,12,768]{2,0,1:T(8,128)} %get-tuple-element.145) | copy-start | bytes 884740
  131.7 27.6 %copy-start.39 = (f32[8,12,768]{2,0,1:T(8,128)S(1)}, f32[8,12,768]{2,0,1:T(8,128)}, u32[]{:S(2)}) copy-start(f32[8,12,768]{2,0,1:T(8,128)} %get-tuple-element.124) | copy-start | bytes 884740
  177.2 41.9 %copy-start.34 = (f32[12]{0:T(128)S(1)}, f32[12]{0:T(128)}, u32[]{:S(2)}) copy-start(f32[12]{0:T(128)} %param.19) | copy-start | bytes 148
  177.2 41.9 %copy-start.86 = (pred[12]{0:T(512)(128)(4,1)S(1)}, pred[12]{0:T(512)(128)(4,1)}, u32[]{:S(2)}) copy-start(pred[12]{0:T(512)(128)(4,1)} %get-tuple-element.225) | copy-start | bytes 40
  177.2 41.9 %copy-start.101 = (pred[8,12]{1,0:T(8,128)(4,1)S(1)}, pred[8,12]{1,0:T(8,128)(4,1)}, u32[]{:S(2)}) copy-start(pred[8,12]{1,0:T(8,128)(4,1)} %get-tuple-element.210) | copy-start | bytes 292
  177.2 42.0 %copy-start.102 = (pred[8,12]{1,0:T(8,128)(4,1)S(1)}, pred[8,12]{1,0:T(8,128)(4,1)}, u32[]{:S(2)}) copy-start(pred[8,12]{1,0:T(8,128)(4,1)} %get-tuple-element.215) | copy-start | bytes 292
  177.2 43.2 %copy-start.84 = (pred[12]{0:T(512)(128)(4,1)S(1)}, pred[12]{0:T(512)(128)(4,1)}, u32[]{:S(2)}) copy-start(pred[12]{0:T(512)(128)(4,1)} %get-tuple-element.222) | copy-start | bytes 40
  177.2 46.9 %copy-start.85 = (pred[12]{0:T(512)(128)(4,1)S(1)}, pred[12]{0:T(512)(128)(4,1)}, u32[]{:S(2)}) copy-start(pred[12]{0:T(512)(128)(4,1)} %get-tuple-element.224) | copy-start | bytes 40
  178.3 47.3 %copy-start.83 = (pred[12]{0:T(512)(128)(4,1)S(1)}, pred[12]{0:T(512)(128)(4,1)}, u32[]{:S(2)}) copy-start(pred[12]{0:T(512)(128)(4,1)} %get-tuple-element.220) | copy-start | bytes 40
  182.6 46.9 %copy-start.41 = (f32[8,12,12]{2,1,0:T(8,128)S(1)}, f32[8,12,12]{2,1,0:T(8,128)}, u32[]{:S(2)}) copy-start(f32[8,12,12]{2,1,0:T(8,128)} %copy.1194) | copy-start | bytes 13828
  182.6 47.7 %copy-start.42 = (f32[8,12,12]{2,1,0:T(8,128)S(1)}, f32[8,12,12]{2,1,0:T(8,128)}, u32[]{:S(2)}) copy-start(f32[8,12,12]{2,1,0:T(8,128)} %copy.1195) | copy-start | bytes 13828
  182.6 47.7 %copy-start.82 = (pred[12]{0:T(512)(128)(4,1)S(1)}, pred[12]{0:T(512)(128)(4,1)}, u32[]{:S(2)}) copy-start(pred[12]{0:T(512)(128)(4,1)} %get-tuple-element.219) | copy-start | bytes 40
  182.8 48.3 %copy-start.43 = (f32[8,12,12]{2,1,0:T(8,128)S(1)}, f32[8,12,12]{2,1,0:T(8,128)}, u32[]{:S(2)}) copy-start(f32[8,12,12]{2,1,0:T(8,128)} %copy.1196) | copy-start | bytes 13828
  183.9 48.0 %copy-start.44 = (f32[8,12,12]{2,1,0:T(8,128)S(1)}, f32[8,12,12]{2,1,0:T(8,128)}, u32[]{:S(2)}) copy-start(f32[8,12,12]{2,1,0:T(8,128)} %copy.1197) | copy-start | bytes 13828
  184.0 48.6 %copy-start.45 = (f32[8,12,12]{2,1,0:T(8,128)S(1)}, f32[8,12,12]{2,1,0:T(8,128)}, u32[]{:S(2)}) copy-start(f32[8,12,12]{2,1,0:T(8,128)} %copy.1198) | copy-start | bytes 13828
  185.1 48.3 %copy-start.46 = (f32[8,12,12]{2,1,0:T(8,128)S(1)}, f32[8,12,12]{2,1,0:T(8,128)}, u32[]{:S(2)}) copy-start(f32[8,12,12]{2,1,0:T(8,128)} %copy.1199) | copy-start | bytes 13828
  185.1 49.1 %copy-start.47 = (f32[8,12,12]{2,1,0:T(8,128)S(1)}, f32[8,12,12]{2,1,0:T(8,128)}, u32[]{:S(2)}) copy-start(f32[8,12,12]{2,1,0:T(8,128)} %copy.1200) | copy-start | bytes 13828
  185.3 49.7 %copy-start.48 = (f32[8,12,12]{2,1,0:T(8,128)S(1)}, f32[8,12,12]{2,1,0:T(8,128)}, u32[]{:S(2)}) copy-start(f32[8,12,12]{2,1,0:T(8,128)} %copy.1201) | copy-start | bytes 13828
  186.4 49.4 %copy-start.49 = (f32[8,12,12]{2,1,0:T(8,128)S(1)}, f32[8,12,12]{2,1,0:T(8,128)}, u32[]{:S(2)}) copy-start(f32[8,12,12]{2,1,0:T(8,128)} %copy.1202) | copy-start | bytes 13828
  187.5 49.8 %copy-start.57 = (f32[8,12,12]{2,1,0:T(8,128)}, f32[8,12,12]{2,1,0:T(8,128)S(1)}, u32[]{:S(2)}) copy-start(f32[8,12,12]{2,1,0:T(8,128)S(1)} %copy.1191) | copy-start | bytes 13828
  187.5 49.1 %copy-start.50 = (f32[8,12,12]{2,1,0:T(8,128)S(1)}, f32[8,12,12]{2,1,0:T(8,128)}, u32[]{:S(2)}) copy-start(f32[8,12,12]{2,1,0:T(8,128)} %copy.1203) | copy-start | bytes 13828
  189.2 48.1 %copy-start.51 = (f32[8,12,12]{2,1,0:T(8,128)S(1)}, f32[8,12,12]{2,1,0:T(8,128)}, u32[]{:S(2)}) copy-start(f32[8,12,12]{2,1,0:T(8,128)} %copy.1204) | copy-start | bytes 13828
  190.9 47.2 %copy-start.52 = (f32[8,12,12]{2,1,0:T(8,128)S(1)}, f32[8,12,12]{2,1,0:T(8,128)}, u32[]{:S(2)}) copy-start(f32[8,12,12]{2,1,0:T(8,128)} %copy.1205) | copy-start | bytes 13828
  190.9 48.0 %copy-start.53 = (f32[8,12,12]{2,1,0:T(8,128)S(1)}, f32[8,12,12]{2,1,0:T(8,128)}, u32[]{:S(2)}) copy-start(f32[8,12,12]{2,1,0:T(8,128)} %copy.1206) | copy-start | bytes 13828
  192.6 47.1 %copy-start.54 = (f32[8,12,12]{2,1,0:T(8,128)S(1)}, f32[8,12,12]{2,1,0:T(8,128)}, u32[]{:S(2)}) copy-start(f32[8,12,12]{2,1,0:T(8,128)} %copy.1207) | copy-start | bytes 13828
  194.2 46.1 %copy-start.55 = (f32[8,12,12]{2,1,0:T(8,128)S(1)}, f32[8,12,12]{2,1,0:T(8,128)}, u32[]{:S(2)}) copy-start(f32[8,12,12]{2,1,0:T(8,128)} %copy.1208) | copy-start | bytes 13828
  195.9 45.2 %copy-start.56 = (f32[8,12,12]{2,1,0:T(8,128)S(1)}, f32[8,12,12]{2,1,0:T(8,128)}, u32[]{:S(2)}) copy-start(f32[8,12,12]{2,1,0:T(8,128)} %copy.1209) | copy-start | bytes 13828
  219.1 37.7 %copy-start.76 = (f32[8,12,12]{2,1,0:T(8,128)S(1)}, f32[8,12,12]{2,1,0:T(8,128)}, u32[]{:S(2)}) copy-start(f32[8,12,12]{2,1,0:T(8,128)} %copy.1226) | copy-start | bytes 13828
  219.2 37.7 %copy-start.77 = (f32[8,12,12]{2,1,0:T(8,128)S(1)}, f32[8,12,12]{2,1,0:T(8,128)}, u32[]{:S(2)}) copy-start(f32[8,12,12]{2,1,0:T(8,128)} %copy.1227) | copy-start | bytes 13828
  219.3 37.7 %copy-start.59 = (f32[8,12,12]{2,1,0:T(8,128)S(1)}, f32[8,12,12]{2,1,0:T(8,128)}, u32[]{:S(2)}) copy-start(f32[8,12,12]{2,1,0:T(8,128)} %copy.1192) | copy-start | bytes 13828
  219.3 37.7 %copy-start.60 = (f32[8,12,12]{2,1,0:T(8,128)S(1)}, f32[8,12,12]{2,1,0:T(8,128)}, u32[]{:S(2)}) copy-start(f32[8,12,12]{2,1,0:T(8,128)} %copy.1210) | copy-start | bytes 13828
  219.3 37.7 %copy-start.61 = (f32[8,12,12]{2,1,0:T(8,128)S(1)}, f32[8,12,12]{2,1,0:T(8,128)}, u32[]{:S(2)}) copy-start(f32[8,12,12]{2,1,0:T(8,128)} %copy.1211) | copy-start | bytes 13828
  219.3 37.7 %copy-start.62 = (f32[8,12,12]{2,1,0:T(8,128)S(1)}, f32[8,12,12]{2,1,0:T(8,128)}, u32[]{:S(2)}) copy-start(f32[8,12,12]{2,1,0:T(8,128)} %copy.1212) | copy-start | bytes 13828
  219.3 37.7 %copy-start.63 = (f32[8,12,12]{2,1,0:T(8,128)S(1)}, f32[8,12,12]{2,1,0:T(8,128)}, u32[]{:S(2)}) copy-start(f32[8,12,12]{2,1,0:T(8,128)} %copy.1213) | copy-start | bytes 13828
  219.4 37.7 %copy-start.64 = (f32[8,12,12]{2,1,0:T(8,128)S(1)}, f32[8,12,12]{2,1,0:T(8,128)}, u32[]{:S(2)}) copy-start(f32[8,12,12]{2,1,0:T(8,128)} %copy.1214) | copy-start | bytes 13828
  219.4 37.7 %copy-start.65 = (f32[8,12,12]{2,1,0:T(8,128)S(1)}, f32[8,12,12]{2,1,0:T(8,128)}, u32[]{:S(2)}) copy-start(f32[8,12,12]{2,1,0:T(8,128)} %copy.1215) | copy-start | bytes 13828
  219.4 37.7 %copy-start.66 = (f32[8,12,12]{2,1,0:T(8,128)S(1)}, f32[8,12,12]{2,1,0:T(8,128)}, u32[]{:S(2)}) copy-start(f32[8,12,12]{2,1,0:T(8,128)} %copy.1216) | copy-start | bytes 13828
  219.4 37.7 %copy-start.67 = (f32[8,12,12]{2,1,0:T(8,128)S(1)}, f32[8,12,12]{2,1,0:T(8,128)}, u32[]{:S(2)}) copy-start(f32[8,12,12]{2,1,0:T(8,128)} %copy.1217) | copy-start | bytes 13828
  219.4 37.7 %copy-start.68 = (f32[8,12,12]{2,1,0:T(8,128)S(1)}, f32[8,12,12]{2,1,0:T(8,128)}, u32[]{:S(2)}) copy-start(f32[8,12,12]{2,1,0:T(8,128)} %copy.1218) | copy-start | bytes 13828
  219.4 37.7 %copy-start.69 = (f32[8,12,12]{2,1,0:T(8,128)S(1)}, f32[8,12,12]{2,1,0:T(8,128)}, u32[]{:S(2)}) copy-start(f32[8,12,12]{2,1,0:T(8,128)} %copy.1219) | copy-start | bytes 13828
  219.4 37.7 %copy-start.70 = (f32[8,12,12]{2,1,0:T(8,128)S(1)}, f32[8,12,12]{2,1,0:T(8,128)}, u32[]{:S(2)}) copy-start(f32[8,12,12]{2,1,0:T(8,128)} %copy.1220) | copy-start | bytes 13828
  219.4 37.7 %copy-start.71 = (f32[8,12,12]{2,1,0:T(8,128)S(1)}, f32[8,12,12]{2,1,0:T(8,128)}, u32[]{:S(2)}) copy-start(f32[8,12,12]{2,1,0:T(8,128)} %copy.1221) | copy-start | bytes 13828
  219.4 37.7 %copy-start.72 = (f32[8,12,12]{2,1,0:T(8,128)S(1)}, f32[8,12,12]{2,1,0:T(8,128)}, u32[]{:S(2)}) copy-start(f32[8,12,12]{2,1,0:T(8,128)} %copy.1222) | copy-start | bytes 13828
  219.4 37.7 %copy-start.73 = (f32[8,12,12]{2,1,0:T(8,128)S(1)}, f32[8,12,12]{2,1,0:T(8,128)}, u32[]{:S(2)}) copy-start(f32[8,12,12]{2,1,0:T(8,128)} %copy.1223) | copy-start | bytes 13828
  219.5 37.7 %copy-start.74 = (f32[8,12,12]{2,1,0:T(8,128)S(1)}, f32[8,12,12]{2,1,0:T(8,128)}, u32[]{:S(2)}) copy-start(f32[8,12,12]{2,1,0:T(8,128)} %copy.1224) | copy-start | bytes 13828
  219.5 37.7 %copy-start.75 = (f32[8,12,12]{2,1,0:T(8,128)S(1)}, f32[8,12,12]{2,1,0:T(8,128)}, u32[]{:S(2)}) copy-start(f32[8,12,12]{2,1,0:T(8,128)} %copy.1225) | copy-start | bytes 13828
  221.1 35.8 %copy-start.87 = (pred[8,12]{1,0:T(8,128)(4,1)S(1)}, pred[8,12]{1,0:T(8,128)(4,1)}, u32[]{:S(2)}) copy-start(pred[8,12]{1,0:T(8,128)(4,1)} %get-tuple-element.168) | copy-start | bytes 292
  224.8 28.2 %copy-start.88 = (pred[8,12]{1,0:T(8,128)(4,1)S(1)}, pred[8,12]{1,0:T(8,128)(4,1)}, u32[]{:S(2)}) copy-start(pred[8,12]{1,0:T(8,128)(4,1)} %get-tuple-element.169) | copy-start | bytes 292
  226.4 30.8 %copy-start.89 = (pred[8,12]{1,0:T(8,128)(4,1)S(1)}, pred[8,12]{1,0:T(8,128)(4,1)}, u32[]{:S(2)}) copy-start(pred[8,12]{1,0:T(8,128)(4,1)} %get-tuple-element.170) | copy-start | bytes 292
  230.3 26.9 %copy-start.90 = (pred[8,12]{1,0:T(8,128)(4,1)S(1)}, pred[8,12]{1,0:T(8,128)(4,1)}, u32[]{:S(2)}) copy-start(pred[8,12]{1,0:T(8,128)(4,1)} %get-tuple-element.171) | copy-start | bytes 292
  231.1 25.7 %copy-start.92 = (pred[8,12]{1,0:T(8,128)(4,1)S(1)}, pred[8,12]{1,0:T(8,128)(4,1)}, u32[]{:S(2)}) copy-start(pred[8,12]{1,0:T(8,128)(4,1)} %get-tuple-element.173) | copy-start | bytes 292
  231.1 26.1 %copy-start.91 = (pred[8,12]{1,0:T(8,128)(4,1)S(1)}, pred[8,12]{1,0:T(8,128)(4,1)}, u32[]{:S(2)}) copy-start(pred[8,12]{1,0:T(8,128)(4,1)} %get-tuple-element.172) | copy-start | bytes 292
  231.9 25.3 %copy-start.93 = (pred[8,12]{1,0:T(8,128)(4,1)S(1)}, pred[8,12]{1,0:T(8,128)(4,1)}, u32[]{:S(2)}) copy-start(pred[8,12]{1,0:T(8,128)(4,1)} %get-tuple-element.174) | copy-start | bytes 292
  232.6 24.6 %copy-start.94 = (pred[8,12]{1,0:T(8,128)(4,1)S(1)}, pred[8,12]{1,0:T(8,128)(4,1)}, u32[]{:S(2)}) copy-start(pred[8,12]{1,0:T(8,128)(4,1)} %get-tuple-element.175) | copy-start | bytes 292
  360.1 626.3 %all-gather.9.cloned.1.call-start = ((), (), s32[]{:S(2)}) async-start(), calls=%async_computation.2 | async-start | bytes 4755456 | tf_op jit(solution)/shard_map/all_gather | solution.py:149
  360.8 945.9 %all-gather.11.cloned.1.call-start = ((), (), s32[]{:S(2)}) async-start(), calls=%async_computation.3 | async-start | bytes 9510912 | tf_op jit(solution)/shard_map/all_gather | solution.py:170
  681.7 311.4 %copy-start.104 = (f32[12]{0:T(128)S(1)}, f32[12]{0:T(128)}, u32[]{:S(2)}) copy-start(f32[12]{0:T(128)} %param.23) | copy-start | bytes 148
  1001.3 319.2 %copy-start.103 = (f32[768]{0:T(1024)S(1)}, f32[768]{0:T(1024)}, u32[]{:S(2)}) copy-start(f32[768]{0:T(1024)} %param.27) | copy-start | bytes 9220
  (52 other events, 574.5 us)
Sparse Core Ops, SparseCore 0:
  21.2 323.1 all-gather.4
  360.2 314.8 all-gather.6
  676.8 309.5 all-gather.8
  987.9 318.7 all-gather.10
where the time goes:
time: 1340 us; the launch traced here: 1330 us
  waiting for transfers between devices  923 us (69%)
  local copies, waits for them, and re-layouts  262 us (20%)
  other arithmetic  92 us (7%)
  matrix products  26.2 us (2%)
  between operations  17.4 us (1%)
    all_gather x1, waiting for transfers between devices, shards(): key_piece = lax.all_gather(bkey, ('gy', 'gx'), axis=0, tiled=True)  313 us
    all_gather x1, waiting for transfers between devices, shards(): lax.all_gather(split_weight, ('gy', 'gx'), axis=1, tiled=True)  305 us
    all_gather x1, waiting for transfers between devices, shards(): value_piece = lax.all_gather(bvalue, ('gy', 'gx'), axis=0, tiled=True)  305 us
    convert_element_type x48, local copies, waits for them, and re-layouts, neighbour_attention(): keys = window.reshape(height, width, heads, depth).astype(jnp.float32)  87.8 us
    unnamed x266, local copies, waits for them, and re-layouts  66.4 us
    mul x98, local copies, waits for them, and re-layouts, neighbour_attention(): output = output + weights[..., row_off * WIN + col_off, None] * values  58.6 us
    unnamed x49, other arithmetic  36.8 us
  transfers between devices with their start and end apart: 8, of which 3 were waited for; matrix products, arithmetic and copies ran while one was open for 26% of the time, Pallas kernels for 0%

commit v1 on v0

v1 whole, which is shorter than its diff:
```python
import math

import jax
import jax.numpy as jnp
import numpy as np
from jax import lax
from jax.experimental import pallas as pl
from jax.experimental.pallas import tpu as pltpu
from jax.sharding import Mesh, PartitionSpec as P

HEAD_DIM = 64
WIN = 7
REACH = WIN // 2
EPS = 1e-06
ROWS, COLS = 8, 12
OWN = ROWS * COLS
TOKENS = OWN // 4
KEYS = 256
FAR = 1000
BF16 = jnp.bfloat16
F32 = jnp.float32

ALL = ("z", "yl", "c", "yh", "x")
GY = ("z", "yl", "c")
GX = ("yh", "x")
ZY = ("z", "yl", "yh")
NX = 4

VMEM_LIMIT = 40 * 2**20


def key_places():
    places = []
    for s in range(4):
        for t in range(TOKENS):
            places.append((2 * (t // 6) + s // 2, 2 * (t % 6) + s % 2))
    for r in (-3, -2, -1, 8, 9, 10):
        for c in range(COLS):
            places.append((r, c))
    for cols in ((-3, -2, -1), (12, 13, 14)):
        for r in range(-3, ROWS + 3):
            for c in cols:
                places.append((r, c))
    places += [(FAR, FAR)] * (KEYS - len(places))
    return np.array(places, np.int32)


PLACES = key_places()


def own_to_grid():
    matrix = np.zeros((16 * ROWS, OWN), np.float32)
    for i in range(OWN):
        r, c = PLACES[i]
        matrix[16 * r + c, i] = 1.0
    return matrix


def block_ones():
    return np.kron(np.eye(4), np.ones((HEAD_DIM, HEAD_DIM))).astype(np.float32)


def dot(a, b):
    return jnp.dot(a, b, preferred_element_type=F32)


def dot_t(a, b):
    return lax.dot_general(a, b, (((1,), (1,)), ((), ())), preferred_element_type=F32)


def split_hi_lo(values):
    hi = values.astype(BF16)
    lo = (values - hi.astype(F32)).astype(BF16)
    return hi, lo


def unit_quad(values, ones):
    hi, lo = split_hi_lo(values * values)
    total = dot(hi, ones) + dot(lo, ones)
    return values * lax.rsqrt(total + EPS)


def full(shape):
    return pl.BlockSpec(memory_space=pltpu.VMEM)


def smem():
    return pl.BlockSpec(memory_space=pltpu.SMEM)


def call(body, out_shape, args, in_smem, scratch=(), flops=0, nbytes=0):
    return pl.pallas_call(
        body,
        out_shape=out_shape,
        in_specs=[smem() if i in in_smem else full(None) for i in range(len(args))],
        out_specs=jax.tree.map(lambda _: full(None), out_shape),
        scratch_shapes=list(scratch),
        compiler_params=pltpu.CompilerParams(vmem_limit_bytes=VMEM_LIMIT),
        cost_estimate=pl.CostEstimate(flops=flops, bytes_accessed=nbytes, transcendentals=0),
    )(*args)


def fine_kernel(
    start, windows, scales, own, halo, gain, key_place, query_place, ones, qkv, out_w,
    stream,
):
    width = own.shape[1]

    def normed(ref):
        x = ref[...].astype(F32)
        mean = jnp.mean(x * x, axis=-1, keepdims=True)
        return x, (x * lax.rsqrt(mean + EPS) * gain[...]).astype(BF16)

    x_own, n_own = normed(own)
    _, n_halo = normed(halo)
    n_all = jnp.concatenate([n_own, n_halo], axis=0)

    row_k, col_k = key_place[0:1, :], key_place[1:2, :]
    row_q, col_q = query_place[:, 0:1], query_place[:, 1:2]
    row_g, col_g = row_k + start[0], col_k + start[1]
    inside = (row_g >= 0) & (row_g < start[2]) & (col_g >= 0) & (col_g < start[3])
    apart = jnp.maximum(jnp.abs(row_k - row_q), jnp.abs(col_k - col_q))
    apart = jnp.where(inside, apart, FAR)
    lane = lax.broadcasted_iota(jnp.int32, (OWN, 256), 1) // HEAD_DIM

    update = jnp.zeros((OWN, width), F32)
    for quad in range(width // 256):
        at = quad * 256
        query = unit_quad(dot(n_own, qkv[:, at : at + 256]), ones[...])
        key = unit_quad(dot(n_all, qkv[:, width + at : width + at + 256]), ones[...]).astype(BF16)
        value = dot(n_all, qkv[:, 2 * width + at : 2 * width + at + 256]).astype(BF16)
        hi, lo = split_hi_lo(query)
        rows = [jnp.where(lane == h, hi, 0) for h in range(4)]
        rows += [jnp.where(lane == h, lo, 0) for h in range(4)]
        score = dot_t(jnp.concatenate(rows, axis=0), key)
        score = score[: 4 * OWN] + score[4 * OWN :]
        weights, totals = [], []
        for h in range(4):
            head = quad * 4 + h
            radius = (windows[head] - 1) // 2
            part = jnp.where(apart <= radius, scales[head] * score[h * OWN : (h + 1) * OWN], -jnp.inf)
            part = jnp.exp(part - jnp.max(part, axis=-1, keepdims=True))
            totals.append(jnp.sum(part, axis=-1, keepdims=True))
            weights.append(part.astype(BF16))
        mixed = dot(jnp.concatenate(weights, axis=0), value)
        att = jnp.zeros((OWN, 256), F32)
        for h in range(4):
            att = jnp.where(lane == h, mixed[h * OWN : (h + 1) * OWN] / totals[h], att)
        update = update + dot(att.astype(BF16), out_w[at : at + 256, :])
    result = x_own + update
    for s in range(4):
        stream[s] = result[s * TOKENS : (s + 1) * TOKENS].astype(BF16)


def merge_kernel(place, p0, p1, p2, p3, weight, bottom):
    width = p0.shape[2]
    acc = None
    for s in range(4):
        rows = jnp.concatenate([p[s].astype(F32) for p in (p0, p1, p2, p3)], axis=0).astype(BF16)
        term = dot(rows, weight[s * width : (s + 1) * width, :])
        acc = term if acc is None else acc + term
    for k in range(NX):
        bottom[lax.rem(place[0] + NX - k, NX)] = acc[k * TOKENS : (k + 1) * TOKENS].astype(BF16)


def project_kernel(place, p0, p1, p2, p3, ones, weight, bottom, query, pairs, whole):
    block = p0.shape[2]
    for k, p in enumerate((p0, p1, p2, p3)):
        at = pl.multiple_of(lax.rem(place[0] + NX - k, NX) * block, 128)
        rows = jnp.concatenate([p[i].astype(F32) for i in range(NX)], axis=0)
        whole[:, pl.ds(at, block)] = rows
    x = whole[...]
    bottom[...] = x.astype(BF16)
    mean = jnp.mean(x * x, axis=-1, keepdims=True)
    normed = (x * lax.rsqrt(mean + EPS)).astype(BF16)
    proj = dot(normed, weight[...])
    first = proj[:, :256]
    lane = lax.broadcasted_iota(jnp.int32, first.shape, 1)
    first = jnp.where(lane < 192, unit_quad(first, ones[...]), first)
    kv = jnp.concatenate([first, proj[:, 256:384]], axis=1).astype(BF16)
    for i in range(pairs.shape[0]):
        pairs[i] = kv
    query[...] = unit_quad(proj[:, 384:640], ones[...])


def attend_kernel(scales, place, query, near, far, out):
    lane = lax.broadcasted_iota(jnp.int32, query.shape, 1) // HEAD_DIM
    count = query.shape[0]
    q = query[...]
    hi, lo = split_hi_lo(q)
    rows = [jnp.where(lane == h, hi, 0) for h in range(3)]
    rows += [jnp.where(lane == h, lo, 0) for h in range(3)]
    rows = jnp.concatenate(rows, axis=0)
    scale = jnp.concatenate(
        [jnp.full((count, 1), scales[3 * place[0] + h], F32) for h in range(3)], axis=0
    )
    scores = []
    for ref in (near, far):
        score = dot_t(rows, ref[:, :256])
        scores.append(scale * (score[: 3 * count] + score[3 * count :]))
    highest = jnp.maximum(
        jnp.max(scores[0], axis=-1, keepdims=True), jnp.max(scores[1], axis=-1, keepdims=True)
    )
    total = jnp.zeros((3 * count, 1), F32)
    acc = jnp.zeros((3 * count, 256), F32)
    for score, ref in zip(scores, (near, far)):
        part = jnp.exp(score - highest)
        total = total + jnp.sum(part, axis=-1, keepdims=True)
        acc = acc + dot(part.astype(BF16), ref[:, 128:384])
    acc = acc / total
    att = jnp.zeros((count, 256), F32)
    for h in range(3):
        att = jnp.where(lane == h + 1, acc[h * count : (h + 1) * count], att)
    out[...] = att[:, 64:].astype(BF16)


def output_kernel(place, p0, p1, p2, p3, bottom, out_w, split_w, split):
    acc = bottom[...].astype(F32)
    block = p0.shape[1]
    for k, p in enumerate((p0, p1, p2, p3)):
        at = pl.multiple_of(lax.rem(place[0] + NX - k, NX) * block, 64)
        acc = acc + dot(p[...], out_w[pl.ds(at, block), :])
    result = dot_t(acc.astype(BF16), split_w[...])
    for i in range(NX):
        split[i] = result[i * TOKENS : (i + 1) * TOKENS].astype(BF16)


def mix_kernel(stream, upward, mix, matrix, out):
    s = jnp.concatenate([stream[i].astype(F32) for i in range(4)], axis=0)
    u = jnp.concatenate([upward[i].astype(F32) for i in range(4)], axis=0)
    mixed = (s + mix[...] * (u - s)).astype(BF16)
    grid = dot(matrix[...], mixed).astype(BF16)
    for r in range(ROWS):
        out[r] = grid[16 * r : 16 * r + COLS]


def time_features(step, width):
    half = width // 2
    freqs = jnp.exp(-math.log(10000.0) * jnp.arange(half, dtype=F32) / half)
    angles = step[0].astype(F32) * freqs
    return jnp.concatenate([jnp.cos(angles), jnp.sin(angles)])


def shift(x, axis, size, step):
    return lax.ppermute(x, axis, [(i, i + step) for i in range(size) if 0 <= i + step < size])


def gather_x(x):
    return [x] + [
        lax.ppermute(x, "x", [(i, (i + s) % NX) for i in range(NX)]) for s in range(1, NX)
    ]


def swap_core(x):
    return lax.ppermute(x, "c", [(0, 1), (1, 0)])


def merge_columns(merge_weight):
    rows, width = merge_weight.shape
    block = width // NX
    parts = jnp.stack([merge_weight[:, i * block : (i + 1) * block] for i in range(NX)])
    parts = jnp.broadcast_to(parts[None], (16, NX, rows, block)).reshape(16 * NX, rows, block)
    mine = lax.all_to_all(parts, ("z", "yl", "yh", "x"), 0, 0)
    other = swap_core(mine)
    c = lax.axis_index("c")
    first = jnp.where(c == 0, mine, other).reshape(8, 8, rows, block)
    second = jnp.where(c == 0, other, mine).reshape(8, 8, rows, block)
    return jnp.stack([first, second], axis=1).reshape(128 * rows, block)


def split_columns(split_weight):
    chunk = split_weight.T
    rows, depth = chunk.shape
    chunk = lax.ppermute(
        chunk, ("z", "x"), [(z * 4 + x, x * 4 + z) for z in range(4) for x in range(4)]
    )
    mine = lax.all_to_all(jnp.broadcast_to(chunk[None], (16, rows, depth)), ZY, 0, 0)
    other = swap_core(mine)
    c = lax.axis_index("c")
    first = jnp.where(c == 0, mine, other).reshape(4, 2, 2, rows, depth)
    second = jnp.where(c == 0, other, mine).reshape(4, 2, 2, rows, depth)
    whole = jnp.stack([first, second], axis=0)
    return whole.transpose(2, 0, 3, 1, 4, 5).reshape(32 * rows, depth)


def shards(
    fine,
    class_table,
    label,
    timestep,
    windows,
    fine_scale,
    fine_qkv,
    fine_out,
    merge_weight,
    bottom_scale,
    bottom_qkv,
    bottom_out,
    split_weight,
    skip_mix,
):
    height, width, depth = fine.shape
    up = shift(fine[height - REACH :], GY, 16, 1)
    down = shift(fine[:REACH], GY, 16, -1)
    tall_left = jnp.concatenate([up[:, :REACH], fine[:, :REACH], down[:, :REACH]], axis=0)
    tall_right = jnp.concatenate(
        [up[:, width - REACH :], fine[:, width - REACH :], down[:, width - REACH :]], axis=0
    )
    left = shift(tall_right.reshape(-1, depth), GX, 8, 1)
    right = shift(tall_left.reshape(-1, depth), GX, 8, -1)
    own = fine.reshape(height // 2, 2, width // 2, 2, depth).transpose(1, 3, 0, 2, 4)
    own = own.reshape(OWN, depth)
    halo = jnp.concatenate(
        [
            up.reshape(-1, depth),
            down.reshape(-1, depth),
            left,
            right,
            jnp.zeros((4, depth), BF16),
        ],
        axis=0,
    )
    row = lax.dynamic_slice_in_dim(class_table, label[0], 1, 0)[0].astype(F32)
    gain = (1.0 + 0.5 * (row + time_features(timestep, depth)))[None]
    start = jnp.stack(
        [
            lax.axis_index(GY) * height,
            lax.axis_index(GX) * width,
            jnp.int32(16 * height),
            jnp.int32(8 * width),
        ]
    ).astype(jnp.int32)
    ones = jnp.asarray(block_ones(), BF16)
    place = lax.axis_index("x").astype(jnp.int32)[None]

    merge_w = merge_columns(merge_weight)
    split_w = split_columns(split_weight)
    battn = bottom_out.shape[0]
    group = battn // NX
    deep = bottom_qkv.shape[0]
    at = lax.axis_index("x") * group
    picked = [
        lax.dynamic_slice_in_dim(bottom_qkv, part * battn + at, group, 1) for part in (1, 2, 0)
    ]
    qkv_w = jnp.concatenate(picked + [jnp.zeros((deep, 64), BF16)], axis=1)

    stream = call(
        fine_kernel,
        jax.ShapeDtypeStruct((4, TOKENS, depth), BF16),
        [
            start,
            windows,
            fine_scale,
            own,
            halo,
            gain,
            jnp.asarray(PLACES.T.copy()),
            jnp.asarray(PLACES[:OWN].copy()),
            ones,
            fine_qkv,
            fine_out,
        ],
        (0, 1, 2),
        flops=2 * KEYS * depth * 3 * depth,
        nbytes=5 * 2**20,
    )
    bottom = call(
        merge_kernel,
        jax.ShapeDtypeStruct((NX, TOKENS, merge_w.shape[1]), BF16),
        [place, *gather_x(stream), merge_w],
        (0,),
        flops=2 * OWN * 4 * depth * merge_w.shape[1],
        nbytes=3 * 2**20,
    )
    bfull, query, pairs = call(
        project_kernel,
        (
            jax.ShapeDtypeStruct((OWN, deep), BF16),
            jax.ShapeDtypeStruct((OWN, 256), F32),
            jax.ShapeDtypeStruct((16, OWN, 2 * group), BF16),
        ),
        [place, *gather_x(bottom), ones, qkv_w],
        (0,),
        [pltpu.VMEM((OWN, deep), F32)],
        flops=2 * OWN * deep * 640,
        nbytes=4 * 2**20,
    )
    near = lax.all_to_all(pairs, ZY, 0, 0).reshape(16 * OWN, 2 * group)
    far = swap_core(near)
    batt = call(
        attend_kernel,
        jax.ShapeDtypeStruct((OWN, group), BF16),
        [bottom_scale, place, query, near, far],
        (0, 1),
        flops=2 * 3 * OWN * 3072 * 256 * 3,
        nbytes=3 * 2**20,
    )
    split = call(
        output_kernel,
        jax.ShapeDtypeStruct((NX, TOKENS, depth), BF16),
        [place, *gather_x(batt), bfull, bottom_out, split_w],
        (0,),
        flops=2 * OWN * deep * 2 * depth,
        nbytes=5 * 2**20,
    )
    upward = lax.all_to_all(split, "x", 0, 0)
    return call(
        mix_kernel,
        jax.ShapeDtypeStruct((height, width, depth), BF16),
        [stream, upward, skip_mix[None], jnp.asarray(own_to_grid(), BF16)],
        (),
        flops=2 * 128 * 96 * depth,
        nbytes=2**20,
    )


def solution(mesh):
    inner = Mesh(mesh.devices.reshape(4, 2, 2, 2, 4), ALL)
    placed = (
        P(GY, GX, None),
        P(),
        P(),
        P(),
        P(),
        P(),
        P(),
        P(),
        P(ALL, None),
        P(),
        P(),
        P(),
        P(None, ALL),
        P(),
    )
    return jax.shard_map(
        shards, mesh=inner, in_specs=placed, out_specs=P(GY, GX, None), check_vma=False
    )
```

time: 1340 us -> 150 us (0.11)
  waiting for transfers between devices: 923 us -> 49.2 us
  local copies, waits for them, and re-layouts: 262 us -> 27.4 us
  other arithmetic: 92 us -> 5.52 us
  starting transfers between devices: 8.8 us -> 52.1 us
  matrix products: 26.2 us -> 0 us
  between operations: 17.4 us -> 1.73 us
    all_gather x4 -> x0, waiting for transfers between devices: 923 us -> none  [the longest x1 313 us: shards(): key_piece = lax.all_gather(bkey, ('gy', 'gx'), axis=0, tiled=True)]
    convert_element_type x51 -> x0, local copies, waits for them, and re-layouts: 89.3 us -> none  [the longest x48 87.8 us: neighbour_attention(): keys = window.reshape(height, width, heads, depth).astype(jnp.float32)]
    unnamed x266 -> x44, local copies, waits for them, and re-layouts: 66.4 us -> 5.55 us
    mul x103 -> x0, local copies, waits for them, and re-layouts: 59.4 us -> none  [the longest x98 58.6 us: neighbour_attention(): output = output + weights[..., row_off * WIN + col_off, None] * values]
    unnamed x49 -> x0, other arithmetic: 36.8 us -> none
    all_to_all x0 -> x4, waiting for transfers between devices: none -> 36.1 us  [the longest x1 15.6 us: shards(): near = lax.all_to_all(pairs, ZY, 0, 0).reshape(16 * OWN, 2 * group)]
    all_to_all x0 -> x4, starting transfers between devices: none -> 30.5 us  [the longest x1 11.9 us: merge_columns(): mine = lax.all_to_all(parts, ('z', 'yl', 'yh', 'x'), 0, 0)]
    reduce_sum x10 -> x0, other arithmetic: 27.6 us -> none  [the longest x3 24.5 us: neighbour_attention(): score = scales * jnp.sum(queries * keys, axis=-1)]
  transfers between devices with their start and end apart: 8 -> 21, of which waited for: 3 -> 10; matrix products, arithmetic and copies ran while one was open for 26% -> 17% of each run, Pallas kernels for 0% -> 5%
where the time goes in v1:
time: 150 us; the launch traced here: 148 us
  starting transfers between devices  52.1 us (35%)
  waiting for transfers between devices  49.2 us (33%)
  local copies, waits for them, and re-layouts  27.4 us (18%)
  Pallas kernels  12.5 us (8%)
  other arithmetic  5.52 us (4%)
  between operations  1.73 us (1%)
    all_to_all x1, waiting for transfers between devices, shards(): near = lax.all_to_all(pairs, ZY, 0, 0).reshape(16 * OWN, 2 * group)  15.6 us
    all_to_all x1, waiting for transfers between devices, merge_columns(): mine = lax.all_to_all(parts, ('z', 'yl', 'yh', 'x'), 0, 0)  14.4 us
    ppermute x9, starting transfers between devices, gather_x(): lax.ppermute(x, 'x', [(i, (i + s) % NX) for i in range(NX)])  12.6 us
    pallas_call x6, Pallas kernels, call(): pl.pallas_call(body, out_shape=out_shape, in_specs=[smem() if i in in_sme...  12.5 us
    all_to_all x1, starting transfers between devices, merge_columns(): mine = lax.all_to_all(parts, ('z', 'yl', 'yh', 'x'), 0, 0)  11.9 us
    ppermute x9, waiting for transfers between devices, gather_x(): lax.ppermute(x, 'x', [(i, (i + s) % NX) for i in range(NX)])  11.7 us
    all_to_all x1, starting transfers between devices, split_columns(): lax.all_to_all(jnp.broadcast_to(chunk[None], (16, rows, depth)), ZY, 0, 0)  8.38 us
    ppermute x4, starting transfers between devices, shift(): lax.ppermute(x, axis, [(i, i + step) for i in range(size) if 0 <= i + ste...  7.64 us
  transfers between devices with their start and end apart: 21, of which 10 were waited for; matrix products, arithmetic and copies ran while one was open for 17% of the time, Pallas kernels for 5%

profile of v1, /device:TPU:0, one launch (start us, length us, event | category | flops | bytes accessed | tf_op | source)
XLA Modules:
  0.0 148.5 jit_solution(4506869174831940934)
XLA Ops:
  0.0 0.8 slice_bitcast_fusion.3
  0.8 1.1 broadcast_in_dim.27
  2.0 11.9 %all-to-all-start = ((bf16[64,24,384]{2,1,0:T(8,128)(2,1)}), bf16[64,24,384]{2,1,0:T(8,128)(2,1)}, u32[]{:S(2)}, u32[]{:S(2)}) async-start(bf16[64,24,384]{2,1,0:T(8,128)(2,1)} %bitcast.10), calls=%async_computation | async-start | bytes 2359296 | tf_op jit(solution)/shard_map/all_to_all | solution.py:263
  13.9 1.5 collective-permute-start
  15.4 1.3 collective-permute-start.1
  16.7 1.3 collective-permute-start.15
  19.3 0.1 fusion.2
  19.3 14.4 %all-to-all-done = bf16[64,24,384]{2,1,0:T(8,128)(2,1)} async-done(((bf16[64,24,384]{2,1,0:T(8,128)(2,1)}), bf16[64,24,384]{2,1,0:T(8,128)(2,1)}, u32[]{:S(2)}, u32[]{:S(2)}) %all-to-all-start) | async-done | bytes 1179680 | tf_op jit(solution)/shard_map/all_to_all | solution.py:263
  33.8 4.6 %constant_dynamic-slice_fusion.2 = (bf16[1536,192]{1,0:T(8,128)(2,1)}, bf16[1536,192]{1,0:T(8,128)(2,1)}, bf16[1536,192]{1,0:T(8,128)(2,1)}) fusion(bf16[1536,2304]{1,0:T(8,128)(2,1)} %param.28, s32[]{:T(128)S(6)} %select_n.40, s32[]{:T(128)S(6)} %select_n.42, s32[]{:T(128)S(6)} %select_n.41), kind=kLoop, calls=%fused_computation.21 | loop fusion | bytes 3538956 | tf_op jit(solution)/shard_map/dynamic_slice | solution.py:343
  38.4 0.7 fusion.1.gain
  39.1 0.1 reshape.49
  39.3 0.7 reshape.50.own
  40.0 0.7 pad.5.clone
  40.7 0.1 pad_maximum_fusion.1
  40.8 0.7 reshape.53
  41.5 3.6 %collective-permute-start.2 = (bf16[42,768]{1,0:T(8,128)(2,1)}, bf16[42,768]{1,0:T(8,128)(2,1)}, u32[]{:S(2)}, u32[]{:S(2)}) collective-permute-start(bf16[42,768]{1,0:T(8,128)(2,1)} %reshape.53), channel_id=1, source_target_pairs={{0,1},{1,2},{2,3},{3,4},{4,5},{5,6},{6,7},{8,9},{9,10},{10,11},{11... | collective-permute-start | bytes 193544 | tf_op jit(solution)/shard_map/ppermute | solution.py:245
  45.2 0.7 reshape.54
  45.9 1.3 collective-permute-start.3
  47.2 0.1 pad_add_fusion.start
  47.3 0.6 reshape.51
  47.9 0.6 reshape.52
  48.6 2.2 %broadcast_in_dim.29 = bf16[16,24,1536]{2,1,0:T(8,128)(2,1)} broadcast(bf16[24,1536]{1,0:T(8,128)(2,1)} %collective-permute-done.15), dimensions={1,2} | broadcast | bytes 1253376 | tf_op jit(solution)/shard_map/broadcast_in_dim | solution.py:277
  50.7 8.4 %all-to-all-start.2 = ((bf16[16,24,1536]{2,1,0:T(8,128)(2,1)}), bf16[16,24,1536]{2,1,0:T(8,128)(2,1)}, u32[]{:S(2)}, u32[]{:S(2)}) async-start(bf16[16,24,1536]{2,1,0:T(8,128)(2,1)} %broadcast_in_dim.29), calls=%async_computation.2 | async-start | bytes 2359296 | tf_op jit(solution)/shard_map/all_to_all | solution.py:277
  59.1 0.6 broadcast_in_dim.12
  59.7 7.3 %concatenate.18.halo = bf16[160,768]{1,0:T(8,128)(2,1)} concatenate(bf16[36,768]{1,0:T(8,128)(2,1)} %reshape.51, bf16[36,768]{1,0:T(8,128)(2,1)} %reshape.52, bf16[42,768]{1,0:T(8,128)(2,1)} %collective-permute-done.2, bf16[42,768]{1,0:T(8,128)(2,1)} %collective-permute-done.3, bf16[4,768]{1,0:T(4,128)(2,1)} %broadcast_in_dim.12), dimensions={0} | concatenate | bytes 491520 | tf_op jit(solution)/shard_map/concatenate | solution.py:313
  67.0 1.3 copy-done.4
  68.3 0.9 copy-done.5
  69.3 0.9 copy-done.6
  70.2 0.9 copy-done.7
  71.1 0.8 copy-done.9
  71.9 0.7 copy-done.13
  72.5 4.4 %shard_map.172.p0.stream = bf16[4,24,768]{2,1,0:T(8,128)(2,1)S(1)} custom-call(s32[4]{0:T(128)S(1)} %pad_add_fusion.start, s32[12]{0:T(128)S(1)} %copy-done.12, f32[12]{0:T(128)S(1)} %copy-done.13, bf16[96,768]{1,0:T(8,128)(2,1)S(1)} %copy-done.6, bf16[160,768]{1,0:T(8,128)(2,1)S(1)} %copy-done.5, f32[1,768]{1,0:T(1,128)S(1)} %fusion.1.gain, ...), custom_call_target="tpu_custom_call" | custom-call | flops 905969664 | bytes 5242880 | tf_op jit(solution)/shard_map/pallas_call | solution.py:92
  77.0 0.1 collective-permute-start.4
  77.0 1.5 %collective-permute-start.5 = (bf16[4,24,768]{2,1,0:T(8,128)(2,1)S(1)}, bf16[4,24,768]{2,1,0:T(8,128)(2,1)S(1)}, u32[]{:S(2)}, u32[]{:S(2)}) collective-permute-start(bf16[4,24,768]{2,1,0:T(8,128)(2,1)S(1)} %shard_map.172.p0.stream), channel_id=1, source_target_pairs={{0,2},{1,3},{2,0},{3,1},{4,6},{5,7},{6,4},{7,5},{8,10},{9,11},{10,... | collective-permute-start | bytes 442376 | tf_op jit(solution)/shard_map/ppermute | solution.py:250
  78.6 2.5 %collective-permute-start.6 = (bf16[4,24,768]{2,1,0:T(8,128)(2,1)S(1)}, bf16[4,24,768]{2,1,0:T(8,128)(2,1)S(1)}, u32[]{:S(2)}, u32[]{:S(2)}) collective-permute-start(bf16[4,24,768]{2,1,0:T(8,128)(2,1)S(1)} %shard_map.172.p0.stream), channel_id=1, source_target_pairs={{0,3},{1,0},{2,1},{3,2},{4,7},{5,4},{6,5},{7,6},{8,11},{9,8},{10,9... | collective-permute-start | bytes 442376 | tf_op jit(solution)/shard_map/ppermute | solution.py:250
  81.1 1.8 %broadcast_select_fusion.3 = (bf16[64,24,384]{2,1,0:T(8,128)(2,1)S(1)}, bf16[64,24,384]{2,1,0:T(8,128)(2,1)S(1)}) fusion(bf16[64,24,384]{2,1,0:T(8,128)(2,1)} %all-to-all-done, bf16[64,24,384]{2,1,0:T(8,128)(2,1)} %collective-permute-done.7, pred[]{:T(512)S(6)} %eq.2), kind=kLoop, calls=%fused_computation.6 | loop fusion | flops 1179648 | bytes 4718593 | tf_op jit(solution)/shard_map/jit(_where)/select_n | solution.py:266
  83.0 0.3 pad_maximum_fusion
  83.3 3.6 %collective-permute-done.4.p1 = bf16[4,24,768]{2,1,0:T(8,128)(2,1)S(1)} collective-permute-done((bf16[4,24,768]{2,1,0:T(8,128)(2,1)S(1)}, bf16[4,24,768]{2,1,0:T(8,128)(2,1)S(1)}, u32[]{:S(2)}, u32[]{:S(2)}) %collective-permute-start.4) | collective-permute-done | bytes 147488 | tf_op jit(solution)/shard_map/ppermute | solution.py:250
  86.8 0.6 collective-permute-done.6.p3
  87.4 0.6 shard_map.173.p0
  88.0 2.7 %collective-permute-start.10 = (bf16[4,24,384]{2,1,0:T(8,128)(2,1)S(1)}, bf16[4,24,384]{2,1,0:T(8,128)(2,1)S(1)}, u32[]{:S(2)}, u32[]{:S(2)}) collective-permute-start(bf16[4,24,384]{2,1,0:T(8,128)(2,1)S(1)} %shard_map.173.p0), channel_id=1, source_target_pairs={{0,3},{1,0},{2,1},{3,2},{4,7},{5,4},{6,5},{7,6},{8,11},{9,8},{10,9... | collective-permute-start | bytes 221192 | tf_op jit(solution)/shard_map/ppermute | solution.py:250
  90.7 1.5 %collective-permute-start.9 = (bf16[4,24,384]{2,1,0:T(8,128)(2,1)S(1)}, bf16[4,24,384]{2,1,0:T(8,128)(2,1)S(1)}, u32[]{:S(2)}, u32[]{:S(2)}) collective-permute-start(bf16[4,24,384]{2,1,0:T(8,128)(2,1)S(1)} %shard_map.173.p0), channel_id=1, source_target_pairs={{0,2},{1,3},{2,0},{3,1},{4,6},{5,7},{6,4},{7,5},{8,10},{9,11},{10,... | collective-permute-start | bytes 221192 | tf_op jit(solution)/shard_map/ppermute | solution.py:250
  92.3 0.8 maximum_maximum_fusion.weight
  93.1 4.1 %collective-permute-done.8.p1 = bf16[4,24,384]{2,1,0:T(8,128)(2,1)S(1)} collective-permute-done((bf16[4,24,384]{2,1,0:T(8,128)(2,1)S(1)}, bf16[4,24,384]{2,1,0:T(8,128)(2,1)S(1)}, u32[]{:S(2)}, u32[]{:S(2)}) %collective-permute-start.8) | collective-permute-done | bytes 73760 | tf_op jit(solution)/shard_map/ppermute | solution.py:250
  97.2 1.8 %shard_map.174 = (bf16[96,1536]{1,0:T(8,128)(2,1)S(1)}, f32[96,256]{1,0:T(8,128)S(1)}, bf16[16,96,384]{2,1,0:T(8,128)(2,1)}) custom-call(s32[1]{0:T(128)} %bitcast.5.place, bf16[4,24,384]{2,1,0:T(8,128)(2,1)S(1)} %shard_map.173.p0, bf16[4,24,384]{2,1,0:T(8,128)(2,1)S(1)} %collective-permute-done.8.p1, bf16[4,24,384]{2,1,0:T(8,128)(2,1)S(1)} %collective-permute-done.9.p2, ...), custom_call_target="tpu_custom_call" | custom-call | flops 188743680 | bytes 4194304 | tf_op jit(solution)/shard_map/pallas_call | solution.py:92
  99.0 6.9 %all-to-all-start.1 = ((bf16[16,96,384]{2,1,0:T(8,128)(2,1)}), bf16[16,96,384]{2,1,0:T(8,128)(2,1)S(1)}, u32[]{:S(2)}, u32[]{:S(2)}) async-start(bf16[16,96,384]{2,1,0:T(8,128)(2,1)} %get-tuple-element.9), calls=%async_computation.1 | async-start | bytes 2359296 | tf_op jit(solution)/shard_map/all_to_all | solution.py:388
  106.0 0.1 collective-permute-start.16
  106.1 15.6 %all-to-all-done.1 = bf16[16,96,384]{2,1,0:T(8,128)(2,1)S(1)} async-done(((bf16[16,96,384]{2,1,0:T(8,128)(2,1)}), bf16[16,96,384]{2,1,0:T(8,128)(2,1)S(1)}, u32[]{:S(2)}, u32[]{:S(2)}) %all-to-all-start.1) | async-done | bytes 1179680 | tf_op jit(solution)/shard_map/all_to_all | solution.py:388
  121.7 1.4 broadcast_select_fusion.1
  123.2 1.4 collective-permute-done.11.far
  124.6 3.7 %shard_map.175.p0 = bf16[96,192]{1,0:T(8,128)(2,1)S(1)} custom-call(f32[12]{0:T(128)S(1)} %copy-done.14, s32[1]{0:T(128)} %bitcast.5.place, f32[96,256]{1,0:T(8,128)S(1)} %get-tuple-element.8.query, bf16[1536,384]{1,0:T(8,128)(2,1)S(1)} %bitcast.35, bf16[1536,384]{1,0:T(8,128)(2,1)S(1)} %collective-permute-done.11.far), custom_call_target="tpu_custom_call" | custom-call | flops 1358954496 | bytes 3145728 | tf_op jit(solution)/shard_map/pallas_call | solution.py:92
  128.3 0.1 collective-permute-start.12
  128.3 3.9 %collective-permute-start.13 = (bf16[96,192]{1,0:T(8,128)(2,1)S(1)}, bf16[96,192]{1,0:T(8,128)(2,1)S(1)}, u32[]{:S(2)}, u32[]{:S(2)}) collective-permute-start(bf16[96,192]{1,0:T(8,128)(2,1)S(1)} %shard_map.175.p0), channel_id=1, source_target_pairs={{0,2},{1,3},{2,0},{3,1},{4,6},{5,7},{6,4},{7,5},{8,10},{9,11},{10,... | collective-permute-start | bytes 110600 | tf_op jit(solution)/shard_map/ppermute | solution.py:250
  132.3 0.1 collective-permute-start.14
  132.4 0.2 maximum_bitcast_fusion
  132.6 0.2 copy.30
  132.8 1.2 collective-permute-done.12.p1
  134.0 1.0 collective-permute-done.13.p2
  135.1 1.3 collective-permute-done.14.p3
  136.4 1.8 %shard_map.176 = bf16[4,24,768]{2,1,0:T(8,128)(2,1)} custom-call(s32[1]{0:T(128)} %bitcast.5.place, bf16[96,192]{1,0:T(8,128)(2,1)S(1)} %shard_map.175.p0, bf16[96,192]{1,0:T(8,128)(2,1)S(1)} %collective-permute-done.12.p1, bf16[96,192]{1,0:T(8,128)(2,1)S(1)} %collective-permute-done.13.p2, bf16[96,192]{1,0:T(8,128)(2,1)S(1)} %collective-permute-done.14.p3, ...), custom_call_target="tpu_custom_call" | custom-call | flops 452984832 | bytes 5242880 | tf_op jit(solution)/shard_map/pallas_call | solution.py:92
  138.2 3.3 %all-to-all-start.3 = ((bf16[4,24,768]{2,1,0:T(8,128)(2,1)}), bf16[4,24,768]{2,1,0:T(8,128)(2,1)S(1)}, u32[]{:S(2)}, u32[]{:S(2)}) async-start(bf16[4,24,768]{2,1,0:T(8,128)(2,1)} %shard_map.176), calls=%async_computation.3 | async-start | bytes 294912 | tf_op jit(solution)/shard_map/all_to_all | solution.py:406
  141.5 6.0 %all-to-all-done.3.upward = bf16[4,24,768]{2,1,0:T(8,128)(2,1)S(1)} async-done(((bf16[4,24,768]{2,1,0:T(8,128)(2,1)}), bf16[4,24,768]{2,1,0:T(8,128)(2,1)S(1)}, u32[]{:S(2)}, u32[]{:S(2)}) %all-to-all-start.3) | async-done | bytes 147488 | tf_op jit(solution)/shard_map/all_to_all | solution.py:406
  147.5 0.2 shard_map.177
  147.8 0.7 copy.31
  (64 shorter events, 0.4 us)
Async XLA Ops:
  0.8 13.0 %copy-start.18 = (bf16[8,12,768]{2,0,1:T(8,128)(2,1)S(1)}, bf16[8,12,768]{2,0,1:T(8,128)(2,1)}, u32[]{:S(2)}) copy-start(bf16[8,12,768]{2,0,1:T(8,128)(2,1)} %param.18) | copy-start | bytes 442372
  2.0 14.7 %copy-start.21 = (bf16[1536,24]{0,1:T(8,128)(2,1)S(1)}, bf16[1536,24]{0,1:T(8,128)(2,1)}, u32[]{:S(2)}) copy-start(bf16[1536,24]{0,1:T(8,128)(2,1)} %param.30) | copy-start | bytes 221188
  2.0 31.8 %all-to-all-start = ((bf16[64,24,384]{2,1,0:T(8,128)(2,1)}), bf16[64,24,384]{2,1,0:T(8,128)(2,1)}, u32[]{:S(2)}, u32[]{:S(2)}) async-start(bf16[64,24,384]{2,1,0:T(8,128)(2,1)} %bitcast.10), calls=%async_computation | async-start | bytes 2359296 | tf_op jit(solution)/shard_map/all_to_all | solution.py:263
  13.9 26.8 %collective-permute-start = (bf16[3,12,768]{2,0,1:T(4,128)(2,1)S(1)}, bf16[3,12,768]{2,0,1:T(4,128)(2,1)S(1)}, u32[]{:S(2)}, u32[]{:S(2)}) collective-permute-start(bf16[3,12,768]{2,0,1:T(4,128)(2,1)S(1)} %get-tuple-element.21), channel_id=1, source_target_pairs={{0,8},{8,16},{16,24},{24,32},{32,40},{40,48},{48,56},{56,64},{64,7... | collective-permute-start | bytes 165896 | tf_op jit(solution)/shard_map/ppermute | solution.py:245
  15.4 25.3 %collective-permute-start.1 = (bf16[3,12,768]{2,0,1:T(4,128)(2,1)S(1)}, bf16[3,12,768]{2,0,1:T(4,128)(2,1)S(1)}, u32[]{:S(2)}, u32[]{:S(2)}) collective-permute-start(bf16[3,12,768]{2,0,1:T(4,128)(2,1)S(1)} %get-tuple-element.20), channel_id=1, source_target_pairs={{8,0},{16,8},{24,16},{32,24},{40,32},{48,40},{56,48},{64,56},{72,6... | collective-permute-start | bytes 165896 | tf_op jit(solution)/shard_map/ppermute | solution.py:245
  16.7 31.9 %collective-permute-start.15 = (bf16[24,1536]{1,0:T(8,128)(2,1)S(1)}, bf16[24,1536]{1,0:T(8,128)(2,1)}, u32[]{:S(2)}, u32[]{:S(2)}) collective-permute-start(bf16[24,1536]{1,0:T(8,128)(2,1)S(1)} %bitcast.41), channel_id=1, source_target_pairs={{0,0},{1,32},{2,64},{3,96},{32,1},{33,33},{34,65},{35,97},{64,2},{... | collective-permute-start | bytes 221192 | tf_op jit(solution)/shard_map/ppermute | solution.py:274
  33.8 47.3 %collective-permute-start.7 = (bf16[64,24,384]{2,1,0:T(8,128)(2,1)}, bf16[64,24,384]{2,1,0:T(8,128)(2,1)}, u32[]{:S(2)}, u32[]{:S(2)}) collective-permute-start(bf16[64,24,384]{2,1,0:T(8,128)(2,1)} %all-to-all-done), channel_id=1, source_target_pairs={{0,8},{8,0},{1,9},{9,1},{2,10},{10,2},{3,11},{11,3},{4,12},{12,4},... | collective-permute-start | bytes 3538952 | tf_op jit(solution)/shard_map/ppermute | solution.py:255
  41.5 17.6 %collective-permute-start.2 = (bf16[42,768]{1,0:T(8,128)(2,1)}, bf16[42,768]{1,0:T(8,128)(2,1)}, u32[]{:S(2)}, u32[]{:S(2)}) collective-permute-start(bf16[42,768]{1,0:T(8,128)(2,1)} %reshape.53), channel_id=1, source_target_pairs={{0,1},{1,2},{2,3},{3,4},{4,5},{5,6},{6,7},{8,9},{9,10},{10,11},{11... | collective-permute-start | bytes 193544 | tf_op jit(solution)/shard_map/ppermute | solution.py:245
  45.9 13.3 %collective-permute-start.3 = (bf16[42,768]{1,0:T(8,128)(2,1)}, bf16[42,768]{1,0:T(8,128)(2,1)}, u32[]{:S(2)}, u32[]{:S(2)}) collective-permute-start(bf16[42,768]{1,0:T(8,128)(2,1)} %reshape.54), channel_id=1, source_target_pairs={{1,0},{2,1},{3,2},{4,3},{5,4},{6,5},{7,6},{9,8},{10,9},{11,10},{12... | collective-permute-start | bytes 193544 | tf_op jit(solution)/shard_map/ppermute | solution.py:245
  48.6 18.5 %copy-start = (bf16[768,2304]{1,0:T(8,128)(2,1)S(1)}, bf16[768,2304]{1,0:T(8,128)(2,1)}, u32[]{:S(2)}) copy-start(bf16[768,2304]{1,0:T(8,128)(2,1)} %qkv.1) | copy-start | bytes 10616836
  50.7 16.3 %copy-start.11 = (s32[2,256]{1,0:T(2,128)S(1)}, s32[2,256]{1,0:T(2,128)}, u32[]{:S(2)}) copy-start(s32[2,256]{1,0:T(2,128)} %constant.69.clone.key_place) | copy-start | bytes 6148
  50.7 16.3 %copy-start.12 = (s32[12]{0:T(128)S(1)}, s32[12]{0:T(128)}, u32[]{:S(2)}) copy-start(s32[12]{0:T(128)} %windows.1) | copy-start | bytes 148
  50.7 48.3 %all-to-all-start.2 = ((bf16[16,24,1536]{2,1,0:T(8,128)(2,1)}), bf16[16,24,1536]{2,1,0:T(8,128)(2,1)}, u32[]{:S(2)}, u32[]{:S(2)}) async-start(bf16[16,24,1536]{2,1,0:T(8,128)(2,1)} %broadcast_in_dim.29), calls=%async_computation.2 | async-start | bytes 2359296 | tf_op jit(solution)/shard_map/all_to_all | solution.py:277
  67.0 1.3 copy-start.4
  68.3 0.9 copy-start.5
  69.3 0.9 copy-start.6
  70.2 0.9 copy-start.7
  71.1 0.8 copy-start.9
  71.9 0.7 copy-start.13
  76.9 10.5 %copy-start.2 = (bf16[4,24,768]{2,1,0:T(8,128)(2,1)}, bf16[4,24,768]{2,1,0:T(8,128)(2,1)S(1)}, u32[]{:S(2)}) copy-start(bf16[4,24,768]{2,1,0:T(8,128)(2,1)S(1)} %shard_map.172.p0.stream) | copy-start | bytes 442372
  77.0 9.9 %collective-permute-start.4 = (bf16[4,24,768]{2,1,0:T(8,128)(2,1)S(1)}, bf16[4,24,768]{2,1,0:T(8,128)(2,1)S(1)}, u32[]{:S(2)}, u32[]{:S(2)}) collective-permute-start(bf16[4,24,768]{2,1,0:T(8,128)(2,1)S(1)} %shard_map.172.p0.stream), channel_id=1, source_target_pairs={{0,1},{1,2},{2,3},{3,0},{4,5},{5,6},{6,7},{7,4},{8,9},{9,10},{10,1... | collective-permute-start | bytes 442376 | tf_op jit(solution)/shard_map/ppermute | solution.py:250
  77.0 9.8 %collective-permute-start.5 = (bf16[4,24,768]{2,1,0:T(8,128)(2,1)S(1)}, bf16[4,24,768]{2,1,0:T(8,128)(2,1)S(1)}, u32[]{:S(2)}, u32[]{:S(2)}) collective-permute-start(bf16[4,24,768]{2,1,0:T(8,128)(2,1)S(1)} %shard_map.172.p0.stream), channel_id=1, source_target_pairs={{0,2},{1,3},{2,0},{3,1},{4,6},{5,7},{6,4},{7,5},{8,10},{9,11},{10,... | collective-permute-start | bytes 442376 | tf_op jit(solution)/shard_map/ppermute | solution.py:250
  78.6 8.8 %collective-permute-start.6 = (bf16[4,24,768]{2,1,0:T(8,128)(2,1)S(1)}, bf16[4,24,768]{2,1,0:T(8,128)(2,1)S(1)}, u32[]{:S(2)}, u32[]{:S(2)}) collective-permute-start(bf16[4,24,768]{2,1,0:T(8,128)(2,1)S(1)} %shard_map.172.p0.stream), channel_id=1, source_target_pairs={{0,3},{1,0},{2,1},{3,2},{4,7},{5,4},{6,5},{7,6},{8,11},{9,8},{10,9... | collective-permute-start | bytes 442376 | tf_op jit(solution)/shard_map/ppermute | solution.py:250
  83.2 9.0 %copy-start.15 = (bf16[1536,192]{1,0:T(8,128)(2,1)S(1)}, bf16[1536,192]{1,0:T(8,128)(2,1)}, u32[]{:S(2)}) copy-start(bf16[1536,192]{1,0:T(8,128)(2,1)} %get-tuple-element.11) | copy-start | bytes 1769476
  83.2 9.0 %copy-start.16 = (bf16[1536,192]{1,0:T(8,128)(2,1)S(1)}, bf16[1536,192]{1,0:T(8,128)(2,1)}, u32[]{:S(2)}) copy-start(bf16[1536,192]{1,0:T(8,128)(2,1)} %get-tuple-element.12) | copy-start | bytes 1769476
  83.2 9.0 %copy-start.17 = (bf16[1536,192]{1,0:T(8,128)(2,1)S(1)}, bf16[1536,192]{1,0:T(8,128)(2,1)}, u32[]{:S(2)}) copy-start(bf16[1536,192]{1,0:T(8,128)(2,1)} %get-tuple-element.13) | copy-start | bytes 1769476
  83.3 9.0 %copy-start.19 = (bf16[640]{0:T(1024)(128)(2,1)S(1)}, bf16[640]{0:T(1024)(128)(2,1)}, u32[]{:S(2)}) copy-start(bf16[640]{0:T(1024)(128)(2,1)} %pad.5.clone) | copy-start | bytes 3844
  88.0 5.1 %collective-permute-start.10 = (bf16[4,24,384]{2,1,0:T(8,128)(2,1)S(1)}, bf16[4,24,384]{2,1,0:T(8,128)(2,1)S(1)}, u32[]{:S(2)}, u32[]{:S(2)}) collective-permute-start(bf16[4,24,384]{2,1,0:T(8,128)(2,1)S(1)} %shard_map.173.p0), channel_id=1, source_target_pairs={{0,3},{1,0},{2,1},{3,2},{4,7},{5,4},{6,5},{7,6},{8,11},{9,8},{10,9... | collective-permute-start | bytes 221192 | tf_op jit(solution)/shard_map/ppermute | solution.py:250
  90.7 6.5 %collective-permute-start.8 = (bf16[4,24,384]{2,1,0:T(8,128)(2,1)S(1)}, bf16[4,24,384]{2,1,0:T(8,128)(2,1)S(1)}, u32[]{:S(2)}, u32[]{:S(2)}) collective-permute-start(bf16[4,24,384]{2,1,0:T(8,128)(2,1)S(1)} %shard_map.173.p0), channel_id=1, source_target_pairs={{0,1},{1,2},{2,3},{3,0},{4,5},{5,6},{6,7},{7,4},{8,9},{9,10},{10,1... | collective-permute-start | bytes 221192 | tf_op jit(solution)/shard_map/ppermute | solution.py:250
  90.7 6.5 %collective-permute-start.9 = (bf16[4,24,384]{2,1,0:T(8,128)(2,1)S(1)}, bf16[4,24,384]{2,1,0:T(8,128)(2,1)S(1)}, u32[]{:S(2)}, u32[]{:S(2)}) collective-permute-start(bf16[4,24,384]{2,1,0:T(8,128)(2,1)S(1)} %shard_map.173.p0), channel_id=1, source_target_pairs={{0,2},{1,3},{2,0},{3,1},{4,6},{5,7},{6,4},{7,5},{8,10},{9,11},{10,... | collective-permute-start | bytes 221192 | tf_op jit(solution)/shard_map/ppermute | solution.py:250
  92.3 4.9 %copy-start.8 = (bf16[256,256]{1,0:T(8,128)(2,1)S(1)}, bf16[256,256]{1,0:T(8,128)(2,1)}, u32[]{:S(2)}) copy-start(bf16[256,256]{1,0:T(8,128)(2,1)} %constant.68.clone.ones) | copy-start | bytes 393220
  99.0 22.7 %all-to-all-start.1 = ((bf16[16,96,384]{2,1,0:T(8,128)(2,1)}), bf16[16,96,384]{2,1,0:T(8,128)(2,1)S(1)}, u32[]{:S(2)}, u32[]{:S(2)}) async-start(bf16[16,96,384]{2,1,0:T(8,128)(2,1)} %get-tuple-element.9), calls=%async_computation.1 | async-start | bytes 2359296 | tf_op jit(solution)/shard_map/all_to_all | solution.py:388
  106.0 15.7 %collective-permute-start.16 = (bf16[16,24,1536]{2,1,0:T(8,128)(2,1)}, bf16[16,24,1536]{2,1,0:T(8,128)(2,1)S(1)}, u32[]{:S(2)}, u32[]{:S(2)}) collective-permute-start(bf16[16,24,1536]{2,1,0:T(8,128)(2,1)} %all-to-all-done.2), channel_id=1, source_target_pairs={{0,8},{8,0},{1,9},{9,1},{2,10},{10,2},{3,11},{11,3},{4,12},{12,4},... | collective-permute-start | bytes 3538952 | tf_op jit(solution)/shard_map/ppermute | solution.py:255
  121.7 2.9 %copy-start.14 = (f32[12]{0:T(128)S(1)}, f32[12]{0:T(128)}, u32[]{:S(2)}) copy-start(f32[12]{0:T(128)} %scales.3) | copy-start | bytes 148
  121.7 2.8 %collective-permute-start.11 = (bf16[1536,384]{1,0:T(8,128)(2,1)S(1)}, bf16[1536,384]{1,0:T(8,128)(2,1)S(1)}, u32[]{:S(2)}, u32[]{:S(2)}) collective-permute-start(bf16[1536,384]{1,0:T(8,128)(2,1)S(1)} %bitcast.34), channel_id=1, source_target_pairs={{0,8},{8,0},{1,9},{9,1},{2,10},{10,2},{3,11},{11,3},{4,12},{12,4},... | collective-permute-start | bytes 3538952 | tf_op jit(solution)/shard_map/ppermute | solution.py:255
  128.3 5.8 %collective-permute-start.12 = (bf16[96,192]{1,0:T(8,128)(2,1)S(1)}, bf16[96,192]{1,0:T(8,128)(2,1)S(1)}, u32[]{:S(2)}, u32[]{:S(2)}) collective-permute-start(bf16[96,192]{1,0:T(8,128)(2,1)S(1)} %shard_map.175.p0), channel_id=1, source_target_pairs={{0,1},{1,2},{2,3},{3,0},{4,5},{5,6},{6,7},{7,4},{8,9},{9,10},{10,1... | collective-permute-start | bytes 110600 | tf_op jit(solution)/shard_map/ppermute | solution.py:250
  128.3 6.7 %collective-permute-start.13 = (bf16[96,192]{1,0:T(8,128)(2,1)S(1)}, bf16[96,192]{1,0:T(8,128)(2,1)S(1)}, u32[]{:S(2)}, u32[]{:S(2)}) collective-permute-start(bf16[96,192]{1,0:T(8,128)(2,1)S(1)} %shard_map.175.p0), channel_id=1, source_target_pairs={{0,2},{1,3},{2,0},{3,1},{4,6},{5,7},{6,4},{7,5},{8,10},{9,11},{10,... | collective-permute-start | bytes 110600 | tf_op jit(solution)/shard_map/ppermute | solution.py:250
  132.3 4.1 %collective-permute-start.14 = (bf16[96,192]{1,0:T(8,128)(2,1)S(1)}, bf16[96,192]{1,0:T(8,128)(2,1)S(1)}, u32[]{:S(2)}, u32[]{:S(2)}) collective-permute-start(bf16[96,192]{1,0:T(8,128)(2,1)S(1)} %shard_map.175.p0), channel_id=1, source_target_pairs={{0,3},{1,0},{2,1},{3,2},{4,7},{5,4},{6,5},{7,6},{8,11},{9,8},{10,9... | collective-permute-start | bytes 110600 | tf_op jit(solution)/shard_map/ppermute | solution.py:250
  132.6 3.7 %copy-start.1 = (bf16[768,1536]{1,0:T(8,128)(2,1)S(1)}, bf16[768,1536]{1,0:T(8,128)(2,1)}, u32[]{:S(2)}) copy-start(bf16[768,1536]{1,0:T(8,128)(2,1)} %out_w.3) | copy-start | bytes 7077892
  136.3 5.2 %copy-start.20 = (f32[768]{0:T(1024)S(1)}, f32[768]{0:T(1024)}, u32[]{:S(2)}) copy-start(f32[768]{0:T(1024)} %param.31) | copy-start | bytes 9220
  136.3 11.2 %copy-start.3 = (bf16[4,24,768]{2,1,0:T(8,128)(2,1)S(1)}, bf16[4,24,768]{2,1,0:T(8,128)(2,1)}, u32[]{:S(2)}) copy-start(bf16[4,24,768]{2,1,0:T(8,128)(2,1)} %copy-done.2) | copy-start | bytes 442372
  136.3 11.2 %copy-start.10 = (bf16[128,96]{1,0:T(8,128)(2,1)S(1)}, bf16[128,96]{1,0:T(8,128)(2,1)}, u32[]{:S(2)}) copy-start(bf16[128,96]{1,0:T(8,128)(2,1)} %constant.71.clone.matrix) | copy-start | bytes 73732
  138.2 9.4 %all-to-all-start.3 = ((bf16[4,24,768]{2,1,0:T(8,128)(2,1)}), bf16[4,24,768]{2,1,0:T(8,128)(2,1)S(1)}, u32[]{:S(2)}, u32[]{:S(2)}) async-start(bf16[4,24,768]{2,1,0:T(8,128)(2,1)} %shard_map.176), calls=%async_computation.3 | async-start | bytes 294912 | tf_op jit(solution)/shard_map/all_to_all | solution.py:406

commit v2 on v1

v2 whole, which is shorter than its diff:
```python
import math

import jax
import jax.numpy as jnp
import numpy as np
from jax import lax
from jax.experimental import pallas as pl
from jax.experimental.pallas import tpu as pltpu
from jax.sharding import Mesh, PartitionSpec as P

HEAD_DIM = 64
WIN = 7
REACH = WIN // 2
EPS = 1e-06
ROWS, COLS = 8, 12
OWN = ROWS * COLS
TOKENS = OWN // 4
KEYS = 256
FAR = 1000
BF16 = jnp.bfloat16
F32 = jnp.float32

ALL = ("z", "yl", "c", "yh", "x")
GY = ("z", "yl", "c")
GX = ("yh", "x")
REST = ("yl", "yh", "x")
NX = 4

VMEM_LIMIT = 40 * 2**20


def key_places():
    places = []
    for cols in (range(COLS), range(-REACH, 0), range(COLS, COLS + REACH)):
        places += [(r, c) for c in cols for r in range(ROWS)]
    for rows in (range(-REACH, 0), range(ROWS, ROWS + REACH)):
        places += [(r, c) for c in range(-REACH, COLS + REACH) for r in rows]
    places += [(FAR, FAR)] * (KEYS - len(places))
    return np.array(places, np.int32)


PLACES = key_places()


def reorder(flip):
    m = lax.broadcasted_iota(jnp.int32, (OWN, OWN), 1 if flip else 0)
    n = lax.broadcasted_iota(jnp.int32, (OWN, OWN), 0 if flip else 1)
    s = (m >= TOKENS).astype(jnp.int32) + (m >= 2 * TOKENS) + (m >= 3 * TOKENS)
    t = m - s * TOKENS
    source = (2 * (t // 4) + s % 2) * ROWS + 2 * (t % 4) + s // 2
    return (n == source).astype(F32).astype(BF16)


def block_ones():
    row = lax.broadcasted_iota(jnp.int32, (256, 256), 0) // HEAD_DIM
    col = lax.broadcasted_iota(jnp.int32, (256, 256), 1) // HEAD_DIM
    return (row == col).astype(F32).astype(BF16)


def dot(a, b):
    return jnp.dot(a, b, preferred_element_type=F32)


def dot_t(a, b):
    return lax.dot_general(a, b, (((1,), (1,)), ((), ())), preferred_element_type=F32)


def split_hi_lo(values):
    hi = values.astype(BF16)
    lo = (values - hi.astype(F32)).astype(BF16)
    return hi, lo


def unit_quad(values, ones):
    hi, lo = split_hi_lo(values * values)
    total = dot(hi, ones) + dot(lo, ones)
    return values * lax.rsqrt(total + EPS)


def full(shape):
    return pl.BlockSpec(memory_space=pltpu.VMEM)


def smem():
    return pl.BlockSpec(memory_space=pltpu.SMEM)


def call(body, out_shape, args, in_smem, scratch=(), flops=0, nbytes=0):
    return pl.pallas_call(
        body,
        out_shape=out_shape,
        in_specs=[smem() if i in in_smem else full(None) for i in range(len(args))],
        out_specs=jax.tree.map(lambda _: full(None), out_shape),
        scratch_shapes=list(scratch),
        compiler_params=pltpu.CompilerParams(vmem_limit_bytes=VMEM_LIMIT),
        cost_estimate=pl.CostEstimate(flops=flops, bytes_accessed=nbytes, transcendentals=0),
    )(*args)


def gain_kernel(step, row, freqs, gain):
    angles = step[0].astype(F32) * freqs[...]
    features = jnp.concatenate([jnp.cos(angles), jnp.sin(angles)], axis=1)
    gain[...] = 1.0 + 0.5 * (row[...].astype(F32) + features)


def fine_kernel(
    start, windows, scales, own, left, right, up, down, gain, key_place, query_place,
    qkv, out_w, stream, tokens,
):
    width = own.shape[2]
    tokens[KEYS - 8 :] = jnp.zeros((8, width), F32)
    tokens[:OWN] = own[...].astype(F32).reshape(OWN, width)
    at = OWN
    for strip in (left, right):
        tokens[at : at + REACH * ROWS] = strip[...].astype(F32).reshape(REACH * ROWS, width)
        at += REACH * ROWS
    for strip in (up, down):
        for c in range(strip.shape[0]):
            tokens[at : at + REACH] = strip[c].astype(F32)
            at += REACH
    x = tokens[...]
    mean = jnp.mean(x * x, axis=-1, keepdims=True)
    n_all = (x * lax.rsqrt(mean + EPS) * gain[...]).astype(BF16)
    n_own = n_all[:OWN]
    row_k, col_k = key_place[0:1, :], key_place[1:2, :]
    row_q, col_q = query_place[:, 0:1], query_place[:, 1:2]
    row_g, col_g = row_k + start[0], col_k + start[1]
    inside = (row_g >= 0) & (row_g < start[2]) & (col_g >= 0) & (col_g < start[3])
    apart = jnp.maximum(jnp.abs(row_k - row_q), jnp.abs(col_k - col_q))
    apart = jnp.where(inside, apart, FAR)

    ones = block_ones()
    lane = lax.broadcasted_iota(jnp.int32, (OWN, 256), 1) // HEAD_DIM
    update = x[:OWN]
    for quad in range(width // 256):
        at = quad * 256
        query = unit_quad(dot(n_own, qkv[:, at : at + 256]), ones)
        key = unit_quad(dot(n_all, qkv[:, width + at : width + at + 256]), ones).astype(BF16)
        value = dot(n_all, qkv[:, 2 * width + at : 2 * width + at + 256]).astype(BF16)
        hi, lo = split_hi_lo(query)
        rows = [jnp.where(lane == h, hi, 0) for h in range(4)]
        rows += [jnp.where(lane == h, lo, 0) for h in range(4)]
        score = dot_t(jnp.concatenate(rows, axis=0), key)
        score = score[: 4 * OWN] + score[4 * OWN :]
        weights, totals = [], []
        for h in range(4):
            head = quad * 4 + h
            radius = (windows[head] - 1) // 2
            part = scales[head] * score[h * OWN : (h + 1) * OWN]
            part = jnp.where(apart <= radius, part, -jnp.inf)
            part = jnp.exp(part - jnp.max(part, axis=-1, keepdims=True))
            totals.append(jnp.sum(part, axis=-1, keepdims=True))
            weights.append(part.astype(BF16))
        mixed = dot(jnp.concatenate(weights, axis=0), value)
        att = jnp.zeros((OWN, 256), F32)
        for h in range(4):
            att = jnp.where(lane == h, mixed[h * OWN : (h + 1) * OWN] / totals[h], att)
        update = update + dot(att.astype(BF16), out_w[at : at + 256, :])
    result = dot(reorder(False), update.astype(BF16))
    for s in range(4):
        stream[s] = result[s * TOKENS : (s + 1) * TOKENS].astype(BF16)


def merge_kernel(place, p0, p1, p2, p3, mine, other, bottom, weight):
    width = p0.shape[2]
    half = mine.shape[0] * mine.shape[1] // 8
    for i in range(8):
        for ref, core in ((mine, place[1]), (other, 1 - place[1])):
            at = pl.multiple_of(i * 2 * half + core * half, half)
            weight[pl.ds(at, half), :] = ref[i * 8 : i * 8 + 8].reshape(half, ref.shape[2])
    acc = None
    for s in range(4):
        rows = jnp.concatenate([p[s].astype(F32) for p in (p0, p1, p2, p3)], axis=0).astype(BF16)
        term = dot(rows, weight[s * width : (s + 1) * width, :])
        acc = term if acc is None else acc + term
    for k in range(NX):
        bottom[lax.rem(place[0] + NX - k, NX)] = acc[k * TOKENS : (k + 1) * TOKENS].astype(BF16)


def project_kernel(place, p0, p1, p2, p3, weight, bottom, query, pairs, whole):
    block = p0.shape[2]
    ones = block_ones()
    for k, p in enumerate((p0, p1, p2, p3)):
        at = pl.multiple_of(lax.rem(place[0] + NX - k, NX) * block, 128)
        rows = jnp.concatenate([p[i].astype(F32) for i in range(NX)], axis=0)
        whole[:, pl.ds(at, block)] = rows
    x = whole[...]
    bottom[...] = x.astype(BF16)
    mean = jnp.mean(x * x, axis=-1, keepdims=True)
    normed = (x * lax.rsqrt(mean + EPS)).astype(BF16)
    proj = dot(normed, weight[...])
    first = proj[:, :256]
    lane = lax.broadcasted_iota(jnp.int32, first.shape, 1)
    first = jnp.where(lane < 192, unit_quad(first, ones), first)
    kv = jnp.concatenate([first, proj[:, 256:384]], axis=1).astype(BF16)
    for i in range(pairs.shape[0]):
        pairs[i] = kv
    query[...] = unit_quad(proj[:, 384:640], ones)


def attend_part(scales, place, query, ref):
    lane = lax.broadcasted_iota(jnp.int32, query.shape, 1) // HEAD_DIM
    count = query.shape[0]
    hi, lo = split_hi_lo(query[...])
    rows = [jnp.where(lane == h, hi, 0) for h in range(3)]
    rows += [jnp.where(lane == h, lo, 0) for h in range(3)]
    scale = jnp.concatenate(
        [jnp.full((count, 1), scales[3 * place[0] + h], F32) for h in range(3)], axis=0
    )
    score = dot_t(jnp.concatenate(rows, axis=0), ref[:, :256])
    score = scale * (score[: 3 * count] + score[3 * count :])
    highest = jnp.max(score, axis=-1, keepdims=True)
    part = jnp.exp(score - highest)
    total = jnp.sum(part, axis=-1, keepdims=True)
    return highest, total, dot(part.astype(BF16), ref[:, 128:384])


def near_kernel(scales, place, query, near, highest, total, acc):
    highest[...], total[...], acc[...] = attend_part(scales, place, query, near)


def far_kernel(scales, place, query, far, near_highest, near_total, near_acc, out):
    count = query.shape[0]
    highest, total, acc = attend_part(scales, place, query, far)
    top = jnp.maximum(highest, near_highest[...])
    fade, near_fade = jnp.exp(highest - top), jnp.exp(near_highest[...] - top)
    acc = acc * fade + near_acc[...] * near_fade
    acc = acc / (total * fade + near_total[...] * near_fade)
    lane = lax.broadcasted_iota(jnp.int32, query.shape, 1) // HEAD_DIM
    att = jnp.zeros((count, 256), F32)
    for h in range(3):
        att = jnp.where(lane == h + 1, acc[h * count : (h + 1) * count], att)
    out[...] = att[:, 64:].astype(BF16)


def output_kernel(place, p0, p1, p2, p3, bottom, out_w, split_w, split):
    acc = bottom[...].astype(F32)
    block = p0.shape[1]
    for k, p in enumerate((p0, p1, p2, p3)):
        at = pl.multiple_of(lax.rem(place[0] + NX - k, NX) * block, 64)
        acc = acc + dot(p[...], out_w[pl.ds(at, block), :])
    result = dot_t(acc.astype(BF16), split_w[...])
    for i in range(NX):
        split[i] = result[i * TOKENS : (i + 1) * TOKENS].astype(BF16)


def mix_kernel(place, stream, u0, u1, u2, u3, mix, out, upward):
    for k, u in enumerate((u0, u1, u2, u3)):
        upward[lax.rem(place[0] + NX - k, NX)] = u[...].astype(F32)
    s = jnp.concatenate([stream[i].astype(F32) for i in range(4)], axis=0)
    u = upward[...].reshape(OWN, out.shape[2])
    mixed = (s + mix[...] * (u - s)).astype(BF16)
    grid = dot(reorder(True), mixed)
    out[...] = grid.reshape(out.shape).astype(BF16)


def shift(x, axis, size, step):
    return lax.ppermute(x, axis, [(i, i + step) for i in range(size) if 0 <= i + step < size])


def gather_z(x):
    return [x] + [
        lax.ppermute(x, "z", [(i, (i + s) % NX) for i in range(NX)]) for s in range(1, NX)
    ]


def scatter_z(x):
    z = lax.axis_index("z")
    parts = [lax.dynamic_index_in_dim(x, (z + s) % NX, 0, keepdims=False) for s in range(NX)]
    return parts[:1] + [
        lax.ppermute(parts[s], "z", [(i, (i + s) % NX) for i in range(NX)]) for s in range(1, NX)
    ]


def swap_core(x):
    return lax.ppermute(x, "c", [(0, 1), (1, 0)])


def after(x, *others):
    return lax.optimization_barrier((x, *others))[0]


def merge_columns(merge_weight):
    rows, width = merge_weight.shape
    block = width // NX
    parts = jnp.stack([merge_weight[:, i * block : (i + 1) * block] for i in range(NX)])
    parts = jnp.broadcast_to(parts[:, None], (NX, 16, rows, block)).reshape(16 * NX, rows, block)
    return lax.all_to_all(parts, ("z", *REST), 0, 0)


def spread(chunk):
    return jnp.broadcast_to(chunk[None], (16, *chunk.shape))


def split_columns(mine):
    rows, depth = mine.shape[1:]
    other = swap_core(mine)
    c = lax.axis_index("c")
    first = jnp.where(c == 0, mine, other).reshape(2, 8, rows, depth)
    second = jnp.where(c == 0, other, mine).reshape(2, 8, rows, depth)
    return jnp.stack([first, second], axis=1).reshape(32 * rows, depth)


def shards(
    fine,
    class_table,
    label,
    timestep,
    windows,
    fine_scale,
    fine_qkv,
    fine_out,
    merge_weight,
    bottom_scale,
    bottom_qkv,
    bottom_out,
    split_weight,
    skip_mix,
):
    height, width, depth = fine.shape
    own = fine.transpose(1, 0, 2)
    left = shift(own[width - REACH :], GX, 8, 1)
    right = shift(own[:REACH], GX, 8, -1)
    wide = jnp.concatenate([left, own, right], axis=0)
    up = shift(wide[:, height - REACH :], GY, 16, 1)
    down = shift(wide[:, :REACH], GY, 16, -1)
    row = lax.dynamic_slice_in_dim(class_table, label[0], 1, 0)
    half = depth // 2
    freqs = np.exp(np.float32(-math.log(10000.0)) * np.arange(half, dtype=np.float32) / half)
    gain = call(
        gain_kernel,
        jax.ShapeDtypeStruct((1, depth), F32),
        [timestep, row, jnp.asarray(freqs[None], F32)],
        (0,),
    )
    start = jnp.stack(
        [
            lax.axis_index(GY) * height,
            lax.axis_index(GX) * width,
            jnp.int32(16 * height),
            jnp.int32(8 * width),
        ]
    ).astype(jnp.int32)
    place = jnp.stack([lax.axis_index("z"), lax.axis_index("c")]).astype(jnp.int32)

    merge_w = merge_columns(merge_weight)
    stream = call(
        fine_kernel,
        jax.ShapeDtypeStruct((4, TOKENS, depth), BF16),
        [
            start, windows, fine_scale, own, left, right, up, down, gain,
            jnp.asarray(PLACES.T.copy()), jnp.asarray(PLACES[:OWN].copy()), fine_qkv, fine_out,
        ],
        (0, 1, 2),
        [pltpu.VMEM((KEYS, depth), F32)],
        flops=2 * KEYS * depth * 3 * depth,
        nbytes=5 * 2**20,
    )
    streams = gather_z(stream)
    split_w = lax.all_to_all(after(spread(split_weight.T), merge_w, up, down), REST, 0, 0)
    merge_w = after(merge_w, stream)
    block = merge_w.shape[2]
    bottom = call(
        merge_kernel,
        jax.ShapeDtypeStruct((NX, TOKENS, block), BF16),
        [place, *streams, merge_w, swap_core(merge_w)],
        (0,),
        [pltpu.VMEM((4 * depth, block), BF16)],
        flops=2 * OWN * 4 * depth * block,
        nbytes=3 * 2**20,
    )
    battn = bottom_out.shape[0]
    group = battn // NX
    deep = bottom_qkv.shape[0]
    weight = after(bottom_qkv, bottom)
    at = lax.axis_index("z") * group
    picked = [
        lax.dynamic_slice_in_dim(weight, part * battn + at, group, 1) for part in (1, 2, 0)
    ]
    qkv_w = jnp.concatenate(picked + [jnp.zeros((deep, 64), BF16)], axis=1)
    bfull, query, pairs = call(
        project_kernel,
        (
            jax.ShapeDtypeStruct((OWN, deep), BF16),
            jax.ShapeDtypeStruct((OWN, 256), F32),
            jax.ShapeDtypeStruct((16, OWN, 2 * group), BF16),
        ),
        [place, *gather_z(bottom), qkv_w],
        (0,),
        [pltpu.VMEM((OWN, deep), F32)],
        flops=2 * OWN * deep * 640,
        nbytes=4 * 2**20,
    )
    pairs = after(pairs, split_w)
    near = lax.all_to_all(pairs, REST, 0, 0).reshape(16 * OWN, 2 * group)
    far = swap_core(near)
    near_part = call(
        near_kernel,
        (
            jax.ShapeDtypeStruct((3 * OWN, 1), F32),
            jax.ShapeDtypeStruct((3 * OWN, 1), F32),
            jax.ShapeDtypeStruct((3 * OWN, 256), F32),
        ),
        [bottom_scale, place, query, near],
        (0, 1),
        flops=2 * 3 * OWN * 1536 * 256 * 3,
        nbytes=2 * 2**20,
    )
    batt = call(
        far_kernel,
        jax.ShapeDtypeStruct((OWN, group), BF16),
        [bottom_scale, place, query, far, *near_part],
        (0, 1),
        flops=2 * 3 * OWN * 1536 * 256 * 3,
        nbytes=2 * 2**20,
    )
    split_w = split_columns(after(split_w, batt))
    split = call(
        output_kernel,
        jax.ShapeDtypeStruct((NX, TOKENS, depth), BF16),
        [place, *gather_z(batt), bfull, bottom_out, split_w],
        (0,),
        flops=2 * OWN * deep * 2 * depth,
        nbytes=5 * 2**20,
    )
    mixed = call(
        mix_kernel,
        jax.ShapeDtypeStruct((width, height, depth), BF16),
        [place, stream, *scatter_z(split), skip_mix[None]],
        (0,),
        [pltpu.VMEM((4, TOKENS, depth), F32)],
        flops=2 * 128 * 96 * depth,
        nbytes=2**20,
    )
    return mixed.transpose(1, 0, 2)


def solution(mesh):
    inner = Mesh(mesh.devices.reshape(4, 2, 2, 2, 4), ALL)
    placed = (
        P(GY, GX, None),
        P(),
        P(),
        P(),
        P(),
        P(),
        P(),
        P(),
        P(ALL, None),
        P(),
        P(),
        P(),
        P(None, ALL),
        P(),
    )
    return jax.shard_map(
        shards, mesh=inner, in_specs=placed, out_specs=P(GY, GX, None), check_vma=False
    )
```

time: 150 us -> 126 us (0.84)
  waiting for transfers between devices: 49.2 us -> 22.2 us
  blocking collectives: 0 us -> 23.2 us
  local copies, waits for them, and re-layouts: 27.4 us -> 10.1 us
  Pallas kernels: 12.5 us -> 15.8 us
  other arithmetic: 5.52 us -> 2.66 us
  starting transfers between devices: 52.1 us -> 50.1 us
    all_to_all x4 -> x2, waiting for transfers between devices: 36.1 us -> 0.01 us  [the longest x1 0.01 us: shards(): lax.all_to_all(after(spread(split_weight.T), merge_w, up, down), REST, 0, 0)]
    all_to_all x0 -> x1, blocking collectives: none -> 23.2 us  [shards(): near = lax.all_to_all(pairs, REST, 0, 0).reshape(16 * OWN, 2 * group)]
    ppermute x4, waiting for transfers between devices: 0.01 us -> 12.3 us  [shift(): lax.ppermute(x, axis, [(i, i + step) for i in range(size) if 0 <= i + ste...]
    all_to_all x4 -> x2, starting transfers between devices: 30.5 us -> 19.1 us  [the longest x1 11.6 us: merge_columns(): return lax.all_to_all(parts, ('z', *REST), 0, 0)]
    concatenate x3 -> x0, local copies, waits for them, and re-layouts: 7.38 us -> none  [the longest x1 7.29 us: shards(): jnp.concatenate([up.reshape(-1, depth), down.reshape(-1, depth), left, ri...]
    ppermute x10 -> x12, starting transfers between devices: 13.8 us -> 20 us  [the longest x9 15.6 us: gather_z(): lax.ppermute(x, 'z', [(i, (i + s) % NX) for i in range(NX)])]
    ppermute x3, starting transfers between devices: 0.09 us -> 3.65 us  [swap_core(): return lax.ppermute(x, 'c', [(0, 1), (1, 0)])]
    reshape x7 -> x0, local copies, waits for them, and re-layouts: 3.49 us -> none  [the longest x1 0.71 us: shards(): own = own.reshape(OWN, depth)]
  transfers between devices with their start and end apart: 21 -> 21, of which waited for: 10 -> 12; matrix products, arithmetic and copies ran while one was open for 17% -> 6% of each run, Pallas kernels for 5% -> 8%
where the time goes in v2:
time: 126 us
  starting transfers between devices  50.1 us (40%)
  blocking collectives  23.2 us (18%)
  waiting for transfers between devices  22.2 us (18%)
  Pallas kernels  15.8 us (13%)
  local copies, waits for them, and re-layouts  10.1 us (8%)
  other arithmetic  2.66 us (2%)
  between operations  1.6 us (1%)
    all_to_all x1, blocking collectives, shards(): near = lax.all_to_all(pairs, REST, 0, 0).reshape(16 * OWN, 2 * group)  23.2 us
    pallas_call x8, Pallas kernels, call(): pl.pallas_call(body, out_shape=out_shape, in_specs=[smem() if i in in_sme...  15.8 us
    ppermute x9, starting transfers between devices, gather_z(): lax.ppermute(x, 'z', [(i, (i + s) % NX) for i in range(NX)])  15.6 us
    ppermute x4, waiting for transfers between devices, shift(): lax.ppermute(x, axis, [(i, i + step) for i in range(size) if 0 <= i + ste...  12.3 us
    all_to_all x1, starting transfers between devices, merge_columns(): return lax.all_to_all(parts, ('z', *REST), 0, 0)  11.6 us
    all_to_all x1, starting transfers between devices, shards(): lax.all_to_all(after(spread(split_weight.T), merge_w, up, down), REST, 0, 0)  7.44 us
    ppermute x4, starting transfers between devices, shift(): lax.ppermute(x, axis, [(i, i + step) for i in range(size) if 0 <= i + ste...  7.36 us
    ppermute x9, waiting for transfers between devices, gather_z(): lax.ppermute(x, 'z', [(i, (i + s) % NX) for i in range(NX)])  6.03 us
  transfers between devices with their start and end apart: 21, of which 12 were waited for; matrix products, arithmetic and copies ran while one was open for 6% of the time, Pallas kernels for 8%

profile of v2, /device:TPU:0, one launch (start us, length us, event | category | flops | bytes accessed | tf_op | source)
XLA Modules:
  0.0 125.7 jit_solution(9359358809155203754)
XLA Ops:
  0.0 0.9 slice_bitcast_fusion.3
  0.9 0.0 copy-start.7
  1.0 1.1 broadcast_in_dim.8
  2.1 11.6 %all-to-all-start = ((bf16[64,24,384]{2,1,0:T(8,128)(2,1)}), bf16[64,24,384]{2,1,0:T(8,128)(2,1)S(1)}, u32[]{:S(2)}, u32[]{:S(2)}) async-start(bf16[64,24,384]{2,1,0:T(8,128)(2,1)} %bitcast.38), calls=%async_computation | async-start | bytes 2359296 | tf_op jit(solution)/shard_map/all_to_all | solution.py:288
  13.8 3.5 %collective-permute-start = (bf16[3,8,768]{2,1,0:T(8,128)(2,1)S(1)}, bf16[3,8,768]{2,1,0:T(8,128)(2,1)S(1)}, u32[]{:S(2)}, u32[]{:S(2)}) collective-permute-start(bf16[3,8,768]{2,1,0:T(8,128)(2,1)S(1)} %get-tuple-element.39), channel_id=1, source_target_pairs={{0,1},{1,2},{2,3},{3,4},{4,5},{5,6},{6,7},{8,9},{9,10},{10,11},{11... | collective-permute-start | bytes 110600 | tf_op jit(solution)/shard_map/ppermute | solution.py:258
  17.3 1.3 %collective-permute-start.1 = (bf16[3,8,768]{2,1,0:T(8,128)(2,1)S(1)}, bf16[3,8,768]{2,1,0:T(8,128)(2,1)S(1)}, u32[]{:S(2)}, u32[]{:S(2)}) collective-permute-start(bf16[3,8,768]{2,1,0:T(8,128)(2,1)S(1)} %get-tuple-element.38), channel_id=1, source_target_pairs={{1,0},{2,1},{3,2},{4,3},{5,4},{6,5},{7,6},{9,8},{10,9},{11,10},{12... | collective-permute-start | bytes 110600 | tf_op jit(solution)/shard_map/ppermute | solution.py:258
  19.9 0.1 shard_map.163.gain
  20.0 6.9 %collective-permute-done.left = bf16[3,8,768]{2,1,0:T(8,128)(2,1)S(1)} collective-permute-done((bf16[3,8,768]{2,1,0:T(8,128)(2,1)S(1)}, bf16[3,8,768]{2,1,0:T(8,128)(2,1)S(1)}, u32[]{:S(2)}, u32[]{:S(2)}) %collective-permute-start) | collective-permute-done | bytes 36896 | tf_op jit(solution)/shard_map/ppermute | solution.py:258
  26.8 1.9 %collective-permute-done.1.right = bf16[3,8,768]{2,1,0:T(8,128)(2,1)S(1)} collective-permute-done((bf16[3,8,768]{2,1,0:T(8,128)(2,1)S(1)}, bf16[3,8,768]{2,1,0:T(8,128)(2,1)S(1)}, u32[]{:S(2)}, u32[]{:S(2)}) %collective-permute-start.1) | collective-permute-done | bytes 36896 | tf_op jit(solution)/shard_map/ppermute | solution.py:258
  28.7 0.1 fusion
  28.8 1.3 %collective-permute-start.2 = (bf16[18,3,768]{2,1,0:T(4,128)(2,1)S(1)}, bf16[18,3,768]{2,1,0:T(4,128)(2,1)S(1)}, u32[]{:S(2)}, u32[]{:S(2)}) collective-permute-start(bf16[18,3,768]{2,1,0:T(4,128)(2,1)S(1)} %get-tuple-element.33), channel_id=1, source_target_pairs={{0,8},{8,16},{16,24},{24,32},{32,40},{40,48},{48,56},{56,64},{64,7... | collective-permute-start | bytes 248840 | tf_op jit(solution)/shard_map/ppermute | solution.py:258
  30.1 1.3 %collective-permute-start.3 = (bf16[18,3,768]{2,1,0:T(4,128)(2,1)S(1)}, bf16[18,3,768]{2,1,0:T(4,128)(2,1)S(1)}, u32[]{:S(2)}, u32[]{:S(2)}) collective-permute-start(bf16[18,3,768]{2,1,0:T(4,128)(2,1)S(1)} %get-tuple-element.32), channel_id=1, source_target_pairs={{8,0},{16,8},{24,16},{32,24},{40,32},{48,40},{56,48},{64,56},{72,6... | collective-permute-start | bytes 248840 | tf_op jit(solution)/shard_map/ppermute | solution.py:258
  31.4 0.1 pad_add_fusion.1.start
  31.5 0.0 collective-permute-done.2.up
  31.5 3.5 %collective-permute-done.3.down = bf16[18,3,768]{2,1,0:T(4,128)(2,1)S(1)} collective-permute-done((bf16[18,3,768]{2,1,0:T(4,128)(2,1)S(1)}, bf16[18,3,768]{2,1,0:T(4,128)(2,1)S(1)}, u32[]{:S(2)}, u32[]{:S(2)}) %collective-permute-start.3) | collective-permute-done | bytes 82976 | tf_op jit(solution)/shard_map/ppermute | solution.py:258
  35.1 0.0 copy-start.1
  35.1 2.0 %copy-done.1 = bf16[768,2304]{1,0:T(8,128)(2,1)S(1)} copy-done((bf16[768,2304]{1,0:T(8,128)(2,1)S(1)}, bf16[768,2304]{1,0:T(8,128)(2,1)}, u32[]{:S(2)}) %copy-start.1) | copy-done | bytes 3538968
  37.1 1.3 %copy-done.3 = bf16[768,768]{1,0:T(8,128)(2,1)S(1)} copy-done((bf16[768,768]{1,0:T(8,128)(2,1)S(1)}, bf16[768,768]{1,0:T(8,128)(2,1)}, u32[]{:S(2)}) %copy-start.3) | copy-done | bytes 1179672
  38.3 4.9 %shard_map.164.p0.stream = bf16[4,24,768]{2,1,0:T(8,128)(2,1)S(1)} custom-call(s32[4]{0:T(128)S(1)} %pad_add_fusion.1.start, s32[12]{0:T(128)S(1)} %copy-done.8, f32[12]{0:T(128)S(1)} %copy-done.9, bf16[12,8,768]{2,1,0:T(8,128)(2,1)S(1)} %bitcast.37, bf16[3,8,768]{2,1,0:T(8,128)(2,1)S(1)} %collective-permute-done.left, ...), custom_call_target="tpu_custom_call" | custom-call | flops 905969664 | bytes 5242880 | tf_op jit(solution)/shard_map/pallas_call | solution.py:89
  43.2 3.4 %collective-permute-start.7 = (bf16[64,24,384]{2,1,0:T(8,128)(2,1)S(1)}, bf16[64,24,384]{2,1,0:T(8,128)(2,1)}, u32[]{:S(2)}, u32[]{:S(2)}) collective-permute-start(bf16[64,24,384]{2,1,0:T(8,128)(2,1)S(1)} %all-to-all-done.mine), channel_id=1, source_target_pairs={{0,8},{8,0},{1,9},{9,1},{2,10},{10,2},{3,11},{11,3},{4,12},{12,4},... | collective-permute-start | bytes 3538952 | tf_op jit(solution)/shard_map/ppermute | solution.py:276
  46.7 1.1 broadcast_in_dim.20
  47.8 7.4 %all-to-all-start.1 = ((bf16[16,24,1536]{2,1,0:T(8,128)(2,1)}), bf16[16,24,1536]{2,1,0:T(8,128)(2,1)}, u32[]{:S(2)}, u32[]{:S(2)}) async-start(bf16[16,24,1536]{2,1,0:T(8,128)(2,1)} %broadcast_in_dim.20), calls=%async_computation.1 | async-start | bytes 2359296 | tf_op jit(solution)/shard_map/all_to_all | solution.py:360
  55.2 1.6 %collective-permute-start.4 = (bf16[4,24,768]{2,1,0:T(8,128)(2,1)S(1)}, bf16[4,24,768]{2,1,0:T(8,128)(2,1)S(1)}, u32[]{:S(2)}, u32[]{:S(2)}) collective-permute-start(bf16[4,24,768]{2,1,0:T(8,128)(2,1)S(1)} %shard_map.164.p0.stream), channel_id=1, source_target_pairs={{0,32},{32,64},{64,96},{96,0},{1,33},{33,65},{65,97},{97,1},{2,34}... | collective-permute-start | bytes 442376 | tf_op jit(solution)/shard_map/ppermute | solution.py:263
  56.9 1.6 %collective-permute-start.5 = (bf16[4,24,768]{2,1,0:T(8,128)(2,1)S(1)}, bf16[4,24,768]{2,1,0:T(8,128)(2,1)S(1)}, u32[]{:S(2)}, u32[]{:S(2)}) collective-permute-start(bf16[4,24,768]{2,1,0:T(8,128)(2,1)S(1)} %shard_map.164.p0.stream), channel_id=1, source_target_pairs={{0,64},{32,96},{64,0},{96,32},{1,65},{33,97},{65,1},{97,33},{2,66}... | collective-permute-start | bytes 442376 | tf_op jit(solution)/shard_map/ppermute | solution.py:263
  58.5 2.3 %collective-permute-start.6 = (bf16[4,24,768]{2,1,0:T(8,128)(2,1)S(1)}, bf16[4,24,768]{2,1,0:T(8,128)(2,1)S(1)}, u32[]{:S(2)}, u32[]{:S(2)}) collective-permute-start(bf16[4,24,768]{2,1,0:T(8,128)(2,1)S(1)} %shard_map.164.p0.stream), channel_id=1, source_target_pairs={{0,96},{32,0},{64,32},{96,64},{1,97},{33,1},{65,33},{97,65},{2,98}... | collective-permute-start | bytes 442376 | tf_op jit(solution)/shard_map/ppermute | solution.py:263
  60.8 0.1 pad.5.clone
  60.9 0.1 pad_add_fusion.place
  61.0 2.3 %collective-permute-done.4.p1 = bf16[4,24,768]{2,1,0:T(8,128)(2,1)S(1)} collective-permute-done((bf16[4,24,768]{2,1,0:T(8,128)(2,1)S(1)}, bf16[4,24,768]{2,1,0:T(8,128)(2,1)S(1)}, u32[]{:S(2)}, u32[]{:S(2)}) %collective-permute-start.4) | collective-permute-done | bytes 147488 | tf_op jit(solution)/shard_map/ppermute | solution.py:263
  63.3 1.9 %collective-permute-done.5.p2 = bf16[4,24,768]{2,1,0:T(8,128)(2,1)S(1)} collective-permute-done((bf16[4,24,768]{2,1,0:T(8,128)(2,1)S(1)}, bf16[4,24,768]{2,1,0:T(8,128)(2,1)S(1)}, u32[]{:S(2)}, u32[]{:S(2)}) %collective-permute-start.5) | collective-permute-done | bytes 147488 | tf_op jit(solution)/shard_map/ppermute | solution.py:263
  65.1 0.6 collective-permute-done.6.p3
  65.7 0.0 collective-permute-done.7.other
  65.7 2.0 %shard_map.165.p0 = bf16[4,24,384]{2,1,0:T(8,128)(2,1)S(1)} custom-call(s32[2]{0:T(128)S(1)} %pad_add_fusion.place, bf16[4,24,768]{2,1,0:T(8,128)(2,1)S(1)} %shard_map.164.p0.stream, bf16[4,24,768]{2,1,0:T(8,128)(2,1)S(1)} %collective-permute-done.4.p1, bf16[4,24,768]{2,1,0:T(8,128)(2,1)S(1)} %collective-permute-done.5.p2, ...), custom_call_target="tpu_custom_call" | custom-call | flops 226492416 | bytes 3145728 | tf_op jit(solution)/shard_map/pallas_call | solution.py:89
  67.8 2.8 %collective-permute-start.10 = (bf16[4,24,384]{2,1,0:T(8,128)(2,1)S(1)}, bf16[4,24,384]{2,1,0:T(8,128)(2,1)S(1)}, u32[]{:S(2)}, u32[]{:S(2)}) collective-permute-start(bf16[4,24,384]{2,1,0:T(8,128)(2,1)S(1)} %shard_map.165.p0), channel_id=1, source_target_pairs={{0,96},{32,0},{64,32},{96,64},{1,97},{33,1},{65,33},{97,65},{2,98}... | collective-permute-start | bytes 221192 | tf_op jit(solution)/shard_map/ppermute | solution.py:263
  70.6 0.0 collective-permute-start.8
  70.6 2.2 %collective-permute-start.9 = (bf16[4,24,384]{2,1,0:T(8,128)(2,1)S(1)}, bf16[4,24,384]{2,1,0:T(8,128)(2,1)S(1)}, u32[]{:S(2)}, u32[]{:S(2)}) collective-permute-start(bf16[4,24,384]{2,1,0:T(8,128)(2,1)S(1)} %shard_map.165.p0), channel_id=1, source_target_pairs={{0,64},{32,96},{64,0},{96,32},{1,65},{33,97},{65,1},{97,33},{2,66}... | collective-permute-start | bytes 221192 | tf_op jit(solution)/shard_map/ppermute | solution.py:263
  72.8 3.2 %constant_dynamic-slice_fusion.2 = (bf16[1536,192]{1,0:T(8,128)(2,1)S(1)}, bf16[1536,192]{1,0:T(8,128)(2,1)S(1)}, bf16[1536,192]{1,0:T(8,128)(2,1)S(1)}) fusion(bf16[1536,2304]{1,0:T(8,128)(2,1)} %param.27, s32[]{:T(128)S(6)} %select_n.57, s32[]{:T(128)S(6)} %select_n.59, s32[]{:T(128)S(6)} %select_n.58), kind=kLoop, calls=%fused_computation.16 | loop fusion | bytes 3538956 | tf_op jit(solution)/shard_map/dynamic_slice | solution.py:378
  76.0 0.8 maximum_maximum_fusion.weight
  76.8 0.0 copy-start.10
  76.8 0.0 collective-permute-done.10.p3
  76.9 0.1 collective-permute-done.8.p1
  76.9 1.4 %shard_map.166 = (bf16[96,1536]{1,0:T(8,128)(2,1)S(1)}, f32[96,256]{1,0:T(8,128)S(1)}, bf16[16,96,384]{2,1,0:T(8,128)(2,1)S(1)}) custom-call(s32[2]{0:T(128)S(1)} %pad_add_fusion.place, bf16[4,24,384]{2,1,0:T(8,128)(2,1)S(1)} %shard_map.165.p0, bf16[4,24,384]{2,1,0:T(8,128)(2,1)S(1)} %collective-permute-done.8.p1, ...), custom_call_target="tpu_custom_call" | custom-call | flops 188743680 | bytes 4194304 | tf_op jit(solution)/shard_map/pallas_call | solution.py:89
  78.3 23.2 %all_to_all.15 = bf16[16,96,384]{2,1,0:T(8,128)(2,1)S(1)} all-to-all(bf16[16,96,384]{2,1,0:T(8,128)(2,1)S(1)} %get-tuple-element.21), channel_id=1, replica_groups=mesh['z'=4,'yl'=2,'c'=2,'yh'=2,'x'=4] {'yl','yh','x'}, dimensions={0} | all-to-all | bytes 2359296 | tf_op jit(solution)/shard_map/all_to_all | solution.py:395
  101.5 0.0 collective-permute-start.11
  101.5 2.2 %shard_map.167 = (f32[288,1]{1,0:T(8,128)S(1)}, f32[288,1]{1,0:T(8,128)S(1)}, f32[288,256]{1,0:T(8,128)S(1)}) custom-call(f32[12]{0:T(128)S(1)} %copy-done.10, s32[2]{0:T(128)S(1)} %pad_add_fusion.place, f32[96,256]{1,0:T(8,128)S(1)} %get-tuple-element.18.query, bf16[1536,384]{1,0:T(8,128)(2,1)S(1)} %bitcast.34), custom_call_target="tpu_custom_call" | custom-call | flops 679477248 | bytes 2097152 | tf_op jit(solution)/shard_map/pallas_call | solution.py:89
  103.7 0.6 collective-permute-done.11.far
  104.3 2.2 %shard_map.168.p0 = bf16[96,192]{1,0:T(8,128)(2,1)S(1)} custom-call(f32[12]{0:T(128)S(1)} %copy-done.10, s32[2]{0:T(128)S(1)} %pad_add_fusion.place, f32[96,256]{1,0:T(8,128)S(1)} %get-tuple-element.18.query, bf16[1536,384]{1,0:T(8,128)(2,1)S(1)} %collective-permute-done.11.far, f32[288,1]{1,0:T(8,128)S(1)} %get-tuple-element.22.near_highest, ...), custom_call_target="tpu_custom_call" | custom-call | flops 679477248 | bytes 2097152 | tf_op jit(solution)/shard_map/pallas_call | solution.py:89
  106.5 0.2 collective-permute-start.15
  106.8 2.2 %collective-permute-start.12 = (bf16[96,192]{1,0:T(8,128)(2,1)S(1)}, bf16[96,192]{1,0:T(8,128)(2,1)S(1)}, u32[]{:S(2)}, u32[]{:S(2)}) collective-permute-start(bf16[96,192]{1,0:T(8,128)(2,1)S(1)} %shard_map.168.p0), channel_id=1, source_target_pairs={{0,32},{32,64},{64,96},{96,0},{1,33},{33,65},{65,97},{97,1},{2,34}... | collective-permute-start | bytes 110600 | tf_op jit(solution)/shard_map/ppermute | solution.py:263
  109.0 1.5 %collective-permute-start.13 = (bf16[96,192]{1,0:T(8,128)(2,1)S(1)}, bf16[96,192]{1,0:T(8,128)(2,1)S(1)}, u32[]{:S(2)}, u32[]{:S(2)}) collective-permute-start(bf16[96,192]{1,0:T(8,128)(2,1)S(1)} %shard_map.168.p0), channel_id=1, source_target_pairs={{0,64},{32,96},{64,0},{96,32},{1,65},{33,97},{65,1},{97,33},{2,66}... | collective-permute-start | bytes 110600 | tf_op jit(solution)/shard_map/ppermute | solution.py:263
  110.5 1.2 collective-permute-start.14
  111.7 1.4 %broadcast_select_fusion.1 = (bf16[16,24,1536]{2,1,0:T(8,128)(2,1)S(1)}, bf16[16,24,1536]{2,1,0:T(8,128)(2,1)S(1)}) fusion(bf16[16,24,1536]{2,1,0:T(8,128)(2,1)} %all-to-all-done.1, bf16[16,24,1536]{2,1,0:T(8,128)(2,1)S(1)} %collective-permute-done.15, pred[]{:T(512)S(6)} %eq.9), kind=kLoop, calls=%fused_computation.3 | loop fusion | flops 1179648 | bytes 4718593 | tf_op jit(solution)/shard_map/jit(_where)/select_n | solution.py:299
  113.2 0.0 copy-start.2
  113.2 0.2 pad_maximum_fusion
  113.4 1.2 collective-permute-done.13.p2
  114.6 0.0 collective-permute-done.14.p3
  114.6 0.2 copy-done.2
  114.8 1.7 %shard_map.169 = bf16[4,24,768]{2,1,0:T(8,128)(2,1)S(1)} custom-call(s32[2]{0:T(128)S(1)} %pad_add_fusion.place, bf16[96,192]{1,0:T(8,128)(2,1)S(1)} %shard_map.168.p0, bf16[96,192]{1,0:T(8,128)(2,1)S(1)} %collective-permute-done.12.p1, bf16[96,192]{1,0:T(8,128)(2,1)S(1)} %collective-permute-done.13.p2, bf16[96,192]{1,0:T(8,128)(2,1)S(1)} %collective-permute-done.14.p3, ...), custom_call_target="tpu_custom_call" | custom-call | flops 452984832 | bytes 5242880 | tf_op jit(solution)/shard_map/pallas_call | solution.py:89
  116.5 0.9 collective-permute-start.16
  117.4 2.9 %collective-permute-start.17 = (bf16[24,768]{1,0:T(8,128)(2,1)S(1)}, bf16[24,768]{1,0:T(8,128)(2,1)S(1)}, u32[]{:S(2)}, u32[]{:S(2)}) collective-permute-start(bf16[24,768]{1,0:T(8,128)(2,1)S(1)} %get-tuple-element.35), channel_id=1, source_target_pairs={{0,64},{32,96},{64,0},{96,32},{1,65},{33,97},{65,1},{97,33},{2,66}... | collective-permute-start | bytes 110600 | tf_op jit(solution)/shard_map/ppermute | solution.py:271
  120.3 0.7 collective-permute-start.18
  121.0 0.8 collective-permute-done.16.u1
  121.8 1.1 collective-permute-done.17.u2
  122.9 1.4 %collective-permute-done.18.u3 = bf16[24,768]{1,0:T(8,128)(2,1)S(1)} collective-permute-done((bf16[24,768]{1,0:T(8,128)(2,1)S(1)}, bf16[24,768]{1,0:T(8,128)(2,1)S(1)}, u32[]{:S(2)}, u32[]{:S(2)}) %collective-permute-start.18) | collective-permute-done | bytes 36896 | tf_op jit(solution)/shard_map/ppermute | solution.py:271
  124.2 1.4 %shard_map.170 = bf16[12,8,768]{2,1,0:T(8,128)(2,1)} custom-call(s32[2]{0:T(128)S(1)} %pad_add_fusion.place, bf16[4,24,768]{2,1,0:T(8,128)(2,1)S(1)} %shard_map.164.p0.stream, bf16[24,768]{1,0:T(8,128)(2,1)S(1)} %get-tuple-element.37.u0, bf16[24,768]{1,0:T(8,128)(2,1)S(1)} %collective-permute-done.16.u1, bf16[24,768]{1,0:T(8,128)(2,1)S(1)} %collective-permute-done.17.u2, ...), custom_call_target="tpu_custom_call" | custom-call | flops 18874368 | bytes 1048576 | tf_op jit(solution)/shard_map/pallas_call | solution.py:89
  (31 shorter events, 0.1 us)
Async XLA Ops:
  0.0 19.2 %copy-start = (bf16[1000,768]{1,0:T(8,128)(2,1)S(1)}, bf16[1000,768]{1,0:T(8,128)(2,1)}, u32[]{:S(2)}) copy-start(bf16[1000,768]{1,0:T(8,128)(2,1)} %param.18) | copy-start | bytes 4608004
  0.0 13.7 %copy-start.4 = (bf16[8,12,768]{2,0,1:T(8,128)(2,1)S(1)}, bf16[8,12,768]{2,0,1:T(8,128)(2,1)}, u32[]{:S(2)}) copy-start(bf16[8,12,768]{2,0,1:T(8,128)(2,1)} %param.17) | copy-start | bytes 442372
  0.9 19.0 %copy-start.7 = (f32[1,384]{1,0:T(1,128)S(1)}, f32[1,384]{1,0:T(1,128)}, u32[]{:S(2)}) copy-start(f32[1,384]{1,0:T(1,128)} %constant.91.clone.freqs) | copy-start | bytes 4612
  2.1 33.0 %copy-start.5 = (s32[96,2]{1,0:T(8,128)S(1)}, s32[96,2]{1,0:T(8,128)}, u32[]{:S(2)}) copy-start(s32[96,2]{1,0:T(8,128)} %constant.93.clone.query_place) | copy-start | bytes 2308
  2.1 33.0 %copy-start.6 = (s32[2,256]{1,0:T(2,128)S(1)}, s32[2,256]{1,0:T(2,128)}, u32[]{:S(2)}) copy-start(s32[2,256]{1,0:T(2,128)} %constant.92.clone.key_place) | copy-start | bytes 6148
  2.1 33.0 %copy-start.8 = (s32[12]{0:T(128)S(1)}, s32[12]{0:T(128)}, u32[]{:S(2)}) copy-start(s32[12]{0:T(128)} %windows.1) | copy-start | bytes 148
  2.1 33.0 %copy-start.9 = (f32[12]{0:T(128)S(1)}, f32[12]{0:T(128)}, u32[]{:S(2)}) copy-start(f32[12]{0:T(128)} %scales.3) | copy-start | bytes 148
  2.1 41.1 %all-to-all-start = ((bf16[64,24,384]{2,1,0:T(8,128)(2,1)}), bf16[64,24,384]{2,1,0:T(8,128)(2,1)S(1)}, u32[]{:S(2)}, u32[]{:S(2)}) async-start(bf16[64,24,384]{2,1,0:T(8,128)(2,1)} %bitcast.38), calls=%async_computation | async-start | bytes 2359296 | tf_op jit(solution)/shard_map/all_to_all | solution.py:288
  13.8 13.1 %collective-permute-start = (bf16[3,8,768]{2,1,0:T(8,128)(2,1)S(1)}, bf16[3,8,768]{2,1,0:T(8,128)(2,1)S(1)}, u32[]{:S(2)}, u32[]{:S(2)}) collective-permute-start(bf16[3,8,768]{2,1,0:T(8,128)(2,1)S(1)} %get-tuple-element.39), channel_id=1, source_target_pairs={{0,1},{1,2},{2,3},{3,4},{4,5},{5,6},{6,7},{8,9},{9,10},{10,11},{11... | collective-permute-start | bytes 110600 | tf_op jit(solution)/shard_map/ppermute | solution.py:258
  17.3 11.5 %collective-permute-start.1 = (bf16[3,8,768]{2,1,0:T(8,128)(2,1)S(1)}, bf16[3,8,768]{2,1,0:T(8,128)(2,1)S(1)}, u32[]{:S(2)}, u32[]{:S(2)}) collective-permute-start(bf16[3,8,768]{2,1,0:T(8,128)(2,1)S(1)} %get-tuple-element.38), channel_id=1, source_target_pairs={{1,0},{2,1},{3,2},{4,3},{5,4},{6,5},{7,6},{9,8},{10,9},{11,10},{12... | collective-permute-start | bytes 110600 | tf_op jit(solution)/shard_map/ppermute | solution.py:258
  28.8 2.7 %collective-permute-start.2 = (bf16[18,3,768]{2,1,0:T(4,128)(2,1)S(1)}, bf16[18,3,768]{2,1,0:T(4,128)(2,1)S(1)}, u32[]{:S(2)}, u32[]{:S(2)}) collective-permute-start(bf16[18,3,768]{2,1,0:T(4,128)(2,1)S(1)} %get-tuple-element.33), channel_id=1, source_target_pairs={{0,8},{8,16},{16,24},{24,32},{32,40},{40,48},{48,56},{56,64},{64,7... | collective-permute-start | bytes 248840 | tf_op jit(solution)/shard_map/ppermute | solution.py:258
  30.1 4.9 %collective-permute-start.3 = (bf16[18,3,768]{2,1,0:T(4,128)(2,1)S(1)}, bf16[18,3,768]{2,1,0:T(4,128)(2,1)S(1)}, u32[]{:S(2)}, u32[]{:S(2)}) collective-permute-start(bf16[18,3,768]{2,1,0:T(4,128)(2,1)S(1)} %get-tuple-element.32), channel_id=1, source_target_pairs={{8,0},{16,8},{24,16},{32,24},{40,32},{48,40},{56,48},{64,56},{72,6... | collective-permute-start | bytes 248840 | tf_op jit(solution)/shard_map/ppermute | solution.py:258
  35.1 2.0 %copy-start.1 = (bf16[768,2304]{1,0:T(8,128)(2,1)S(1)}, bf16[768,2304]{1,0:T(8,128)(2,1)}, u32[]{:S(2)}) copy-start(bf16[768,2304]{1,0:T(8,128)(2,1)} %qkv.1) | copy-start | bytes 10616836
  37.1 1.3 %copy-start.3 = (bf16[768,768]{1,0:T(8,128)(2,1)S(1)}, bf16[768,768]{1,0:T(8,128)(2,1)}, u32[]{:S(2)}) copy-start(bf16[768,768]{1,0:T(8,128)(2,1)} %out_w.2) | copy-start | bytes 3538948
  38.3 8.3 %copy-start.11 = (bf16[1536,24]{0,1:T(8,128)(2,1)S(1)}, bf16[1536,24]{0,1:T(8,128)(2,1)}, u32[]{:S(2)}) copy-start(bf16[1536,24]{0,1:T(8,128)(2,1)} %param.29) | copy-start | bytes 221188
  43.2 22.5 %collective-permute-start.7 = (bf16[64,24,384]{2,1,0:T(8,128)(2,1)S(1)}, bf16[64,24,384]{2,1,0:T(8,128)(2,1)}, u32[]{:S(2)}, u32[]{:S(2)}) collective-permute-start(bf16[64,24,384]{2,1,0:T(8,128)(2,1)S(1)} %all-to-all-done.mine), channel_id=1, source_target_pairs={{0,8},{8,0},{1,9},{9,1},{2,10},{10,2},{3,11},{11,3},{4,12},{12,4},... | collective-permute-start | bytes 3538952 | tf_op jit(solution)/shard_map/ppermute | solution.py:276
  47.8 30.5 %all-to-all-start.1 = ((bf16[16,24,1536]{2,1,0:T(8,128)(2,1)}), bf16[16,24,1536]{2,1,0:T(8,128)(2,1)}, u32[]{:S(2)}, u32[]{:S(2)}) async-start(bf16[16,24,1536]{2,1,0:T(8,128)(2,1)} %broadcast_in_dim.20), calls=%async_computation.1 | async-start | bytes 2359296 | tf_op jit(solution)/shard_map/all_to_all | solution.py:360
  55.2 8.0 %collective-permute-start.4 = (bf16[4,24,768]{2,1,0:T(8,128)(2,1)S(1)}, bf16[4,24,768]{2,1,0:T(8,128)(2,1)S(1)}, u32[]{:S(2)}, u32[]{:S(2)}) collective-permute-start(bf16[4,24,768]{2,1,0:T(8,128)(2,1)S(1)} %shard_map.164.p0.stream), channel_id=1, source_target_pairs={{0,32},{32,64},{64,96},{96,0},{1,33},{33,65},{65,97},{97,1},{2,34}... | collective-permute-start | bytes 442376 | tf_op jit(solution)/shard_map/ppermute | solution.py:263
  56.9 8.3 %collective-permute-start.5 = (bf16[4,24,768]{2,1,0:T(8,128)(2,1)S(1)}, bf16[4,24,768]{2,1,0:T(8,128)(2,1)S(1)}, u32[]{:S(2)}, u32[]{:S(2)}) collective-permute-start(bf16[4,24,768]{2,1,0:T(8,128)(2,1)S(1)} %shard_map.164.p0.stream), channel_id=1, source_target_pairs={{0,64},{32,96},{64,0},{96,32},{1,65},{33,97},{65,1},{97,33},{2,66}... | collective-permute-start | bytes 442376 | tf_op jit(solution)/shard_map/ppermute | solution.py:263
  58.5 7.2 %collective-permute-start.6 = (bf16[4,24,768]{2,1,0:T(8,128)(2,1)S(1)}, bf16[4,24,768]{2,1,0:T(8,128)(2,1)S(1)}, u32[]{:S(2)}, u32[]{:S(2)}) collective-permute-start(bf16[4,24,768]{2,1,0:T(8,128)(2,1)S(1)} %shard_map.164.p0.stream), channel_id=1, source_target_pairs={{0,96},{32,0},{64,32},{96,64},{1,97},{33,1},{65,33},{97,65},{2,98}... | collective-permute-start | bytes 442376 | tf_op jit(solution)/shard_map/ppermute | solution.py:263
  67.8 9.1 %collective-permute-start.10 = (bf16[4,24,384]{2,1,0:T(8,128)(2,1)S(1)}, bf16[4,24,384]{2,1,0:T(8,128)(2,1)S(1)}, u32[]{:S(2)}, u32[]{:S(2)}) collective-permute-start(bf16[4,24,384]{2,1,0:T(8,128)(2,1)S(1)} %shard_map.165.p0), channel_id=1, source_target_pairs={{0,96},{32,0},{64,32},{96,64},{1,97},{33,1},{65,33},{97,65},{2,98}... | collective-permute-start | bytes 221192 | tf_op jit(solution)/shard_map/ppermute | solution.py:263
  70.6 6.4 %collective-permute-start.8 = (bf16[4,24,384]{2,1,0:T(8,128)(2,1)S(1)}, bf16[4,24,384]{2,1,0:T(8,128)(2,1)S(1)}, u32[]{:S(2)}, u32[]{:S(2)}) collective-permute-start(bf16[4,24,384]{2,1,0:T(8,128)(2,1)S(1)} %shard_map.165.p0), channel_id=1, source_target_pairs={{0,32},{32,64},{64,96},{96,0},{1,33},{33,65},{65,97},{97,1},{2,34}... | collective-permute-start | bytes 221192 | tf_op jit(solution)/shard_map/ppermute | solution.py:263
  70.6 6.4 %collective-permute-start.9 = (bf16[4,24,384]{2,1,0:T(8,128)(2,1)S(1)}, bf16[4,24,384]{2,1,0:T(8,128)(2,1)S(1)}, u32[]{:S(2)}, u32[]{:S(2)}) collective-permute-start(bf16[4,24,384]{2,1,0:T(8,128)(2,1)S(1)} %shard_map.165.p0), channel_id=1, source_target_pairs={{0,64},{32,96},{64,0},{96,32},{1,65},{33,97},{65,1},{97,33},{2,66}... | collective-permute-start | bytes 221192 | tf_op jit(solution)/shard_map/ppermute | solution.py:263
  76.8 24.7 %copy-start.10 = (f32[12]{0:T(128)S(1)}, f32[12]{0:T(128)}, u32[]{:S(2)}) copy-start(f32[12]{0:T(128)} %scales.5) | copy-start | bytes 148
  101.5 2.8 %collective-permute-start.11 = (bf16[1536,384]{1,0:T(8,128)(2,1)S(1)}, bf16[1536,384]{1,0:T(8,128)(2,1)S(1)}, u32[]{:S(2)}, u32[]{:S(2)}) collective-permute-start(bf16[1536,384]{1,0:T(8,128)(2,1)S(1)} %bitcast.33), channel_id=1, source_target_pairs={{0,8},{8,0},{1,9},{9,1},{2,10},{10,2},{3,11},{11,3},{4,12},{12,4},... | collective-permute-start | bytes 3538952 | tf_op jit(solution)/shard_map/ppermute | solution.py:276
  106.5 5.2 %collective-permute-start.15 = (bf16[16,24,1536]{2,1,0:T(8,128)(2,1)}, bf16[16,24,1536]{2,1,0:T(8,128)(2,1)S(1)}, u32[]{:S(2)}, u32[]{:S(2)}) collective-permute-start(bf16[16,24,1536]{2,1,0:T(8,128)(2,1)} %all-to-all-done.1), channel_id=1, source_target_pairs={{0,8},{8,0},{1,9},{9,1},{2,10},{10,2},{3,11},{11,3},{4,12},{12,4},... | collective-permute-start | bytes 3538952 | tf_op jit(solution)/shard_map/ppermute | solution.py:276
  106.8 6.6 %collective-permute-start.12 = (bf16[96,192]{1,0:T(8,128)(2,1)S(1)}, bf16[96,192]{1,0:T(8,128)(2,1)S(1)}, u32[]{:S(2)}, u32[]{:S(2)}) collective-permute-start(bf16[96,192]{1,0:T(8,128)(2,1)S(1)} %shard_map.168.p0), channel_id=1, source_target_pairs={{0,32},{32,64},{64,96},{96,0},{1,33},{33,65},{65,97},{97,1},{2,34}... | collective-permute-start | bytes 110600 | tf_op jit(solution)/shard_map/ppermute | solution.py:263
  109.0 5.6 %collective-permute-start.13 = (bf16[96,192]{1,0:T(8,128)(2,1)S(1)}, bf16[96,192]{1,0:T(8,128)(2,1)S(1)}, u32[]{:S(2)}, u32[]{:S(2)}) collective-permute-start(bf16[96,192]{1,0:T(8,128)(2,1)S(1)} %shard_map.168.p0), channel_id=1, source_target_pairs={{0,64},{32,96},{64,0},{96,32},{1,65},{33,97},{65,1},{97,33},{2,66}... | collective-permute-start | bytes 110600 | tf_op jit(solution)/shard_map/ppermute | solution.py:263
  110.5 4.1 %collective-permute-start.14 = (bf16[96,192]{1,0:T(8,128)(2,1)S(1)}, bf16[96,192]{1,0:T(8,128)(2,1)S(1)}, u32[]{:S(2)}, u32[]{:S(2)}) collective-permute-start(bf16[96,192]{1,0:T(8,128)(2,1)S(1)} %shard_map.168.p0), channel_id=1, source_target_pairs={{0,96},{32,0},{64,32},{96,64},{1,97},{33,1},{65,33},{97,65},{2,98}... | collective-permute-start | bytes 110600 | tf_op jit(solution)/shard_map/ppermute | solution.py:263
  113.2 1.7 %copy-start.2 = (bf16[768,1536]{1,0:T(8,128)(2,1)S(1)}, bf16[768,1536]{1,0:T(8,128)(2,1)}, u32[]{:S(2)}) copy-start(bf16[768,1536]{1,0:T(8,128)(2,1)} %out_w.3) | copy-start | bytes 7077892
  114.8 6.2 %copy-start.12 = (f32[768]{0:T(1024)S(1)}, f32[768]{0:T(1024)}, u32[]{:S(2)}) copy-start(f32[768]{0:T(1024)} %param.30) | copy-start | bytes 9220
  116.5 5.2 %collective-permute-start.16 = (bf16[24,768]{1,0:T(8,128)(2,1)S(1)}, bf16[24,768]{1,0:T(8,128)(2,1)S(1)}, u32[]{:S(2)}, u32[]{:S(2)}) collective-permute-start(bf16[24,768]{1,0:T(8,128)(2,1)S(1)} %get-tuple-element.36), channel_id=1, source_target_pairs={{0,32},{32,64},{64,96},{96,0},{1,33},{33,65},{65,97},{97,1},{2,34}... | collective-permute-start | bytes 110600 | tf_op jit(solution)/shard_map/ppermute | solution.py:271
  117.4 5.5 %collective-permute-start.17 = (bf16[24,768]{1,0:T(8,128)(2,1)S(1)}, bf16[24,768]{1,0:T(8,128)(2,1)S(1)}, u32[]{:S(2)}, u32[]{:S(2)}) collective-permute-start(bf16[24,768]{1,0:T(8,128)(2,1)S(1)} %get-tuple-element.35), channel_id=1, source_target_pairs={{0,64},{32,96},{64,0},{96,32},{1,65},{33,97},{65,1},{97,33},{2,66}... | collective-permute-start | bytes 110600 | tf_op jit(solution)/shard_map/ppermute | solution.py:271
  120.3 4.0 %collective-permute-start.18 = (bf16[24,768]{1,0:T(8,128)(2,1)S(1)}, bf16[24,768]{1,0:T(8,128)(2,1)S(1)}, u32[]{:S(2)}, u32[]{:S(2)}) collective-permute-start(bf16[24,768]{1,0:T(8,128)(2,1)S(1)} %get-tuple-element.34), channel_id=1, source_target_pairs={{0,96},{32,0},{64,32},{96,64},{1,97},{33,1},{65,33},{97,65},{2,98}... | collective-permute-start | bytes 110600 | tf_op jit(solution)/shard_map/ppermute | solution.py:271

commit v3 on v2

--- a/solution.py
+++ b/solution.py
@@ -103,14 +103,30 @@
     gain[...] = 1.0 + 0.5 * (row[...].astype(F32) + features)
 
 
+def normalise(x, gain):
+    mean = jnp.mean(x * x, axis=-1, keepdims=True)
+    return (x * lax.rsqrt(mean + EPS) * gain).astype(BF16)
+
+
+def own_kernel(own, gain, qkv, out_w, query, key, value):
+    width = own.shape[2]
+    ones = block_ones()
+    tokens = normalise(own[...].astype(F32).reshape(OWN, width), gain[...])
+    for at in range(0, width, 256):
+        here = slice(at, at + 256)
+        query[:, here] = unit_quad(dot(tokens, qkv[:, here]), ones)
+        part = dot(tokens, qkv[:, width + at : width + at + 256])
+        key[:, here] = unit_quad(part, ones).astype(BF16)
+        value[:, here] = dot(tokens, qkv[:, 2 * width + at : 2 * width + at + 256]).astype(BF16)
+
+
 def fine_kernel(
     start, windows, scales, own, left, right, up, down, gain, key_place, query_place,
-    qkv, out_w, stream, tokens,
+    own_query, own_key, own_value, qkv, out_w, stream, tokens,
 ):
     width = own.shape[2]
-    tokens[KEYS - 8 :] = jnp.zeros((8, width), F32)
-    tokens[:OWN] = own[...].astype(F32).reshape(OWN, width)
-    at = OWN
+    tokens[KEYS - OWN - 8 :] = jnp.zeros((8, width), F32)
+    at = 0
     for strip in (left, right):
         tokens[at : at + REACH * ROWS] = strip[...].astype(F32).reshape(REACH * ROWS, width)
         at += REACH * ROWS
@@ -118,10 +134,7 @@
         for c in range(strip.shape[0]):
             tokens[at : at + REACH] = strip[c].astype(F32)
             at += REACH
-    x = tokens[...]
-    mean = jnp.mean(x * x, axis=-1, keepdims=True)
-    n_all = (x * lax.rsqrt(mean + EPS) * gain[...]).astype(BF16)
-    n_own = n_all[:OWN]
+    halo = normalise(tokens[...], gain[...])
     row_k, col_k = key_place[0:1, :], key_place[1:2, :]
     row_q, col_q = query_place[:, 0:1], query_place[:, 1:2]
     row_g, col_g = row_k + start[0], col_k + start[1]
@@ -131,12 +144,14 @@
 
     ones = block_ones()
     lane = lax.broadcasted_iota(jnp.int32, (OWN, 256), 1) // HEAD_DIM
-    update = x[:OWN]
+    update = own[...].astype(F32).reshape(OWN, width)
     for quad in range(width // 256):
         at = quad * 256
-        query = unit_quad(dot(n_own, qkv[:, at : at + 256]), ones)
-        key = unit_quad(dot(n_all, qkv[:, width + at : width + at + 256]), ones).astype(BF16)
-        value = dot(n_all, qkv[:, 2 * width + at : 2 * width + at + 256]).astype(BF16)
+        query = own_query[:, at : at + 256]
+        key = unit_quad(dot(halo, qkv[:, width + at : width + at + 256]), ones).astype(BF16)
+        key = jnp.concatenate([own_key[:, at : at + 256], key], axis=0)
+        value = dot(halo, qkv[:, 2 * width + at : 2 * width + at + 256]).astype(BF16)
+        value = jnp.concatenate([own_value[:, at : at + 256], value], axis=0)
         hi, lo = split_hi_lo(query)
         rows = [jnp.where(lane == h, hi, 0) for h in range(4)]
         rows += [jnp.where(lane == h, lo, 0) for h in range(4)]
@@ -322,8 +337,6 @@
     left = shift(own[width - REACH :], GX, 8, 1)
     right = shift(own[:REACH], GX, 8, -1)
     wide = jnp.concatenate([left, own, right], axis=0)
-    up = shift(wide[:, height - REACH :], GY, 16, 1)
-    down = shift(wide[:, :REACH], GY, 16, -1)
     row = lax.dynamic_slice_in_dim(class_table, label[0], 1, 0)
     half = depth // 2
     freqs = np.exp(np.float32(-math.log(10000.0)) * np.arange(half, dtype=np.float32) / half)
@@ -333,6 +346,22 @@
         [timestep, row, jnp.asarray(freqs[None], F32)],
         (0,),
     )
+    own_heads = call(
+        own_kernel,
+        (
+            jax.ShapeDtypeStruct((OWN, depth), F32),
+            jax.ShapeDtypeStruct((OWN, depth), BF16),
+            jax.ShapeDtypeStruct((OWN, depth), BF16),
+        ),
+        [own, gain, fine_qkv, fine_out],
+        (),
+        flops=2 * OWN * depth * 3 * depth,
+        nbytes=5 * 2**20,
+    )
+    chunks = spread(split_weight.T)
+    wide = after(wide, chunks, *own_heads)
+    up = shift(wide[:, height - REACH :], GY, 16, 1)
+    down = shift(wide[:, :REACH], GY, 16, -1)
     start = jnp.stack(
         [
             lax.axis_index(GY) * height,
@@ -349,15 +378,15 @@
         jax.ShapeDtypeStruct((4, TOKENS, depth), BF16),
         [
             start, windows, fine_scale, own, left, right, up, down, gain,
-            jnp.asarray(PLACES.T.copy()), jnp.asarray(PLACES[:OWN].copy()), fine_qkv, fine_out,
+            jnp.asarray(PLACES.T.copy()), jnp.asarray(PLACES[:OWN].copy()), *own_heads, fine_qkv, fine_out,
         ],
         (0, 1, 2),
-        [pltpu.VMEM((KEYS, depth), F32)],
+        [pltpu.VMEM((KEYS - OWN, depth), F32)],
         flops=2 * KEYS * depth * 3 * depth,
         nbytes=5 * 2**20,
     )
     streams = gather_z(stream)
-    split_w = lax.all_to_all(after(spread(split_weight.T), merge_w, up, down), REST, 0, 0)
+    split_w = lax.all_to_all(after(chunks, merge_w, up, down), REST, 0, 0)
     merge_w = after(merge_w, stream)
     block = merge_w.shape[2]
     bottom = call(

time: 126 us -> 123 us (0.976)
  starting transfers between devices: 50.1 us -> 45.9 us
  local copies, waits for them, and re-layouts: 10.1 us -> 8.61 us
  blocking collectives: 23.2 us -> 24.6 us
    ppermute x4, waiting for transfers between devices: 12.3 us -> 4.89 us  [shift(): lax.ppermute(x, axis, [(i, i + step) for i in range(size) if 0 <= i + ste...]
    ppermute x9, waiting for transfers between devices: 6.03 us -> 12.3 us  [gather_z(): lax.ppermute(x, 'z', [(i, (i + s) % NX) for i in range(NX)])]
    ppermute x9, starting transfers between devices: 15.6 us -> 12.1 us  [gather_z(): lax.ppermute(x, 'z', [(i, (i + s) % NX) for i in range(NX)])]
    ppermute x4, starting transfers between devices: 7.36 us -> 10.2 us  [shift(): lax.ppermute(x, axis, [(i, i + step) for i in range(size) if 0 <= i + ste...]
    ppermute x3, starting transfers between devices: 4.47 us -> 2.63 us  [scatter_z(): lax.ppermute(parts[s], 'z', [(i, (i + s) % NX) for i in range(NX)])]
    ppermute x3, waiting for transfers between devices: 3.22 us -> 4.76 us  [scatter_z(): lax.ppermute(parts[s], 'z', [(i, (i + s) % NX) for i in range(NX)])]
    unnamed x26, local copies, waits for them, and re-layouts: 3.56 us -> 2.06 us
    ppermute x3, starting transfers between devices: 3.65 us -> 2.18 us  [swap_core(): return lax.ppermute(x, 'c', [(0, 1), (1, 0)])]
  transfers between devices with their start and end apart: 21 -> 21, of which waited for: 12 -> 13; matrix products, arithmetic and copies ran while one was open for 6% -> 6% of each run, Pallas kernels for 8% -> 9%
where the time goes in v3:
time: 123 us; the launch traced here: 122 us
  starting transfers between devices  45.9 us (37%)
  blocking collectives  24.6 us (20%)
  waiting for transfers between devices  22.6 us (18%)
  Pallas kernels  16.3 us (13%)
  local copies, waits for them, and re-layouts  8.61 us (7%)
  other arithmetic  2.66 us (2%)
  between operations  1.64 us (1%)
    all_to_all x1, blocking collectives, shards(): near = lax.all_to_all(pairs, REST, 0, 0).reshape(16 * OWN, 2 * group)  24.6 us
    pallas_call x9, Pallas kernels, call(): pl.pallas_call(body, out_shape=out_shape, in_specs=[smem() if i in in_sme...  16.3 us
    ppermute x9, waiting for transfers between devices, gather_z(): lax.ppermute(x, 'z', [(i, (i + s) % NX) for i in range(NX)])  12.3 us
    ppermute x9, starting transfers between devices, gather_z(): lax.ppermute(x, 'z', [(i, (i + s) % NX) for i in range(NX)])  12.1 us
    all_to_all x1, starting transfers between devices, merge_columns(): return lax.all_to_all(parts, ('z', *REST), 0, 0)  11.7 us
    ppermute x4, starting transfers between devices, shift(): lax.ppermute(x, axis, [(i, i + step) for i in range(size) if 0 <= i + ste...  10.2 us
    all_to_all x1, starting transfers between devices, shards(): split_w = lax.all_to_all(after(chunks, merge_w, up, down), REST, 0, 0)  7.08 us
    ppermute x4, waiting for transfers between devices, shift(): lax.ppermute(x, axis, [(i, i + step) for i in range(size) if 0 <= i + ste...  4.89 us
  transfers between devices with their start and end apart: 21, of which 13 were waited for; matrix products, arithmetic and copies ran while one was open for 6% of the time, Pallas kernels for 9%

profile of v3, /device:TPU:0, one launch (start us, length us, event | category | flops | bytes accessed | tf_op | source)
XLA Modules:
  0.0 122.2 jit_solution(12576422992114266875)
XLA Ops:
  0.0 0.9 slice_bitcast_fusion.3
  0.9 0.0 copy-start.7
  0.9 0.0 copy-start.2
  1.0 1.1 broadcast_in_dim.9
  2.1 11.7 %all-to-all-start = ((bf16[64,24,384]{2,1,0:T(8,128)(2,1)}), bf16[64,24,384]{2,1,0:T(8,128)(2,1)}, u32[]{:S(2)}, u32[]{:S(2)}) async-start(bf16[64,24,384]{2,1,0:T(8,128)(2,1)} %bitcast.39), calls=%async_computation | async-start | bytes 2359296 | tf_op jit(solution)/shard_map/all_to_all | solution.py:303
  13.8 1.3 %collective-permute-start.1 = (bf16[3,8,768]{2,1,0:T(8,128)(2,1)S(1)}, bf16[3,8,768]{2,1,0:T(8,128)(2,1)S(1)}, u32[]{:S(2)}, u32[]{:S(2)}) collective-permute-start(bf16[3,8,768]{2,1,0:T(8,128)(2,1)S(1)} %get-tuple-element.46), channel_id=1, source_target_pairs={{1,0},{2,1},{3,2},{4,3},{5,4},{6,5},{7,6},{9,8},{10,9},{11,10},{12... | collective-permute-start | bytes 110600 | tf_op jit(solution)/shard_map/ppermute | solution.py:273
  15.1 4.5 %collective-permute-start = (bf16[3,8,768]{2,1,0:T(8,128)(2,1)S(1)}, bf16[3,8,768]{2,1,0:T(8,128)(2,1)S(1)}, u32[]{:S(2)}, u32[]{:S(2)}) collective-permute-start(bf16[3,8,768]{2,1,0:T(8,128)(2,1)S(1)} %get-tuple-element.47), channel_id=1, source_target_pairs={{0,1},{1,2},{2,3},{3,4},{4,5},{5,6},{6,7},{8,9},{9,10},{10,11},{11... | collective-permute-start | bytes 110600 | tf_op jit(solution)/shard_map/ppermute | solution.py:273
  21.1 0.1 shard_map.163.gain
  21.1 0.0 copy-start.1
  21.1 2.0 %copy-done.1 = bf16[768,2304]{1,0:T(8,128)(2,1)S(1)} copy-done((bf16[768,2304]{1,0:T(8,128)(2,1)S(1)}, bf16[768,2304]{1,0:T(8,128)(2,1)}, u32[]{:S(2)}) %copy-start.1) | copy-done | bytes 3538968
  23.1 1.3 %shard_map.164 = (f32[96,768]{1,0:T(8,128)S(1)}, bf16[96,768]{1,0:T(8,128)(2,1)S(1)}, bf16[96,768]{1,0:T(8,128)(2,1)S(1)}) custom-call(bf16[12,8,768]{2,1,0:T(8,128)(2,1)S(1)} %bitcast.34, f32[1,768]{1,0:T(1,128)S(1)} %shard_map.163.gain, bf16[768,2304]{1,0:T(8,128)(2,1)S(1)} %copy-done.1, bf16[768,768]{1,0:T(8,128)(2,1)S(1)} %copy-done.2), custom_call_target="tpu_custom_call" | custom-call | flops 339738624 | bytes 5242880 | tf_op jit(solution)/shard_map/pallas_call | solution.py:89
  24.5 0.0 copy-start.5
  24.5 0.0 copy-start.6
  24.5 0.0 copy-start.8
  24.5 0.0 copy-start.9
  24.5 4.0 %collective-permute-done.1.right = bf16[3,8,768]{2,1,0:T(8,128)(2,1)S(1)} collective-permute-done((bf16[3,8,768]{2,1,0:T(8,128)(2,1)S(1)}, bf16[3,8,768]{2,1,0:T(8,128)(2,1)S(1)}, u32[]{:S(2)}, u32[]{:S(2)}) %collective-permute-start.1) | collective-permute-done | bytes 36896 | tf_op jit(solution)/shard_map/ppermute | solution.py:273
  28.6 1.1 broadcast_in_dim.8
  29.7 0.1 fusion
  29.8 1.3 %collective-permute-start.3 = (bf16[18,3,768]{2,1,0:T(4,128)(2,1)S(1)}, bf16[18,3,768]{2,1,0:T(4,128)(2,1)S(1)}, u32[]{:S(2)}, u32[]{:S(2)}) collective-permute-start(bf16[18,3,768]{2,1,0:T(4,128)(2,1)S(1)} %get-tuple-element.40), channel_id=1, source_target_pairs={{8,0},{16,8},{24,16},{32,24},{40,32},{48,40},{56,48},{64,56},{72,6... | collective-permute-start | bytes 248840 | tf_op jit(solution)/shard_map/ppermute | solution.py:273
  31.1 3.0 %collective-permute-start.2 = (bf16[18,3,768]{2,1,0:T(4,128)(2,1)S(1)}, bf16[18,3,768]{2,1,0:T(4,128)(2,1)S(1)}, u32[]{:S(2)}, u32[]{:S(2)}) collective-permute-start(bf16[18,3,768]{2,1,0:T(4,128)(2,1)S(1)} %get-tuple-element.41), channel_id=1, source_target_pairs={{0,8},{8,16},{16,24},{24,32},{32,40},{40,48},{48,56},{56,64},{64,7... | collective-permute-start | bytes 248840 | tf_op jit(solution)/shard_map/ppermute | solution.py:273
  34.1 0.1 pad_add_fusion.1.start
  34.2 0.9 collective-permute-done.2.up
  35.1 4.0 %shard_map.165.p0.stream = bf16[4,24,768]{2,1,0:T(8,128)(2,1)S(1)} custom-call(s32[4]{0:T(128)S(1)} %pad_add_fusion.1.start, s32[12]{0:T(128)S(1)} %copy-done.8, f32[12]{0:T(128)S(1)} %copy-done.9, bf16[12,8,768]{2,1,0:T(8,128)(2,1)S(1)} %bitcast.36, bf16[3,8,768]{2,1,0:T(8,128)(2,1)S(1)} %collective-permute-done.left, ...), custom_call_target="tpu_custom_call" | custom-call | flops 905969664 | bytes 5242880 | tf_op jit(solution)/shard_map/pallas_call | solution.py:89
  39.1 2.0 %collective-permute-start.7 = (bf16[64,24,384]{2,1,0:T(8,128)(2,1)}, bf16[64,24,384]{2,1,0:T(8,128)(2,1)S(1)}, u32[]{:S(2)}, u32[]{:S(2)}) collective-permute-start(bf16[64,24,384]{2,1,0:T(8,128)(2,1)} %all-to-all-done.mine), channel_id=1, source_target_pairs={{0,8},{8,0},{1,9},{9,1},{2,10},{10,2},{3,11},{11,3},{4,12},{12,4},... | collective-permute-start | bytes 3538952 | tf_op jit(solution)/shard_map/ppermute | solution.py:291
  41.1 7.1 %all-to-all-start.1 = ((bf16[16,24,1536]{2,1,0:T(8,128)(2,1)}), bf16[16,24,1536]{2,1,0:T(8,128)(2,1)}, u32[]{:S(2)}, u32[]{:S(2)}) async-start(bf16[16,24,1536]{2,1,0:T(8,128)(2,1)} %broadcast_in_dim.8), calls=%async_computation.1 | async-start | bytes 2359296 | tf_op jit(solution)/shard_map/all_to_all | solution.py:389
  48.1 4.2 %collective-permute-start.6 = (bf16[4,24,768]{2,1,0:T(8,128)(2,1)S(1)}, bf16[4,24,768]{2,1,0:T(8,128)(2,1)S(1)}, u32[]{:S(2)}, u32[]{:S(2)}) collective-permute-start(bf16[4,24,768]{2,1,0:T(8,128)(2,1)S(1)} %shard_map.165.p0.stream), channel_id=1, source_target_pairs={{0,96},{32,0},{64,32},{96,64},{1,97},{33,1},{65,33},{97,65},{2,98}... | collective-permute-start | bytes 442376 | tf_op jit(solution)/shard_map/ppermute | solution.py:278
  52.3 0.6 collective-permute-start.5
  53.0 1.0 collective-permute-start.4
  53.9 0.1 pad.5.clone
  54.0 0.1 pad_add_fusion.place
  54.1 4.9 %collective-permute-done.6.p3 = bf16[4,24,768]{2,1,0:T(8,128)(2,1)S(1)} collective-permute-done((bf16[4,24,768]{2,1,0:T(8,128)(2,1)S(1)}, bf16[4,24,768]{2,1,0:T(8,128)(2,1)S(1)}, u32[]{:S(2)}, u32[]{:S(2)}) %collective-permute-start.6) | collective-permute-done | bytes 147488 | tf_op jit(solution)/shard_map/ppermute | solution.py:278
  59.0 1.6 %collective-permute-done.5.p2 = bf16[4,24,768]{2,1,0:T(8,128)(2,1)S(1)} collective-permute-done((bf16[4,24,768]{2,1,0:T(8,128)(2,1)S(1)}, bf16[4,24,768]{2,1,0:T(8,128)(2,1)S(1)}, u32[]{:S(2)}, u32[]{:S(2)}) %collective-permute-start.5) | collective-permute-done | bytes 147488 | tf_op jit(solution)/shard_map/ppermute | solution.py:278
  60.6 2.1 %collective-permute-done.4.p1 = bf16[4,24,768]{2,1,0:T(8,128)(2,1)S(1)} collective-permute-done((bf16[4,24,768]{2,1,0:T(8,128)(2,1)S(1)}, bf16[4,24,768]{2,1,0:T(8,128)(2,1)S(1)}, u32[]{:S(2)}, u32[]{:S(2)}) %collective-permute-start.4) | collective-permute-done | bytes 147488 | tf_op jit(solution)/shard_map/ppermute | solution.py:278
  62.7 2.0 %shard_map.166.p0 = bf16[4,24,384]{2,1,0:T(8,128)(2,1)S(1)} custom-call(s32[2]{0:T(128)S(1)} %pad_add_fusion.place, bf16[4,24,768]{2,1,0:T(8,128)(2,1)S(1)} %shard_map.165.p0.stream, bf16[4,24,768]{2,1,0:T(8,128)(2,1)S(1)} %collective-permute-done.4.p1, bf16[4,24,768]{2,1,0:T(8,128)(2,1)S(1)} %collective-permute-done.5.p2, ...), custom_call_target="tpu_custom_call" | custom-call | flops 226492416 | bytes 3145728 | tf_op jit(solution)/shard_map/pallas_call | solution.py:89
  64.7 0.7 collective-permute-start.10
  65.4 0.6 collective-permute-start.9
  66.0 0.9 collective-permute-start.8
  66.9 3.2 %constant_dynamic-slice_fusion.2 = (bf16[1536,192]{1,0:T(8,128)(2,1)S(1)}, bf16[1536,192]{1,0:T(8,128)(2,1)S(1)}, bf16[1536,192]{1,0:T(8,128)(2,1)S(1)}) fusion(bf16[1536,2304]{1,0:T(8,128)(2,1)} %param.27, s32[]{:T(128)S(6)} %select_n.57, s32[]{:T(128)S(6)} %select_n.59, s32[]{:T(128)S(6)} %select_n.58), kind=kLoop, calls=%fused_computation.16 | loop fusion | bytes 3538956 | tf_op jit(solution)/shard_map/dynamic_slice | solution.py:407
  70.1 0.8 maximum_maximum_fusion.weight
  70.9 0.0 copy-start.10
  70.9 0.6 collective-permute-done.9.p2
  71.5 0.8 collective-permute-done.8.p1
  72.3 1.4 %shard_map.167 = (bf16[96,1536]{1,0:T(8,128)(2,1)S(1)}, f32[96,256]{1,0:T(8,128)S(1)}, bf16[16,96,384]{2,1,0:T(8,128)(2,1)S(1)}) custom-call(s32[2]{0:T(128)S(1)} %pad_add_fusion.place, bf16[4,24,384]{2,1,0:T(8,128)(2,1)S(1)} %shard_map.166.p0, bf16[4,24,384]{2,1,0:T(8,128)(2,1)S(1)} %collective-permute-done.8.p1, ...), custom_call_target="tpu_custom_call" | custom-call | flops 188743680 | bytes 4194304 | tf_op jit(solution)/shard_map/pallas_call | solution.py:89
  73.6 24.6 %all_to_all.15 = bf16[16,96,384]{2,1,0:T(8,128)(2,1)S(1)} all-to-all(bf16[16,96,384]{2,1,0:T(8,128)(2,1)S(1)} %get-tuple-element.29), channel_id=1, replica_groups=mesh['z'=4,'yl'=2,'c'=2,'yh'=2,'x'=4] {'yl','yh','x'}, dimensions={0} | all-to-all | bytes 2359296 | tf_op jit(solution)/shard_map/all_to_all | solution.py:424
  98.2 2.2 %shard_map.168 = (f32[288,1]{1,0:T(8,128)S(1)}, f32[288,1]{1,0:T(8,128)S(1)}, f32[288,256]{1,0:T(8,128)S(1)}) custom-call(f32[12]{0:T(128)S(1)} %copy-done.10, s32[2]{0:T(128)S(1)} %pad_add_fusion.place, f32[96,256]{1,0:T(8,128)S(1)} %get-tuple-element.26.query, bf16[1536,384]{1,0:T(8,128)(2,1)S(1)} %bitcast.38), custom_call_target="tpu_custom_call" | custom-call | flops 679477248 | bytes 2097152 | tf_op jit(solution)/shard_map/pallas_call | solution.py:89
  100.4 0.6 collective-permute-done.11.far
  101.0 2.2 %shard_map.169.p0 = bf16[96,192]{1,0:T(8,128)(2,1)S(1)} custom-call(f32[12]{0:T(128)S(1)} %copy-done.10, s32[2]{0:T(128)S(1)} %pad_add_fusion.place, f32[96,256]{1,0:T(8,128)S(1)} %get-tuple-element.26.query, bf16[1536,384]{1,0:T(8,128)(2,1)S(1)} %collective-permute-done.11.far, f32[288,1]{1,0:T(8,128)S(1)} %get-tuple-element.30.near_highest, ...), custom_call_target="tpu_custom_call" | custom-call | flops 679477248 | bytes 2097152 | tf_op jit(solution)/shard_map/pallas_call | solution.py:89
  103.3 0.2 collective-permute-start.15
  103.5 1.5 %collective-permute-start.14 = (bf16[96,192]{1,0:T(8,128)(2,1)S(1)}, bf16[96,192]{1,0:T(8,128)(2,1)S(1)}, u32[]{:S(2)}, u32[]{:S(2)}) collective-permute-start(bf16[96,192]{1,0:T(8,128)(2,1)S(1)} %shard_map.169.p0), channel_id=1, source_target_pairs={{0,96},{32,0},{64,32},{96,64},{1,97},{33,1},{65,33},{97,65},{2,98}... | collective-permute-start | bytes 110600 | tf_op jit(solution)/shard_map/ppermute | solution.py:278
  105.0 1.4 %collective-permute-start.13 = (bf16[96,192]{1,0:T(8,128)(2,1)S(1)}, bf16[96,192]{1,0:T(8,128)(2,1)S(1)}, u32[]{:S(2)}, u32[]{:S(2)}) collective-permute-start(bf16[96,192]{1,0:T(8,128)(2,1)S(1)} %shard_map.169.p0), channel_id=1, source_target_pairs={{0,64},{32,96},{64,0},{96,32},{1,65},{33,97},{65,1},{97,33},{2,66}... | collective-permute-start | bytes 110600 | tf_op jit(solution)/shard_map/ppermute | solution.py:278
  106.3 1.3 %collective-permute-start.12 = (bf16[96,192]{1,0:T(8,128)(2,1)S(1)}, bf16[96,192]{1,0:T(8,128)(2,1)S(1)}, u32[]{:S(2)}, u32[]{:S(2)}) collective-permute-start(bf16[96,192]{1,0:T(8,128)(2,1)S(1)} %shard_map.169.p0), channel_id=1, source_target_pairs={{0,32},{32,64},{64,96},{96,0},{1,33},{33,65},{65,97},{97,1},{2,34}... | collective-permute-start | bytes 110600 | tf_op jit(solution)/shard_map/ppermute | solution.py:278
  107.7 1.4 %broadcast_select_fusion.1 = (bf16[16,24,1536]{2,1,0:T(8,128)(2,1)S(1)}, bf16[16,24,1536]{2,1,0:T(8,128)(2,1)S(1)}) fusion(bf16[16,24,1536]{2,1,0:T(8,128)(2,1)} %all-to-all-done.1, bf16[16,24,1536]{2,1,0:T(8,128)(2,1)S(1)} %collective-permute-done.15, pred[]{:T(512)S(6)} %eq.9), kind=kLoop, calls=%fused_computation.3 | loop fusion | flops 1179648 | bytes 4718593 | tf_op jit(solution)/shard_map/jit(_where)/select_n | solution.py:314
  109.1 0.0 copy-start.3
  109.1 0.2 pad_maximum_fusion
  109.4 1.8 %collective-permute-done.13.p2 = bf16[96,192]{1,0:T(8,128)(2,1)S(1)} collective-permute-done((bf16[96,192]{1,0:T(8,128)(2,1)S(1)}, bf16[96,192]{1,0:T(8,128)(2,1)S(1)}, u32[]{:S(2)}, u32[]{:S(2)}) %collective-permute-start.13) | collective-permute-done | bytes 36896 | tf_op jit(solution)/shard_map/ppermute | solution.py:278
  111.2 0.5 collective-permute-done.12.p1
  111.7 1.7 %shard_map.170 = bf16[4,24,768]{2,1,0:T(8,128)(2,1)S(1)} custom-call(s32[2]{0:T(128)S(1)} %pad_add_fusion.place, bf16[96,192]{1,0:T(8,128)(2,1)S(1)} %shard_map.169.p0, bf16[96,192]{1,0:T(8,128)(2,1)S(1)} %collective-permute-done.12.p1, bf16[96,192]{1,0:T(8,128)(2,1)S(1)} %collective-permute-done.13.p2, bf16[96,192]{1,0:T(8,128)(2,1)S(1)} %collective-permute-done.14.p3, ...), custom_call_target="tpu_custom_call" | custom-call | flops 452984832 | bytes 5242880 | tf_op jit(solution)/shard_map/pallas_call | solution.py:89
  113.4 1.1 collective-permute-start.18
  114.5 1.2 collective-permute-start.17
  115.6 0.4 collective-permute-start.16
  116.0 1.4 %collective-permute-done.18.u3 = bf16[24,768]{1,0:T(8,128)(2,1)S(1)} collective-permute-done((bf16[24,768]{1,0:T(8,128)(2,1)S(1)}, bf16[24,768]{1,0:T(8,128)(2,1)S(1)}, u32[]{:S(2)}, u32[]{:S(2)}) %collective-permute-start.18) | collective-permute-done | bytes 36896 | tf_op jit(solution)/shard_map/ppermute | solution.py:286
  117.4 2.6 %collective-permute-done.17.u2 = bf16[24,768]{1,0:T(8,128)(2,1)S(1)} collective-permute-done((bf16[24,768]{1,0:T(8,128)(2,1)S(1)}, bf16[24,768]{1,0:T(8,128)(2,1)S(1)}, u32[]{:S(2)}, u32[]{:S(2)}) %collective-permute-start.17) | collective-permute-done | bytes 36896 | tf_op jit(solution)/shard_map/ppermute | solution.py:286
  120.0 0.8 collective-permute-done.16.u1
  120.8 1.4 %shard_map.171 = bf16[12,8,768]{2,1,0:T(8,128)(2,1)} custom-call(s32[2]{0:T(128)S(1)} %pad_add_fusion.place, bf16[4,24,768]{2,1,0:T(8,128)(2,1)S(1)} %shard_map.165.p0.stream, bf16[24,768]{1,0:T(8,128)(2,1)S(1)} %get-tuple-element.45.u0, bf16[24,768]{1,0:T(8,128)(2,1)S(1)} %collective-permute-done.16.u1, bf16[24,768]{1,0:T(8,128)(2,1)S(1)} %collective-permute-done.17.u2, ...), custom_call_target="tpu_custom_call" | custom-call | flops 18874368 | bytes 1048576 | tf_op jit(solution)/shard_map/pallas_call | solution.py:89
  (32 shorter events, 0.2 us)
Async XLA Ops:
  0.0 20.4 %copy-start = (bf16[1000,768]{1,0:T(8,128)(2,1)S(1)}, bf16[1000,768]{1,0:T(8,128)(2,1)}, u32[]{:S(2)}) copy-start(bf16[1000,768]{1,0:T(8,128)(2,1)} %param.18) | copy-start | bytes 4608004
  0.0 13.8 %copy-start.4 = (bf16[8,12,768]{2,0,1:T(8,128)(2,1)S(1)}, bf16[8,12,768]{2,0,1:T(8,128)(2,1)}, u32[]{:S(2)}) copy-start(bf16[8,12,768]{2,0,1:T(8,128)(2,1)} %param.17) | copy-start | bytes 442372
  0.9 20.1 %copy-start.7 = (f32[1,384]{1,0:T(1,128)S(1)}, f32[1,384]{1,0:T(1,128)}, u32[]{:S(2)}) copy-start(f32[1,384]{1,0:T(1,128)} %constant.91.clone.freqs) | copy-start | bytes 4612
  0.9 20.2 %copy-start.2 = (bf16[768,768]{1,0:T(8,128)(2,1)S(1)}, bf16[768,768]{1,0:T(8,128)(2,1)}, u32[]{:S(2)}) copy-start(bf16[768,768]{1,0:T(8,128)(2,1)} %out_w.4) | copy-start | bytes 3538948
  2.1 37.0 %all-to-all-start = ((bf16[64,24,384]{2,1,0:T(8,128)(2,1)}), bf16[64,24,384]{2,1,0:T(8,128)(2,1)}, u32[]{:S(2)}, u32[]{:S(2)}) async-start(bf16[64,24,384]{2,1,0:T(8,128)(2,1)} %bitcast.39), calls=%async_computation | async-start | bytes 2359296 | tf_op jit(solution)/shard_map/all_to_all | solution.py:303
  13.8 14.7 %collective-permute-start.1 = (bf16[3,8,768]{2,1,0:T(8,128)(2,1)S(1)}, bf16[3,8,768]{2,1,0:T(8,128)(2,1)S(1)}, u32[]{:S(2)}, u32[]{:S(2)}) collective-permute-start(bf16[3,8,768]{2,1,0:T(8,128)(2,1)S(1)} %get-tuple-element.46), channel_id=1, source_target_pairs={{1,0},{2,1},{3,2},{4,3},{5,4},{6,5},{7,6},{9,8},{10,9},{11,10},{12... | collective-permute-start | bytes 110600 | tf_op jit(solution)/shard_map/ppermute | solution.py:273
  15.1 13.4 %collective-permute-start = (bf16[3,8,768]{2,1,0:T(8,128)(2,1)S(1)}, bf16[3,8,768]{2,1,0:T(8,128)(2,1)S(1)}, u32[]{:S(2)}, u32[]{:S(2)}) collective-permute-start(bf16[3,8,768]{2,1,0:T(8,128)(2,1)S(1)} %get-tuple-element.47), channel_id=1, source_target_pairs={{0,1},{1,2},{2,3},{3,4},{4,5},{5,6},{6,7},{8,9},{9,10},{10,11},{11... | collective-permute-start | bytes 110600 | tf_op jit(solution)/shard_map/ppermute | solution.py:273
  21.1 2.0 %copy-start.1 = (bf16[768,2304]{1,0:T(8,128)(2,1)S(1)}, bf16[768,2304]{1,0:T(8,128)(2,1)}, u32[]{:S(2)}) copy-start(bf16[768,2304]{1,0:T(8,128)(2,1)} %qkv.3) | copy-start | bytes 10616836
  23.1 5.5 %copy-start.11 = (bf16[1536,24]{0,1:T(8,128)(2,1)S(1)}, bf16[1536,24]{0,1:T(8,128)(2,1)}, u32[]{:S(2)}) copy-start(bf16[1536,24]{0,1:T(8,128)(2,1)} %param.29) | copy-start | bytes 221188
  24.5 10.6 %copy-start.5 = (s32[96,2]{1,0:T(8,128)S(1)}, s32[96,2]{1,0:T(8,128)}, u32[]{:S(2)}) copy-start(s32[96,2]{1,0:T(8,128)} %constant.93.clone.query_place) | copy-start | bytes 2308
  24.5 10.6 %copy-start.6 = (s32[2,256]{1,0:T(2,128)S(1)}, s32[2,256]{1,0:T(2,128)}, u32[]{:S(2)}) copy-start(s32[2,256]{1,0:T(2,128)} %constant.92.clone.key_place) | copy-start | bytes 6148
  24.5 10.6 %copy-start.8 = (s32[12]{0:T(128)S(1)}, s32[12]{0:T(128)}, u32[]{:S(2)}) copy-start(s32[12]{0:T(128)} %windows.1) | copy-start | bytes 148
  24.5 10.6 %copy-start.9 = (f32[12]{0:T(128)S(1)}, f32[12]{0:T(128)}, u32[]{:S(2)}) copy-start(f32[12]{0:T(128)} %scales.3) | copy-start | bytes 148
  29.8 4.4 %collective-permute-start.3 = (bf16[18,3,768]{2,1,0:T(4,128)(2,1)S(1)}, bf16[18,3,768]{2,1,0:T(4,128)(2,1)S(1)}, u32[]{:S(2)}, u32[]{:S(2)}) collective-permute-start(bf16[18,3,768]{2,1,0:T(4,128)(2,1)S(1)} %get-tuple-element.40), channel_id=1, source_target_pairs={{8,0},{16,8},{24,16},{32,24},{40,32},{48,40},{56,48},{64,56},{72,6... | collective-permute-start | bytes 248840 | tf_op jit(solution)/shard_map/ppermute | solution.py:273
  31.1 4.0 %collective-permute-start.2 = (bf16[18,3,768]{2,1,0:T(4,128)(2,1)S(1)}, bf16[18,3,768]{2,1,0:T(4,128)(2,1)S(1)}, u32[]{:S(2)}, u32[]{:S(2)}) collective-permute-start(bf16[18,3,768]{2,1,0:T(4,128)(2,1)S(1)} %get-tuple-element.41), channel_id=1, source_target_pairs={{0,8},{8,16},{16,24},{24,32},{32,40},{40,48},{48,56},{56,64},{64,7... | collective-permute-start | bytes 248840 | tf_op jit(solution)/shard_map/ppermute | solution.py:273
  39.1 23.6 %collective-permute-start.7 = (bf16[64,24,384]{2,1,0:T(8,128)(2,1)}, bf16[64,24,384]{2,1,0:T(8,128)(2,1)S(1)}, u32[]{:S(2)}, u32[]{:S(2)}) collective-permute-start(bf16[64,24,384]{2,1,0:T(8,128)(2,1)} %all-to-all-done.mine), channel_id=1, source_target_pairs={{0,8},{8,0},{1,9},{9,1},{2,10},{10,2},{3,11},{11,3},{4,12},{12,4},... | collective-permute-start | bytes 3538952 | tf_op jit(solution)/shard_map/ppermute | solution.py:291
  41.1 32.6 %all-to-all-start.1 = ((bf16[16,24,1536]{2,1,0:T(8,128)(2,1)}), bf16[16,24,1536]{2,1,0:T(8,128)(2,1)}, u32[]{:S(2)}, u32[]{:S(2)}) async-start(bf16[16,24,1536]{2,1,0:T(8,128)(2,1)} %broadcast_in_dim.8), calls=%async_computation.1 | async-start | bytes 2359296 | tf_op jit(solution)/shard_map/all_to_all | solution.py:389
  48.1 10.8 %collective-permute-start.6 = (bf16[4,24,768]{2,1,0:T(8,128)(2,1)S(1)}, bf16[4,24,768]{2,1,0:T(8,128)(2,1)S(1)}, u32[]{:S(2)}, u32[]{:S(2)}) collective-permute-start(bf16[4,24,768]{2,1,0:T(8,128)(2,1)S(1)} %shard_map.165.p0.stream), channel_id=1, source_target_pairs={{0,96},{32,0},{64,32},{96,64},{1,97},{33,1},{65,33},{97,65},{2,98}... | collective-permute-start | bytes 442376 | tf_op jit(solution)/shard_map/ppermute | solution.py:278
  52.3 8.3 %collective-permute-start.5 = (bf16[4,24,768]{2,1,0:T(8,128)(2,1)S(1)}, bf16[4,24,768]{2,1,0:T(8,128)(2,1)S(1)}, u32[]{:S(2)}, u32[]{:S(2)}) collective-permute-start(bf16[4,24,768]{2,1,0:T(8,128)(2,1)S(1)} %shard_map.165.p0.stream), channel_id=1, source_target_pairs={{0,64},{32,96},{64,0},{96,32},{1,65},{33,97},{65,1},{97,33},{2,66}... | collective-permute-start | bytes 442376 | tf_op jit(solution)/shard_map/ppermute | solution.py:278
  53.0 9.7 %collective-permute-start.4 = (bf16[4,24,768]{2,1,0:T(8,128)(2,1)S(1)}, bf16[4,24,768]{2,1,0:T(8,128)(2,1)S(1)}, u32[]{:S(2)}, u32[]{:S(2)}) collective-permute-start(bf16[4,24,768]{2,1,0:T(8,128)(2,1)S(1)} %shard_map.165.p0.stream), channel_id=1, source_target_pairs={{0,32},{32,64},{64,96},{96,0},{1,33},{33,65},{65,97},{97,1},{2,34}... | collective-permute-start | bytes 442376 | tf_op jit(solution)/shard_map/ppermute | solution.py:278
  64.7 6.2 %collective-permute-start.10 = (bf16[4,24,384]{2,1,0:T(8,128)(2,1)S(1)}, bf16[4,24,384]{2,1,0:T(8,128)(2,1)S(1)}, u32[]{:S(2)}, u32[]{:S(2)}) collective-permute-start(bf16[4,24,384]{2,1,0:T(8,128)(2,1)S(1)} %shard_map.166.p0), channel_id=1, source_target_pairs={{0,96},{32,0},{64,32},{96,64},{1,97},{33,1},{65,33},{97,65},{2,98}... | collective-permute-start | bytes 221192 | tf_op jit(solution)/shard_map/ppermute | solution.py:278
  65.4 6.1 %collective-permute-start.9 = (bf16[4,24,384]{2,1,0:T(8,128)(2,1)S(1)}, bf16[4,24,384]{2,1,0:T(8,128)(2,1)S(1)}, u32[]{:S(2)}, u32[]{:S(2)}) collective-permute-start(bf16[4,24,384]{2,1,0:T(8,128)(2,1)S(1)} %shard_map.166.p0), channel_id=1, source_target_pairs={{0,64},{32,96},{64,0},{96,32},{1,65},{33,97},{65,1},{97,33},{2,66}... | collective-permute-start | bytes 221192 | tf_op jit(solution)/shard_map/ppermute | solution.py:278
  66.0 6.3 %collective-permute-start.8 = (bf16[4,24,384]{2,1,0:T(8,128)(2,1)S(1)}, bf16[4,24,384]{2,1,0:T(8,128)(2,1)S(1)}, u32[]{:S(2)}, u32[]{:S(2)}) collective-permute-start(bf16[4,24,384]{2,1,0:T(8,128)(2,1)S(1)} %shard_map.166.p0), channel_id=1, source_target_pairs={{0,32},{32,64},{64,96},{96,0},{1,33},{33,65},{65,97},{97,1},{2,34}... | collective-permute-start | bytes 221192 | tf_op jit(solution)/shard_map/ppermute | solution.py:278
  70.9 27.3 %copy-start.10 = (f32[12]{0:T(128)S(1)}, f32[12]{0:T(128)}, u32[]{:S(2)}) copy-start(f32[12]{0:T(128)} %scales.5) | copy-start | bytes 148
  98.2 2.8 %collective-permute-start.11 = (bf16[1536,384]{1,0:T(8,128)(2,1)S(1)}, bf16[1536,384]{1,0:T(8,128)(2,1)S(1)}, u32[]{:S(2)}, u32[]{:S(2)}) collective-permute-start(bf16[1536,384]{1,0:T(8,128)(2,1)S(1)} %bitcast.37), channel_id=1, source_target_pairs={{0,8},{8,0},{1,9},{9,1},{2,10},{10,2},{3,11},{11,3},{4,12},{12,4},... | collective-permute-start | bytes 3538952 | tf_op jit(solution)/shard_map/ppermute | solution.py:291
  103.3 4.4 %collective-permute-start.15 = (bf16[16,24,1536]{2,1,0:T(8,128)(2,1)}, bf16[16,24,1536]{2,1,0:T(8,128)(2,1)S(1)}, u32[]{:S(2)}, u32[]{:S(2)}) collective-permute-start(bf16[16,24,1536]{2,1,0:T(8,128)(2,1)} %all-to-all-done.1), channel_id=1, source_target_pairs={{0,8},{8,0},{1,9},{9,1},{2,10},{10,2},{3,11},{11,3},{4,12},{12,4},... | collective-permute-start | bytes 3538952 | tf_op jit(solution)/shard_map/ppermute | solution.py:291
  103.5 5.9 %collective-permute-start.14 = (bf16[96,192]{1,0:T(8,128)(2,1)S(1)}, bf16[96,192]{1,0:T(8,128)(2,1)S(1)}, u32[]{:S(2)}, u32[]{:S(2)}) collective-permute-start(bf16[96,192]{1,0:T(8,128)(2,1)S(1)} %shard_map.169.p0), channel_id=1, source_target_pairs={{0,96},{32,0},{64,32},{96,64},{1,97},{33,1},{65,33},{97,65},{2,98}... | collective-permute-start | bytes 110600 | tf_op jit(solution)/shard_map/ppermute | solution.py:278
  105.0 6.2 %collective-permute-start.13 = (bf16[96,192]{1,0:T(8,128)(2,1)S(1)}, bf16[96,192]{1,0:T(8,128)(2,1)S(1)}, u32[]{:S(2)}, u32[]{:S(2)}) collective-permute-start(bf16[96,192]{1,0:T(8,128)(2,1)S(1)} %shard_map.169.p0), channel_id=1, source_target_pairs={{0,64},{32,96},{64,0},{96,32},{1,65},{33,97},{65,1},{97,33},{2,66}... | collective-permute-start | bytes 110600 | tf_op jit(solution)/shard_map/ppermute | solution.py:278
  106.3 5.3 %collective-permute-start.12 = (bf16[96,192]{1,0:T(8,128)(2,1)S(1)}, bf16[96,192]{1,0:T(8,128)(2,1)S(1)}, u32[]{:S(2)}, u32[]{:S(2)}) collective-permute-start(bf16[96,192]{1,0:T(8,128)(2,1)S(1)} %shard_map.169.p0), channel_id=1, source_target_pairs={{0,32},{32,64},{64,96},{96,0},{1,33},{33,65},{65,97},{97,1},{2,34}... | collective-permute-start | bytes 110600 | tf_op jit(solution)/shard_map/ppermute | solution.py:278
  109.1 2.6 %copy-start.3 = (bf16[768,1536]{1,0:T(8,128)(2,1)S(1)}, bf16[768,1536]{1,0:T(8,128)(2,1)}, u32[]{:S(2)}) copy-start(bf16[768,1536]{1,0:T(8,128)(2,1)} %out_w.5) | copy-start | bytes 7077892
  111.7 4.4 %copy-start.12 = (f32[768]{0:T(1024)S(1)}, f32[768]{0:T(1024)}, u32[]{:S(2)}) copy-start(f32[768]{0:T(1024)} %param.30) | copy-start | bytes 9220
  113.4 4.0 %collective-permute-start.18 = (bf16[24,768]{1,0:T(8,128)(2,1)S(1)}, bf16[24,768]{1,0:T(8,128)(2,1)S(1)}, u32[]{:S(2)}, u32[]{:S(2)}) collective-permute-start(bf16[24,768]{1,0:T(8,128)(2,1)S(1)} %get-tuple-element.42), channel_id=1, source_target_pairs={{0,96},{32,0},{64,32},{96,64},{1,97},{33,1},{65,33},{97,65},{2,98}... | collective-permute-start | bytes 110600 | tf_op jit(solution)/shard_map/ppermute | solution.py:286
  114.5 5.5 %collective-permute-start.17 = (bf16[24,768]{1,0:T(8,128)(2,1)S(1)}, bf16[24,768]{1,0:T(8,128)(2,1)S(1)}, u32[]{:S(2)}, u32[]{:S(2)}) collective-permute-start(bf16[24,768]{1,0:T(8,128)(2,1)S(1)} %get-tuple-element.43), channel_id=1, source_target_pairs={{0,64},{32,96},{64,0},{96,32},{1,65},{33,97},{65,1},{97,33},{2,66}... | collective-permute-start | bytes 110600 | tf_op jit(solution)/shard_map/ppermute | solution.py:286
  115.6 5.2 %collective-permute-start.16 = (bf16[24,768]{1,0:T(8,128)(2,1)S(1)}, bf16[24,768]{1,0:T(8,128)(2,1)S(1)}, u32[]{:S(2)}, u32[]{:S(2)}) collective-permute-start(bf16[24,768]{1,0:T(8,128)(2,1)S(1)} %get-tuple-element.44), channel_id=1, source_target_pairs={{0,32},{32,64},{64,96},{96,0},{1,33},{33,65},{65,97},{97,1},{2,34}... | collective-permute-start | bytes 110600 | tf_op jit(solution)/shard_map/ppermute | solution.py:286

commit v4 on v3

--- a/solution.py
+++ b/solution.py
@@ -248,6 +248,16 @@
     out[...] = att[:, 64:].astype(BF16)
 
 
+def arrange_kernel(place, mine, other, weight):
+    for ref, core in ((mine, place[1]), (other, 1 - place[1])):
+        for step in range(4):
+            yl = place[2] if step < 2 else 1 - place[2]
+            yh = place[3] if step % 2 == 0 else 1 - place[3]
+            for k in range(4):
+                x = lax.rem(place[4] + 4 - k, 4)
+                weight[(yl * 2 + core) * 8 + yh * 4 + x] = ref[step, k]
+
+
 def output_kernel(place, p0, p1, p2, p3, bottom, out_w, split_w, split):
     acc = bottom[...].astype(F32)
     block = p0.shape[1]
@@ -303,17 +313,16 @@
     return lax.all_to_all(parts, ("z", *REST), 0, 0)
 
 
-def spread(chunk):
-    return jnp.broadcast_to(chunk[None], (16, *chunk.shape))
-
-
-def split_columns(mine):
-    rows, depth = mine.shape[1:]
-    other = swap_core(mine)
-    c = lax.axis_index("c")
-    first = jnp.where(c == 0, mine, other).reshape(2, 8, rows, depth)
-    second = jnp.where(c == 0, other, mine).reshape(2, 8, rows, depth)
-    return jnp.stack([first, second], axis=1).reshape(32 * rows, depth)
+def gather_x(x):
+    return jnp.stack(
+        [x] + [lax.ppermute(x, "x", [(i, (i + s) % 4) for i in range(4)]) for s in range(1, 4)]
+    )
+
+
+def gather_y(x):
+    return [x] + [
+        lax.ppermute(x, ("yl", "yh"), [(i, i ^ s) for i in range(4)]) for s in range(1, 4)
+    ]
 
 
 def shards(
@@ -358,8 +367,8 @@
         flops=2 * OWN * depth * 3 * depth,
         nbytes=5 * 2**20,
     )
-    chunks = spread(split_weight.T)
-    wide = after(wide, chunks, *own_heads)
+    chunk = split_weight.T
+    wide = after(wide, chunk, *own_heads)
     up = shift(wide[:, height - REACH :], GY, 16, 1)
     down = shift(wide[:, :REACH], GY, 16, -1)
     start = jnp.stack(
@@ -370,7 +379,8 @@
             jnp.int32(8 * width),
         ]
     ).astype(jnp.int32)
-    place = jnp.stack([lax.axis_index("z"), lax.axis_index("c")]).astype(jnp.int32)
+    place = jnp.stack([lax.axis_index(name) for name in ("z", "c", "yl", "yh", "x")])
+    place = place.astype(jnp.int32)
 
     merge_w = merge_columns(merge_weight)
     stream = call(
@@ -386,7 +396,7 @@
         nbytes=5 * 2**20,
     )
     streams = gather_z(stream)
-    split_w = lax.all_to_all(after(chunks, merge_w, up, down), REST, 0, 0)
+    split_w = gather_y(gather_x(after(chunk, up, down)))
     merge_w = after(merge_w, stream)
     block = merge_w.shape[2]
     bottom = call(
@@ -420,7 +430,7 @@
         flops=2 * OWN * deep * 640,
         nbytes=4 * 2**20,
     )
-    pairs = after(pairs, split_w)
+    pairs = after(pairs, *split_w)
     near = lax.all_to_all(pairs, REST, 0, 0).reshape(16 * OWN, 2 * group)
     far = swap_core(near)
     near_part = call(
@@ -443,7 +453,13 @@
         flops=2 * 3 * OWN * 1536 * 256 * 3,
         nbytes=2 * 2**20,
     )
-    split_w = split_columns(after(split_w, batt))
+    near_w = after(jnp.stack(split_w), near)
+    split_w = call(
+        arrange_kernel,
+        jax.ShapeDtypeStruct((32, TOKENS, deep), BF16),
+        [place, near_w, swap_core(near_w)],
+        (0,),
+    ).reshape(depth, deep)
     split = call(
         output_kernel,
         jax.ShapeDtypeStruct((NX, TOKENS, depth), BF16),

time: 123 us -> 121 us (0.984)
  starting transfers between devices: 45.9 us -> 52.7 us
  waiting for transfers between devices: 22.6 us -> 17.3 us
  blocking collectives: 24.6 us -> 22.1 us
  Pallas kernels: 16.3 us -> 17.9 us
  other arithmetic: 2.66 us -> 1.12 us
    ppermute x0 -> x6, starting transfers between devices: none -> 8.97 us  [the longest x3 4.88 us: gather_y(): lax.ppermute(x, ('yl', 'yh'), [(i, i ^ s) for i in range(4)])]
    ppermute x9, waiting for transfers between devices: 12.3 us -> 5.16 us  [gather_z(): lax.ppermute(x, 'z', [(i, (i + s) % NX) for i in range(NX)])]
    all_to_all x1 -> x0, starting transfers between devices: 7.08 us -> none  [shards(): split_w = lax.all_to_all(after(chunks, merge_w, up, down), REST, 0, 0)]
    ppermute x9, starting transfers between devices: 12.1 us -> 16.5 us  [gather_z(): lax.ppermute(x, 'z', [(i, (i + s) % NX) for i in range(NX)])]
    ppermute x4, waiting for transfers between devices: 4.89 us -> 8.74 us  [shift(): lax.ppermute(x, axis, [(i, i + step) for i in range(size) if 0 <= i + ste...]
    ppermute x4, starting transfers between devices: 10.2 us -> 7.29 us  [shift(): lax.ppermute(x, axis, [(i, i + step) for i in range(size) if 0 <= i + ste...]
    all_to_all x1, blocking collectives: 24.6 us -> 22.1 us  [shards(): near = lax.all_to_all(pairs, REST, 0, 0).reshape(16 * OWN, 2 * group)]
    ppermute x3, waiting for transfers between devices: 4.76 us -> 2.79 us  [scatter_z(): lax.ppermute(parts[s], 'z', [(i, (i + s) % NX) for i in range(NX)])]
  transfers between devices with their start and end apart: 21 -> 26, of which waited for: 13 -> 11; matrix products, arithmetic and copies ran while one was open for 6% -> 4% of each run, Pallas kernels for 9% -> 12%
where the time goes in v4:
time: 121 us; the launch traced here: 120 us
  starting transfers between devices  52.7 us (44%)
  blocking collectives  22.1 us (18%)
  Pallas kernels  17.9 us (15%)
  waiting for transfers between devices  17.3 us (14%)
  local copies, waits for them, and re-layouts  7.59 us (6%)
  between operations  1.64 us (1%)
    all_to_all x1, blocking collectives, shards(): near = lax.all_to_all(pairs, REST, 0, 0).reshape(16 * OWN, 2 * group)  22.1 us
    pallas_call x10, Pallas kernels, call(): pl.pallas_call(body, out_shape=out_shape, in_specs=[smem() if i in in_sme...  17.9 us
    ppermute x9, starting transfers between devices, gather_z(): lax.ppermute(x, 'z', [(i, (i + s) % NX) for i in range(NX)])  16.5 us
    all_to_all x1, starting transfers between devices, merge_columns(): return lax.all_to_all(parts, ('z', *REST), 0, 0)  11.7 us
    ppermute x4, waiting for transfers between devices, shift(): lax.ppermute(x, axis, [(i, i + step) for i in range(size) if 0 <= i + ste...  8.74 us
    ppermute x4, starting transfers between devices, shift(): lax.ppermute(x, axis, [(i, i + step) for i in range(size) if 0 <= i + ste...  7.29 us
    ppermute x9, waiting for transfers between devices, gather_z(): lax.ppermute(x, 'z', [(i, (i + s) % NX) for i in range(NX)])  5.16 us
    ppermute x3, starting transfers between devices, gather_y(): lax.ppermute(x, ('yl', 'yh'), [(i, i ^ s) for i in range(4)])  4.88 us
  transfers between devices with their start and end apart: 26, of which 11 were waited for; matrix products, arithmetic and copies ran while one was open for 4% of the time, Pallas kernels for 12%

profile of v4, /device:TPU:0, one launch (start us, length us, event | category | flops | bytes accessed | tf_op | source)
XLA Modules:
  0.0 120.4 jit_solution(13196965652269214859)
XLA Ops:
  0.0 0.9 slice_bitcast_fusion.3
  0.9 0.0 copy-start.7
  0.9 0.0 copy-start.2
  1.0 1.1 broadcast_in_dim.12
  2.1 11.7 %all-to-all-start = ((bf16[64,24,384]{2,1,0:T(8,128)(2,1)}), bf16[64,24,384]{2,1,0:T(8,128)(2,1)}, u32[]{:S(2)}, u32[]{:S(2)}) async-start(bf16[64,24,384]{2,1,0:T(8,128)(2,1)} %bitcast.49), calls=%async_computation | async-start | bytes 2359296 | tf_op jit(solution)/shard_map/all_to_all | solution.py:313
  13.9 3.4 %collective-permute-start = (bf16[3,8,768]{2,1,0:T(8,128)(2,1)S(1)}, bf16[3,8,768]{2,1,0:T(8,128)(2,1)S(1)}, u32[]{:S(2)}, u32[]{:S(2)}) collective-permute-start(bf16[3,8,768]{2,1,0:T(8,128)(2,1)S(1)} %get-tuple-element.47), channel_id=1, source_target_pairs={{0,1},{1,2},{2,3},{3,4},{4,5},{5,6},{6,7},{8,9},{9,10},{10,11},{11... | collective-permute-start | bytes 110600 | tf_op jit(solution)/shard_map/ppermute | solution.py:283
  17.3 1.3 %collective-permute-start.1 = (bf16[3,8,768]{2,1,0:T(8,128)(2,1)S(1)}, bf16[3,8,768]{2,1,0:T(8,128)(2,1)S(1)}, u32[]{:S(2)}, u32[]{:S(2)}) collective-permute-start(bf16[3,8,768]{2,1,0:T(8,128)(2,1)S(1)} %get-tuple-element.46), channel_id=1, source_target_pairs={{1,0},{2,1},{3,2},{4,3},{5,4},{6,5},{7,6},{9,8},{10,9},{11,10},{12... | collective-permute-start | bytes 110600 | tf_op jit(solution)/shard_map/ppermute | solution.py:283
  19.9 0.1 shard_map.163.gain
  20.0 0.0 copy-start.1
  20.0 2.0 %copy-done.1 = bf16[768,2304]{1,0:T(8,128)(2,1)S(1)} copy-done((bf16[768,2304]{1,0:T(8,128)(2,1)S(1)}, bf16[768,2304]{1,0:T(8,128)(2,1)}, u32[]{:S(2)}) %copy-start.1) | copy-done | bytes 3538968
  22.0 1.3 %shard_map.164 = (f32[96,768]{1,0:T(8,128)S(1)}, bf16[96,768]{1,0:T(8,128)(2,1)S(1)}, bf16[96,768]{1,0:T(8,128)(2,1)S(1)}) custom-call(bf16[12,8,768]{2,1,0:T(8,128)(2,1)S(1)} %bitcast.44, f32[1,768]{1,0:T(1,128)S(1)} %shard_map.163.gain, bf16[768,2304]{1,0:T(8,128)(2,1)S(1)} %copy-done.1, bf16[768,768]{1,0:T(8,128)(2,1)S(1)} %copy-done.2), custom_call_target="tpu_custom_call" | custom-call | flops 339738624 | bytes 5242880 | tf_op jit(solution)/shard_map/pallas_call | solution.py:89
  23.4 3.4 %collective-permute-done.left = bf16[3,8,768]{2,1,0:T(8,128)(2,1)S(1)} collective-permute-done((bf16[3,8,768]{2,1,0:T(8,128)(2,1)S(1)}, bf16[3,8,768]{2,1,0:T(8,128)(2,1)S(1)}, u32[]{:S(2)}, u32[]{:S(2)}) %collective-permute-start) | collective-permute-done | bytes 36896 | tf_op jit(solution)/shard_map/ppermute | solution.py:283
  26.7 1.9 %collective-permute-done.1.right = bf16[3,8,768]{2,1,0:T(8,128)(2,1)S(1)} collective-permute-done((bf16[3,8,768]{2,1,0:T(8,128)(2,1)S(1)}, bf16[3,8,768]{2,1,0:T(8,128)(2,1)S(1)}, u32[]{:S(2)}, u32[]{:S(2)}) %collective-permute-start.1) | collective-permute-done | bytes 36896 | tf_op jit(solution)/shard_map/ppermute | solution.py:283
  28.6 0.1 fusion.1
  28.7 1.3 %collective-permute-start.2 = (bf16[18,3,768]{2,1,0:T(4,128)(2,1)S(1)}, bf16[18,3,768]{2,1,0:T(4,128)(2,1)S(1)}, u32[]{:S(2)}, u32[]{:S(2)}) collective-permute-start(bf16[18,3,768]{2,1,0:T(4,128)(2,1)S(1)} %get-tuple-element.41), channel_id=1, source_target_pairs={{0,8},{8,16},{16,24},{24,32},{32,40},{40,48},{48,56},{56,64},{64,7... | collective-permute-start | bytes 248840 | tf_op jit(solution)/shard_map/ppermute | solution.py:283
  30.0 1.3 %collective-permute-start.3 = (bf16[18,3,768]{2,1,0:T(4,128)(2,1)S(1)}, bf16[18,3,768]{2,1,0:T(4,128)(2,1)S(1)}, u32[]{:S(2)}, u32[]{:S(2)}) collective-permute-start(bf16[18,3,768]{2,1,0:T(4,128)(2,1)S(1)} %get-tuple-element.40), channel_id=1, source_target_pairs={{8,0},{16,8},{24,16},{32,24},{40,32},{48,40},{56,48},{64,56},{72,6... | collective-permute-start | bytes 248840 | tf_op jit(solution)/shard_map/ppermute | solution.py:283
  31.3 0.1 pad_add_fusion.start
  31.4 3.5 %collective-permute-done.3.down = bf16[18,3,768]{2,1,0:T(4,128)(2,1)S(1)} collective-permute-done((bf16[18,3,768]{2,1,0:T(4,128)(2,1)S(1)}, bf16[18,3,768]{2,1,0:T(4,128)(2,1)S(1)}, u32[]{:S(2)}, u32[]{:S(2)}) %collective-permute-start.3) | collective-permute-done | bytes 82976 | tf_op jit(solution)/shard_map/ppermute | solution.py:283
  34.9 4.0 %shard_map.165.p0.stream = bf16[4,24,768]{2,1,0:T(8,128)(2,1)S(1)} custom-call(s32[4]{0:T(128)S(1)} %pad_add_fusion.start, s32[12]{0:T(128)S(1)} %copy-done.8, f32[12]{0:T(128)S(1)} %copy-done.9, bf16[12,8,768]{2,1,0:T(8,128)(2,1)S(1)} %bitcast.46, bf16[3,8,768]{2,1,0:T(8,128)(2,1)S(1)} %collective-permute-done.left, ...), custom_call_target="tpu_custom_call" | custom-call | flops 905969664 | bytes 5242880 | tf_op jit(solution)/shard_map/pallas_call | solution.py:89
  38.9 0.0 all-to-all-done.mine
  38.9 3.4 %collective-permute-start.7 = (bf16[64,24,384]{2,1,0:T(8,128)(2,1)}, bf16[64,24,384]{2,1,0:T(8,128)(2,1)S(1)}, u32[]{:S(2)}, u32[]{:S(2)}) collective-permute-start(bf16[64,24,384]{2,1,0:T(8,128)(2,1)} %all-to-all-done.mine), channel_id=1, source_target_pairs={{0,8},{8,0},{1,9},{9,1},{2,10},{10,2},{3,11},{11,3},{4,12},{12,4},... | collective-permute-start | bytes 3538952 | tf_op jit(solution)/shard_map/ppermute | solution.py:301
  42.4 3.0 %collective-permute-start.13 = (bf16[24,1536]{1,0:T(8,128)(2,1)S(1)}, bf16[24,1536]{1,0:T(8,128)(2,1)S(1)}, u32[]{:S(2)}, u32[]{:S(2)}) collective-permute-start(bf16[24,1536]{1,0:T(8,128)(2,1)S(1)} %bitcast.53), channel_id=1, source_target_pairs={{0,3},{1,0},{2,1},{3,2},{4,7},{5,4},{6,5},{7,6},{8,11},{9,8},{10,9... | collective-permute-start | bytes 221192 | tf_op jit(solution)/shard_map/ppermute | solution.py:318
  45.4 0.3 collective-permute-start.12
  45.7 0.8 collective-permute-start.11
  46.5 0.1 pad.11.clone
  46.5 0.1 stack.77.place
  46.6 1.5 %collective-permute-start.4 = (bf16[4,24,768]{2,1,0:T(8,128)(2,1)S(1)}, bf16[4,24,768]{2,1,0:T(8,128)(2,1)S(1)}, u32[]{:S(2)}, u32[]{:S(2)}) collective-permute-start(bf16[4,24,768]{2,1,0:T(8,128)(2,1)S(1)} %shard_map.165.p0.stream), channel_id=1, source_target_pairs={{0,32},{32,64},{64,96},{96,0},{1,33},{33,65},{65,97},{97,1},{2,34}... | collective-permute-start | bytes 442376 | tf_op jit(solution)/shard_map/ppermute | solution.py:288
  48.2 0.6 collective-permute-done.13
  48.8 3.6 %collective-permute-start.5 = (bf16[4,24,768]{2,1,0:T(8,128)(2,1)S(1)}, bf16[4,24,768]{2,1,0:T(8,128)(2,1)S(1)}, u32[]{:S(2)}, u32[]{:S(2)}) collective-permute-start(bf16[4,24,768]{2,1,0:T(8,128)(2,1)S(1)} %shard_map.165.p0.stream), channel_id=1, source_target_pairs={{0,64},{32,96},{64,0},{96,32},{1,65},{33,97},{65,1},{97,33},{2,66}... | collective-permute-start | bytes 442376 | tf_op jit(solution)/shard_map/ppermute | solution.py:288
  52.4 2.7 %collective-permute-start.6 = (bf16[4,24,768]{2,1,0:T(8,128)(2,1)S(1)}, bf16[4,24,768]{2,1,0:T(8,128)(2,1)S(1)}, u32[]{:S(2)}, u32[]{:S(2)}) collective-permute-start(bf16[4,24,768]{2,1,0:T(8,128)(2,1)S(1)} %shard_map.165.p0.stream), channel_id=1, source_target_pairs={{0,96},{32,0},{64,32},{96,64},{1,97},{33,1},{65,33},{97,65},{2,98}... | collective-permute-start | bytes 442376 | tf_op jit(solution)/shard_map/ppermute | solution.py:288
  55.1 0.0 collective-permute-done.11
  55.1 0.1 fusion
  55.1 1.4 %collective-permute-start.14 = (bf16[4,24,1536]{2,1,0:T(8,128)(2,1)S(1)}, bf16[4,24,1536]{2,1,0:T(8,128)(2,1)S(1)}, u32[]{:S(2)}, u32[]{:S(2)}) collective-permute-start(bf16[4,24,1536]{2,1,0:T(8,128)(2,1)S(1)} %get-tuple-element.39), channel_id=1, source_target_pairs={{0,4},{4,0},{16,20},{20,16},{1,5},{5,1},{17,21},{21,17},{2,6},{6,2... | collective-permute-start | bytes 884744 | tf_op jit(solution)/shard_map/ppermute | solution.py:324
  56.6 0.0 collective-permute-done.4.p1
  56.6 1.2 %collective-permute-start.15 = (bf16[4,24,1536]{2,1,0:T(8,128)(2,1)S(1)}, bf16[4,24,1536]{2,1,0:T(8,128)(2,1)S(1)}, u32[]{:S(2)}, u32[]{:S(2)}) collective-permute-start(bf16[4,24,1536]{2,1,0:T(8,128)(2,1)S(1)} %get-tuple-element.39), channel_id=1, source_target_pairs={{0,16},{4,20},{16,0},{20,4},{1,17},{5,21},{17,1},{21,5},{2,18},{6,... | collective-permute-start | bytes 884744 | tf_op jit(solution)/shard_map/ppermute | solution.py:324
  57.8 2.2 %collective-permute-start.16 = (bf16[4,24,1536]{2,1,0:T(8,128)(2,1)S(1)}, bf16[4,24,1536]{2,1,0:T(8,128)(2,1)S(1)}, u32[]{:S(2)}, u32[]{:S(2)}) collective-permute-start(bf16[4,24,1536]{2,1,0:T(8,128)(2,1)S(1)} %get-tuple-element.39), channel_id=1, source_target_pairs={{0,20},{4,16},{16,4},{20,0},{1,21},{5,17},{17,5},{21,1},{2,22},{6,... | collective-permute-start | bytes 884744 | tf_op jit(solution)/shard_map/ppermute | solution.py:324
  60.0 2.0 %shard_map.166.p0 = bf16[4,24,384]{2,1,0:T(8,128)(2,1)S(1)} custom-call(s32[5]{0:T(128)S(1)} %stack.77.place, bf16[4,24,768]{2,1,0:T(8,128)(2,1)S(1)} %shard_map.165.p0.stream, bf16[4,24,768]{2,1,0:T(8,128)(2,1)S(1)} %collective-permute-done.4.p1, bf16[4,24,768]{2,1,0:T(8,128)(2,1)S(1)} %collective-permute-done.5.p2, ...), custom_call_target="tpu_custom_call" | custom-call | flops 226492416 | bytes 3145728 | tf_op jit(solution)/shard_map/pallas_call | solution.py:89
  62.0 1.4 %collective-permute-start.8 = (bf16[4,24,384]{2,1,0:T(8,128)(2,1)S(1)}, bf16[4,24,384]{2,1,0:T(8,128)(2,1)S(1)}, u32[]{:S(2)}, u32[]{:S(2)}) collective-permute-start(bf16[4,24,384]{2,1,0:T(8,128)(2,1)S(1)} %shard_map.166.p0), channel_id=1, source_target_pairs={{0,32},{32,64},{64,96},{96,0},{1,33},{33,65},{65,97},{97,1},{2,34}... | collective-permute-start | bytes 221192 | tf_op jit(solution)/shard_map/ppermute | solution.py:288
  63.4 2.4 %collective-permute-start.9 = (bf16[4,24,384]{2,1,0:T(8,128)(2,1)S(1)}, bf16[4,24,384]{2,1,0:T(8,128)(2,1)S(1)}, u32[]{:S(2)}, u32[]{:S(2)}) collective-permute-start(bf16[4,24,384]{2,1,0:T(8,128)(2,1)S(1)} %shard_map.166.p0), channel_id=1, source_target_pairs={{0,64},{32,96},{64,0},{96,32},{1,65},{33,97},{65,1},{97,33},{2,66}... | collective-permute-start | bytes 221192 | tf_op jit(solution)/shard_map/ppermute | solution.py:288
  65.8 3.2 %constant_dynamic-slice_fusion.2 = (bf16[1536,192]{1,0:T(8,128)(2,1)S(1)}, bf16[1536,192]{1,0:T(8,128)(2,1)S(1)}, bf16[1536,192]{1,0:T(8,128)(2,1)S(1)}) fusion(bf16[1536,2304]{1,0:T(8,128)(2,1)} %param.27, s32[]{:T(128)S(6)} %select_n.45, s32[]{:T(128)S(6)} %select_n.47, s32[]{:T(128)S(6)} %select_n.46), kind=kLoop, calls=%fused_computation.15 | loop fusion | bytes 3538956 | tf_op jit(solution)/shard_map/dynamic_slice | solution.py:417
  69.0 1.1 collective-permute-start.10
  70.1 0.8 maximum_maximum_fusion.weight
  70.9 2.7 %collective-permute-done.10.p3 = bf16[4,24,384]{2,1,0:T(8,128)(2,1)S(1)} collective-permute-done((bf16[4,24,384]{2,1,0:T(8,128)(2,1)S(1)}, bf16[4,24,384]{2,1,0:T(8,128)(2,1)S(1)}, u32[]{:S(2)}, u32[]{:S(2)}) %collective-permute-start.10) | collective-permute-done | bytes 73760 | tf_op jit(solution)/shard_map/ppermute | solution.py:288
  73.6 1.4 %shard_map.167 = (bf16[96,1536]{1,0:T(8,128)(2,1)S(1)}, f32[96,256]{1,0:T(8,128)S(1)}, bf16[16,96,384]{2,1,0:T(8,128)(2,1)S(1)}) custom-call(s32[5]{0:T(128)S(1)} %stack.77.place, bf16[4,24,384]{2,1,0:T(8,128)(2,1)S(1)} %shard_map.166.p0, bf16[4,24,384]{2,1,0:T(8,128)(2,1)S(1)} %collective-permute-done.8.p1, ...), custom_call_target="tpu_custom_call" | custom-call | flops 188743680 | bytes 4194304 | tf_op jit(solution)/shard_map/pallas_call | solution.py:89
  75.0 0.0 copy-start.10
  75.0 22.1 %all_to_all.10 = bf16[16,96,384]{2,1,0:T(8,128)(2,1)S(1)} all-to-all(bf16[16,96,384]{2,1,0:T(8,128)(2,1)S(1)} %get-tuple-element.29), channel_id=1, replica_groups=mesh['z'=4,'yl'=2,'c'=2,'yh'=2,'x'=4] {'yl','yh','x'}, dimensions={0} | all-to-all | bytes 2359296 | tf_op jit(solution)/shard_map/all_to_all | solution.py:434
  97.1 0.1 pad_maximum_fusion.mine
  97.3 0.6 collective-permute-start.21
  97.9 2.2 %shard_map.168 = (f32[288,1]{1,0:T(8,128)S(1)}, f32[288,1]{1,0:T(8,128)S(1)}, f32[288,256]{1,0:T(8,128)S(1)}) custom-call(f32[12]{0:T(128)S(1)} %copy-done.10, s32[5]{0:T(128)S(1)} %stack.77.place, f32[96,256]{1,0:T(8,128)S(1)} %get-tuple-element.26.query, bf16[1536,384]{1,0:T(8,128)(2,1)S(1)} %bitcast.48), custom_call_target="tpu_custom_call" | custom-call | flops 679477248 | bytes 2097152 | tf_op jit(solution)/shard_map/pallas_call | solution.py:89
  100.1 2.2 %shard_map.169.p0 = bf16[96,192]{1,0:T(8,128)(2,1)S(1)} custom-call(f32[12]{0:T(128)S(1)} %copy-done.10, s32[5]{0:T(128)S(1)} %stack.77.place, f32[96,256]{1,0:T(8,128)S(1)} %get-tuple-element.26.query, bf16[1536,384]{1,0:T(8,128)(2,1)S(1)} %collective-permute-done.17.far, f32[288,1]{1,0:T(8,128)S(1)} %get-tuple-element.30.near_highest, ...), custom_call_target="tpu_custom_call" | custom-call | flops 679477248 | bytes 2097152 | tf_op jit(solution)/shard_map/pallas_call | solution.py:89
  102.3 0.2 collective-permute-start.18
  102.5 3.6 %collective-permute-start.19 = (bf16[96,192]{1,0:T(8,128)(2,1)S(1)}, bf16[96,192]{1,0:T(8,128)(2,1)S(1)}, u32[]{:S(2)}, u32[]{:S(2)}) collective-permute-start(bf16[96,192]{1,0:T(8,128)(2,1)S(1)} %shard_map.169.p0), channel_id=1, source_target_pairs={{0,64},{32,96},{64,0},{96,32},{1,65},{33,97},{65,1},{97,33},{2,66}... | collective-permute-start | bytes 110600 | tf_op jit(solution)/shard_map/ppermute | solution.py:288
  106.2 1.6 %shard_map.170 = bf16[32,24,1536]{2,1,0:T(8,128)(2,1)S(1)} custom-call(s32[5]{0:T(128)S(1)} %stack.77.place, bf16[4,4,24,1536]{3,2,1,0:T(8,128)(2,1)S(1)} %pad_maximum_fusion.mine, bf16[4,4,24,1536]{3,2,1,0:T(8,128)(2,1)} %collective-permute-done.21.other), custom_call_target="tpu_custom_call" | custom-call | tf_op jit(solution)/shard_map/pallas_call | solution.py:89
  107.8 0.4 collective-permute-done.18.p1
  108.2 0.6 collective-permute-done.19.p2
  108.8 1.4 %collective-permute-done.20.p3 = bf16[96,192]{1,0:T(8,128)(2,1)S(1)} collective-permute-done((bf16[96,192]{1,0:T(8,128)(2,1)S(1)}, bf16[96,192]{1,0:T(8,128)(2,1)S(1)}, u32[]{:S(2)}, u32[]{:S(2)}) %collective-permute-start.20) | collective-permute-done | bytes 36896 | tf_op jit(solution)/shard_map/ppermute | solution.py:288
  110.2 1.7 %shard_map.171 = bf16[4,24,768]{2,1,0:T(8,128)(2,1)S(1)} custom-call(s32[5]{0:T(128)S(1)} %stack.77.place, bf16[96,192]{1,0:T(8,128)(2,1)S(1)} %shard_map.169.p0, bf16[96,192]{1,0:T(8,128)(2,1)S(1)} %collective-permute-done.18.p1, bf16[96,192]{1,0:T(8,128)(2,1)S(1)} %collective-permute-done.19.p2, bf16[96,192]{1,0:T(8,128)(2,1)S(1)} %collective-permute-done.20.p3, ...), custom_call_target="tpu_custom_call" | custom-call | flops 452984832 | bytes 5242880 | tf_op jit(solution)/shard_map/pallas_call | solution.py:89
  111.9 0.4 collective-permute-start.22
  112.3 2.7 %collective-permute-start.23 = (bf16[24,768]{1,0:T(8,128)(2,1)S(1)}, bf16[24,768]{1,0:T(8,128)(2,1)S(1)}, u32[]{:S(2)}, u32[]{:S(2)}) collective-permute-start(bf16[24,768]{1,0:T(8,128)(2,1)S(1)} %get-tuple-element.43), channel_id=1, source_target_pairs={{0,64},{32,96},{64,0},{96,32},{1,65},{33,97},{65,1},{97,33},{2,66}... | collective-permute-start | bytes 110600 | tf_op jit(solution)/shard_map/ppermute | solution.py:296
  115.0 1.2 collective-permute-start.24
  116.2 1.0 collective-permute-done.22.u1
  117.2 0.6 collective-permute-done.23.u2
  117.8 1.2 collective-permute-done.24.u3
  119.0 1.4 %shard_map.172 = bf16[12,8,768]{2,1,0:T(8,128)(2,1)} custom-call(s32[5]{0:T(128)S(1)} %stack.77.place, bf16[4,24,768]{2,1,0:T(8,128)(2,1)S(1)} %shard_map.165.p0.stream, bf16[24,768]{1,0:T(8,128)(2,1)S(1)} %get-tuple-element.45.u0, bf16[24,768]{1,0:T(8,128)(2,1)S(1)} %collective-permute-done.22.u1, bf16[24,768]{1,0:T(8,128)(2,1)S(1)} %collective-permute-done.23.u2, ...), custom_call_target="tpu_custom_call" | custom-call | flops 18874368 | bytes 1048576 | tf_op jit(solution)/shard_map/pallas_call | solution.py:89
  (42 shorter events, 0.2 us)
Async XLA Ops:
  0.0 19.2 %copy-start = (bf16[1000,768]{1,0:T(8,128)(2,1)S(1)}, bf16[1000,768]{1,0:T(8,128)(2,1)}, u32[]{:S(2)}) copy-start(bf16[1000,768]{1,0:T(8,128)(2,1)} %param.18) | copy-start | bytes 4608004
  0.0 13.8 %copy-start.4 = (bf16[8,12,768]{2,0,1:T(8,128)(2,1)S(1)}, bf16[8,12,768]{2,0,1:T(8,128)(2,1)}, u32[]{:S(2)}) copy-start(bf16[8,12,768]{2,0,1:T(8,128)(2,1)} %param.17) | copy-start | bytes 442372
  0.9 19.0 %copy-start.7 = (f32[1,384]{1,0:T(1,128)S(1)}, f32[1,384]{1,0:T(1,128)}, u32[]{:S(2)}) copy-start(f32[1,384]{1,0:T(1,128)} %constant.91.clone.freqs) | copy-start | bytes 4612
  0.9 19.1 %copy-start.2 = (bf16[768,768]{1,0:T(8,128)(2,1)S(1)}, bf16[768,768]{1,0:T(8,128)(2,1)}, u32[]{:S(2)}) copy-start(bf16[768,768]{1,0:T(8,128)(2,1)} %out_w.4) | copy-start | bytes 3538948
  2.1 36.8 %all-to-all-start = ((bf16[64,24,384]{2,1,0:T(8,128)(2,1)}), bf16[64,24,384]{2,1,0:T(8,128)(2,1)}, u32[]{:S(2)}, u32[]{:S(2)}) async-start(bf16[64,24,384]{2,1,0:T(8,128)(2,1)} %bitcast.49), calls=%async_computation | async-start | bytes 2359296 | tf_op jit(solution)/shard_map/all_to_all | solution.py:313
  13.9 12.8 %collective-permute-start = (bf16[3,8,768]{2,1,0:T(8,128)(2,1)S(1)}, bf16[3,8,768]{2,1,0:T(8,128)(2,1)S(1)}, u32[]{:S(2)}, u32[]{:S(2)}) collective-permute-start(bf16[3,8,768]{2,1,0:T(8,128)(2,1)S(1)} %get-tuple-element.47), channel_id=1, source_target_pairs={{0,1},{1,2},{2,3},{3,4},{4,5},{5,6},{6,7},{8,9},{9,10},{10,11},{11... | collective-permute-start | bytes 110600 | tf_op jit(solution)/shard_map/ppermute | solution.py:283
  17.3 11.3 %collective-permute-start.1 = (bf16[3,8,768]{2,1,0:T(8,128)(2,1)S(1)}, bf16[3,8,768]{2,1,0:T(8,128)(2,1)S(1)}, u32[]{:S(2)}, u32[]{:S(2)}) collective-permute-start(bf16[3,8,768]{2,1,0:T(8,128)(2,1)S(1)} %get-tuple-element.46), channel_id=1, source_target_pairs={{1,0},{2,1},{3,2},{4,3},{5,4},{6,5},{7,6},{9,8},{10,9},{11,10},{12... | collective-permute-start | bytes 110600 | tf_op jit(solution)/shard_map/ppermute | solution.py:283
  20.0 2.0 %copy-start.1 = (bf16[768,2304]{1,0:T(8,128)(2,1)S(1)}, bf16[768,2304]{1,0:T(8,128)(2,1)}, u32[]{:S(2)}) copy-start(bf16[768,2304]{1,0:T(8,128)(2,1)} %qkv.3) | copy-start | bytes 10616836
  22.0 12.9 %copy-start.5 = (s32[96,2]{1,0:T(8,128)S(1)}, s32[96,2]{1,0:T(8,128)}, u32[]{:S(2)}) copy-start(s32[96,2]{1,0:T(8,128)} %constant.93.clone.query_place) | copy-start | bytes 2308
  22.0 12.9 %copy-start.6 = (s32[2,256]{1,0:T(2,128)S(1)}, s32[2,256]{1,0:T(2,128)}, u32[]{:S(2)}) copy-start(s32[2,256]{1,0:T(2,128)} %constant.92.clone.key_place) | copy-start | bytes 6148
  22.0 12.9 %copy-start.8 = (s32[12]{0:T(128)S(1)}, s32[12]{0:T(128)}, u32[]{:S(2)}) copy-start(s32[12]{0:T(128)} %windows.1) | copy-start | bytes 148
  22.0 12.9 %copy-start.9 = (f32[12]{0:T(128)S(1)}, f32[12]{0:T(128)}, u32[]{:S(2)}) copy-start(f32[12]{0:T(128)} %scales.3) | copy-start | bytes 148
  28.7 2.7 %collective-permute-start.2 = (bf16[18,3,768]{2,1,0:T(4,128)(2,1)S(1)}, bf16[18,3,768]{2,1,0:T(4,128)(2,1)S(1)}, u32[]{:S(2)}, u32[]{:S(2)}) collective-permute-start(bf16[18,3,768]{2,1,0:T(4,128)(2,1)S(1)} %get-tuple-element.41), channel_id=1, source_target_pairs={{0,8},{8,16},{16,24},{24,32},{32,40},{40,48},{48,56},{56,64},{64,7... | collective-permute-start | bytes 248840 | tf_op jit(solution)/shard_map/ppermute | solution.py:283
  30.0 4.9 %collective-permute-start.3 = (bf16[18,3,768]{2,1,0:T(4,128)(2,1)S(1)}, bf16[18,3,768]{2,1,0:T(4,128)(2,1)S(1)}, u32[]{:S(2)}, u32[]{:S(2)}) collective-permute-start(bf16[18,3,768]{2,1,0:T(4,128)(2,1)S(1)} %get-tuple-element.40), channel_id=1, source_target_pairs={{8,0},{16,8},{24,16},{32,24},{40,32},{48,40},{56,48},{64,56},{72,6... | collective-permute-start | bytes 248840 | tf_op jit(solution)/shard_map/ppermute | solution.py:283
  31.4 11.0 %copy-start.11 = (bf16[1536,24]{0,1:T(8,128)(2,1)S(1)}, bf16[1536,24]{0,1:T(8,128)(2,1)}, u32[]{:S(2)}) copy-start(bf16[1536,24]{0,1:T(8,128)(2,1)} %param.29) | copy-start | bytes 221188
  38.9 21.1 %collective-permute-start.7 = (bf16[64,24,384]{2,1,0:T(8,128)(2,1)}, bf16[64,24,384]{2,1,0:T(8,128)(2,1)S(1)}, u32[]{:S(2)}, u32[]{:S(2)}) collective-permute-start(bf16[64,24,384]{2,1,0:T(8,128)(2,1)} %all-to-all-done.mine), channel_id=1, source_target_pairs={{0,8},{8,0},{1,9},{9,1},{2,10},{10,2},{3,11},{11,3},{4,12},{12,4},... | collective-permute-start | bytes 3538952 | tf_op jit(solution)/shard_map/ppermute | solution.py:301
  42.4 6.4 %collective-permute-start.13 = (bf16[24,1536]{1,0:T(8,128)(2,1)S(1)}, bf16[24,1536]{1,0:T(8,128)(2,1)S(1)}, u32[]{:S(2)}, u32[]{:S(2)}) collective-permute-start(bf16[24,1536]{1,0:T(8,128)(2,1)S(1)} %bitcast.53), channel_id=1, source_target_pairs={{0,3},{1,0},{2,1},{3,2},{4,7},{5,4},{6,5},{7,6},{8,11},{9,8},{10,9... | collective-permute-start | bytes 221192 | tf_op jit(solution)/shard_map/ppermute | solution.py:318
  45.4 7.0 %collective-permute-start.12 = (bf16[24,1536]{1,0:T(8,128)(2,1)S(1)}, bf16[24,1536]{1,0:T(8,128)(2,1)S(1)}, u32[]{:S(2)}, u32[]{:S(2)}) collective-permute-start(bf16[24,1536]{1,0:T(8,128)(2,1)S(1)} %bitcast.54), channel_id=1, source_target_pairs={{0,2},{1,3},{2,0},{3,1},{4,6},{5,7},{6,4},{7,5},{8,10},{9,11},{10,... | collective-permute-start | bytes 221192 | tf_op jit(solution)/shard_map/ppermute | solution.py:318
  45.7 9.3 %collective-permute-start.11 = (bf16[24,1536]{1,0:T(8,128)(2,1)S(1)}, bf16[24,1536]{1,0:T(8,128)(2,1)S(1)}, u32[]{:S(2)}, u32[]{:S(2)}) collective-permute-start(bf16[24,1536]{1,0:T(8,128)(2,1)S(1)} %bitcast.55), channel_id=1, source_target_pairs={{0,1},{1,2},{2,3},{3,0},{4,5},{5,6},{6,7},{7,4},{8,9},{9,10},{10,1... | collective-permute-start | bytes 221192 | tf_op jit(solution)/shard_map/ppermute | solution.py:318
  46.6 9.9 %collective-permute-start.4 = (bf16[4,24,768]{2,1,0:T(8,128)(2,1)S(1)}, bf16[4,24,768]{2,1,0:T(8,128)(2,1)S(1)}, u32[]{:S(2)}, u32[]{:S(2)}) collective-permute-start(bf16[4,24,768]{2,1,0:T(8,128)(2,1)S(1)} %shard_map.165.p0.stream), channel_id=1, source_target_pairs={{0,32},{32,64},{64,96},{96,0},{1,33},{33,65},{65,97},{97,1},{2,34}... | collective-permute-start | bytes 442376 | tf_op jit(solution)/shard_map/ppermute | solution.py:288
  48.8 9.0 %collective-permute-start.5 = (bf16[4,24,768]{2,1,0:T(8,128)(2,1)S(1)}, bf16[4,24,768]{2,1,0:T(8,128)(2,1)S(1)}, u32[]{:S(2)}, u32[]{:S(2)}) collective-permute-start(bf16[4,24,768]{2,1,0:T(8,128)(2,1)S(1)} %shard_map.165.p0.stream), channel_id=1, source_target_pairs={{0,64},{32,96},{64,0},{96,32},{1,65},{33,97},{65,1},{97,33},{2,66}... | collective-permute-start | bytes 442376 | tf_op jit(solution)/shard_map/ppermute | solution.py:288
  52.4 7.6 %collective-permute-start.6 = (bf16[4,24,768]{2,1,0:T(8,128)(2,1)S(1)}, bf16[4,24,768]{2,1,0:T(8,128)(2,1)S(1)}, u32[]{:S(2)}, u32[]{:S(2)}) collective-permute-start(bf16[4,24,768]{2,1,0:T(8,128)(2,1)S(1)} %shard_map.165.p0.stream), channel_id=1, source_target_pairs={{0,96},{32,0},{64,32},{96,64},{1,97},{33,1},{65,33},{97,65},{2,98}... | collective-permute-start | bytes 442376 | tf_op jit(solution)/shard_map/ppermute | solution.py:288
  55.1 19.9 %collective-permute-start.14 = (bf16[4,24,1536]{2,1,0:T(8,128)(2,1)S(1)}, bf16[4,24,1536]{2,1,0:T(8,128)(2,1)S(1)}, u32[]{:S(2)}, u32[]{:S(2)}) collective-permute-start(bf16[4,24,1536]{2,1,0:T(8,128)(2,1)S(1)} %get-tuple-element.39), channel_id=1, source_target_pairs={{0,4},{4,0},{16,20},{20,16},{1,5},{5,1},{17,21},{21,17},{2,6},{6,2... | collective-permute-start | bytes 884744 | tf_op jit(solution)/shard_map/ppermute | solution.py:324
  56.6 18.4 %collective-permute-start.15 = (bf16[4,24,1536]{2,1,0:T(8,128)(2,1)S(1)}, bf16[4,24,1536]{2,1,0:T(8,128)(2,1)S(1)}, u32[]{:S(2)}, u32[]{:S(2)}) collective-permute-start(bf16[4,24,1536]{2,1,0:T(8,128)(2,1)S(1)} %get-tuple-element.39), channel_id=1, source_target_pairs={{0,16},{4,20},{16,0},{20,4},{1,17},{5,21},{17,1},{21,5},{2,18},{6,... | collective-permute-start | bytes 884744 | tf_op jit(solution)/shard_map/ppermute | solution.py:324
  57.8 17.2 %collective-permute-start.16 = (bf16[4,24,1536]{2,1,0:T(8,128)(2,1)S(1)}, bf16[4,24,1536]{2,1,0:T(8,128)(2,1)S(1)}, u32[]{:S(2)}, u32[]{:S(2)}) collective-permute-start(bf16[4,24,1536]{2,1,0:T(8,128)(2,1)S(1)} %get-tuple-element.39), channel_id=1, source_target_pairs={{0,20},{4,16},{16,4},{20,0},{1,21},{5,17},{17,5},{21,1},{2,22},{6,... | collective-permute-start | bytes 884744 | tf_op jit(solution)/shard_map/ppermute | solution.py:324
  62.0 7.0 %collective-permute-start.8 = (bf16[4,24,384]{2,1,0:T(8,128)(2,1)S(1)}, bf16[4,24,384]{2,1,0:T(8,128)(2,1)S(1)}, u32[]{:S(2)}, u32[]{:S(2)}) collective-permute-start(bf16[4,24,384]{2,1,0:T(8,128)(2,1)S(1)} %shard_map.166.p0), channel_id=1, source_target_pairs={{0,32},{32,64},{64,96},{96,0},{1,33},{33,65},{65,97},{97,1},{2,34}... | collective-permute-start | bytes 221192 | tf_op jit(solution)/shard_map/ppermute | solution.py:288
  63.4 7.5 %collective-permute-start.9 = (bf16[4,24,384]{2,1,0:T(8,128)(2,1)S(1)}, bf16[4,24,384]{2,1,0:T(8,128)(2,1)S(1)}, u32[]{:S(2)}, u32[]{:S(2)}) collective-permute-start(bf16[4,24,384]{2,1,0:T(8,128)(2,1)S(1)} %shard_map.166.p0), channel_id=1, source_target_pairs={{0,64},{32,96},{64,0},{96,32},{1,65},{33,97},{65,1},{97,33},{2,66}... | collective-permute-start | bytes 221192 | tf_op jit(solution)/shard_map/ppermute | solution.py:288
  69.0 4.6 %collective-permute-start.10 = (bf16[4,24,384]{2,1,0:T(8,128)(2,1)S(1)}, bf16[4,24,384]{2,1,0:T(8,128)(2,1)S(1)}, u32[]{:S(2)}, u32[]{:S(2)}) collective-permute-start(bf16[4,24,384]{2,1,0:T(8,128)(2,1)S(1)} %shard_map.166.p0), channel_id=1, source_target_pairs={{0,96},{32,0},{64,32},{96,64},{1,97},{33,1},{65,33},{97,65},{2,98}... | collective-permute-start | bytes 221192 | tf_op jit(solution)/shard_map/ppermute | solution.py:288
  75.0 22.9 %copy-start.10 = (f32[12]{0:T(128)S(1)}, f32[12]{0:T(128)}, u32[]{:S(2)}) copy-start(f32[12]{0:T(128)} %scales.5) | copy-start | bytes 148
  97.1 3.0 %collective-permute-start.17 = (bf16[1536,384]{1,0:T(8,128)(2,1)S(1)}, bf16[1536,384]{1,0:T(8,128)(2,1)S(1)}, u32[]{:S(2)}, u32[]{:S(2)}) collective-permute-start(bf16[1536,384]{1,0:T(8,128)(2,1)S(1)} %bitcast.47), channel_id=1, source_target_pairs={{0,8},{8,0},{1,9},{9,1},{2,10},{10,2},{3,11},{11,3},{4,12},{12,4},... | collective-permute-start | bytes 3538952 | tf_op jit(solution)/shard_map/ppermute | solution.py:301
  97.3 8.9 %collective-permute-start.21 = (bf16[4,4,24,1536]{3,2,1,0:T(8,128)(2,1)S(1)}, bf16[4,4,24,1536]{3,2,1,0:T(8,128)(2,1)}, u32[]{:S(2)}, u32[]{:S(2)}) collective-permute-start(bf16[4,4,24,1536]{3,2,1,0:T(8,128)(2,1)S(1)} %pad_maximum_fusion.mine), channel_id=1, source_target_pairs={{0,8},{8,0},{1,9},{9,1},{2,10},{10,2},{3,11},{11,3},{4,12},{12,4},... | collective-permute-start | bytes 3538952 | tf_op jit(solution)/shard_map/ppermute | solution.py:301
  102.3 5.9 %collective-permute-start.18 = (bf16[96,192]{1,0:T(8,128)(2,1)S(1)}, bf16[96,192]{1,0:T(8,128)(2,1)S(1)}, u32[]{:S(2)}, u32[]{:S(2)}) collective-permute-start(bf16[96,192]{1,0:T(8,128)(2,1)S(1)} %shard_map.169.p0), channel_id=1, source_target_pairs={{0,32},{32,64},{64,96},{96,0},{1,33},{33,65},{65,97},{97,1},{2,34}... | collective-permute-start | bytes 110600 | tf_op jit(solution)/shard_map/ppermute | solution.py:288
  102.5 6.3 %collective-permute-start.19 = (bf16[96,192]{1,0:T(8,128)(2,1)S(1)}, bf16[96,192]{1,0:T(8,128)(2,1)S(1)}, u32[]{:S(2)}, u32[]{:S(2)}) collective-permute-start(bf16[96,192]{1,0:T(8,128)(2,1)S(1)} %shard_map.169.p0), channel_id=1, source_target_pairs={{0,64},{32,96},{64,0},{96,32},{1,65},{33,97},{65,1},{97,33},{2,66}... | collective-permute-start | bytes 110600 | tf_op jit(solution)/shard_map/ppermute | solution.py:288
  106.1 4.1 %collective-permute-start.20 = (bf16[96,192]{1,0:T(8,128)(2,1)S(1)}, bf16[96,192]{1,0:T(8,128)(2,1)S(1)}, u32[]{:S(2)}, u32[]{:S(2)}) collective-permute-start(bf16[96,192]{1,0:T(8,128)(2,1)S(1)} %shard_map.169.p0), channel_id=1, source_target_pairs={{0,96},{32,0},{64,32},{96,64},{1,97},{33,1},{65,33},{97,65},{2,98}... | collective-permute-start | bytes 110600 | tf_op jit(solution)/shard_map/ppermute | solution.py:288
  106.1 4.1 %copy-start.3 = (bf16[768,1536]{1,0:T(8,128)(2,1)S(1)}, bf16[768,1536]{1,0:T(8,128)(2,1)}, u32[]{:S(2)}) copy-start(bf16[768,1536]{1,0:T(8,128)(2,1)} %out_w.5) | copy-start | bytes 7077892
  110.2 5.9 %copy-start.12 = (f32[768]{0:T(1024)S(1)}, f32[768]{0:T(1024)}, u32[]{:S(2)}) copy-start(f32[768]{0:T(1024)} %param.30) | copy-start | bytes 9220
  111.9 5.2 %collective-permute-start.22 = (bf16[24,768]{1,0:T(8,128)(2,1)S(1)}, bf16[24,768]{1,0:T(8,128)(2,1)S(1)}, u32[]{:S(2)}, u32[]{:S(2)}) collective-permute-start(bf16[24,768]{1,0:T(8,128)(2,1)S(1)} %get-tuple-element.44), channel_id=1, source_target_pairs={{0,32},{32,64},{64,96},{96,0},{1,33},{33,65},{65,97},{97,1},{2,34}... | collective-permute-start | bytes 110600 | tf_op jit(solution)/shard_map/ppermute | solution.py:296
  112.3 5.5 %collective-permute-start.23 = (bf16[24,768]{1,0:T(8,128)(2,1)S(1)}, bf16[24,768]{1,0:T(8,128)(2,1)S(1)}, u32[]{:S(2)}, u32[]{:S(2)}) collective-permute-start(bf16[24,768]{1,0:T(8,128)(2,1)S(1)} %get-tuple-element.43), channel_id=1, source_target_pairs={{0,64},{32,96},{64,0},{96,32},{1,65},{33,97},{65,1},{97,33},{2,66}... | collective-permute-start | bytes 110600 | tf_op jit(solution)/shard_map/ppermute | solution.py:296
  115.0 4.0 %collective-permute-start.24 = (bf16[24,768]{1,0:T(8,128)(2,1)S(1)}, bf16[24,768]{1,0:T(8,128)(2,1)S(1)}, u32[]{:S(2)}, u32[]{:S(2)}) collective-permute-start(bf16[24,768]{1,0:T(8,128)(2,1)S(1)} %get-tuple-element.42), channel_id=1, source_target_pairs={{0,96},{32,0},{64,32},{96,64},{1,97},{33,1},{65,33},{97,65},{2,98}... | collective-permute-start | bytes 110600 | tf_op jit(solution)/shard_map/ppermute | solution.py:296

commit v5 on v4

--- a/solution.py
+++ b/solution.py
@@ -430,7 +430,6 @@
         flops=2 * OWN * deep * 640,
         nbytes=4 * 2**20,
     )
-    pairs = after(pairs, *split_w)
     near = lax.all_to_all(pairs, REST, 0, 0).reshape(16 * OWN, 2 * group)
     far = swap_core(near)
     near_part = call(

time: 121 us -> 135 us (1.12)
  waiting for transfers between devices: 17.3 us -> 42.3 us
  blocking collectives: 22.1 us -> 0 us
  starting transfers between devices: 52.7 us -> 59.3 us
  other arithmetic: 1.12 us -> 3.07 us
  Pallas kernels: 17.9 us -> 19.6 us
    all_to_all x1 -> x0, blocking collectives: 22.1 us -> none  [shards(): near = lax.all_to_all(pairs, REST, 0, 0).reshape(16 * OWN, 2 * group)]
    ppermute x3, waiting for transfers between devices: 0.61 us -> 12.6 us  [gather_x(): lax.ppermute(x, 'x', [(i, (i + s) % 4) for i in range(4)])]
    ppermute x3, waiting for transfers between devices: 0.01 us -> 10.7 us  [gather_y(): lax.ppermute(x, ('yl', 'yh'), [(i, i ^ s) for i in range(4)])]
    all_to_all x0 -> x1, starting transfers between devices: none -> 7.2 us  [shards(): near = lax.all_to_all(pairs, REST, 0, 0).reshape(16 * OWN, 2 * group)]
    another operation x2, other arithmetic: 0.2 us -> 2.14 us  [shards(): near_w = after(jnp.stack(split_w), near)]
    pallas_call x10, Pallas kernels: 17.9 us -> 19.6 us  [call(): pl.pallas_call(body, out_shape=out_shape, in_specs=[smem() if i in in_sme...]
    ppermute x9, waiting for transfers between devices: 5.16 us -> 6.68 us  [gather_z(): lax.ppermute(x, 'z', [(i, (i + s) % NX) for i in range(NX)])]
    unnamed x26 -> x32, local copies, waits for them, and re-layouts: 2.05 us -> 2.76 us
  transfers between devices with their start and end apart: 26 -> 27, of which waited for: 11 -> 15; matrix products, arithmetic and copies ran while one was open for 4% -> 5% of each run, Pallas kernels for 12% -> 9%
where the time goes in v5:
time: 135 us; the launch traced here: 134 us
  starting transfers between devices  59.3 us (44%)
  waiting for transfers between devices  42.3 us (31%)
  Pallas kernels  19.6 us (15%)
  local copies, waits for them, and re-layouts  8.3 us (6%)
  other arithmetic  3.07 us (2%)
  between operations  1.66 us (1%)
    pallas_call x10, Pallas kernels, call(): pl.pallas_call(body, out_shape=out_shape, in_specs=[smem() if i in in_sme...  19.6 us
    ppermute x9, starting transfers between devices, gather_z(): lax.ppermute(x, 'z', [(i, (i + s) % NX) for i in range(NX)])  15.3 us
    ppermute x3, waiting for transfers between devices, gather_x(): lax.ppermute(x, 'x', [(i, (i + s) % 4) for i in range(4)])  12.6 us
    all_to_all x1, starting transfers between devices, merge_columns(): return lax.all_to_all(parts, ('z', *REST), 0, 0)  11.7 us
    ppermute x3, waiting for transfers between devices, gather_y(): lax.ppermute(x, ('yl', 'yh'), [(i, i ^ s) for i in range(4)])  10.7 us
    ppermute x4, waiting for transfers between devices, shift(): lax.ppermute(x, axis, [(i, i + step) for i in range(size) if 0 <= i + ste...  8.74 us
    ppermute x4, starting transfers between devices, shift(): lax.ppermute(x, axis, [(i, i + step) for i in range(size) if 0 <= i + ste...  7.29 us
    all_to_all x1, starting transfers between devices, shards(): near = lax.all_to_all(pairs, REST, 0, 0).reshape(16 * OWN, 2 * group)  7.2 us
  transfers between devices with their start and end apart: 27, of which 15 were waited for; matrix products, arithmetic and copies ran while one was open for 5% of the time, Pallas kernels for 9%

profile of v5, /device:TPU:0, one launch (start us, length us, event | category | flops | bytes accessed | tf_op | source)
XLA Modules:
  0.0 134.2 jit_solution(11941303458108286633)
XLA Ops:
  0.0 0.9 slice_bitcast_fusion.3
  0.9 0.0 copy-start.7
  1.0 1.1 broadcast_in_dim.12
  2.1 11.7 %all-to-all-start = ((bf16[64,24,384]{2,1,0:T(8,128)(2,1)}), bf16[64,24,384]{2,1,0:T(8,128)(2,1)}, u32[]{:S(2)}, u32[]{:S(2)}) async-start(bf16[64,24,384]{2,1,0:T(8,128)(2,1)} %bitcast.47), calls=%async_computation | async-start | bytes 2359296 | tf_op jit(solution)/shard_map/all_to_all | solution.py:313
  13.9 3.4 %collective-permute-start = (bf16[3,8,768]{2,1,0:T(8,128)(2,1)S(1)}, bf16[3,8,768]{2,1,0:T(8,128)(2,1)S(1)}, u32[]{:S(2)}, u32[]{:S(2)}) collective-permute-start(bf16[3,8,768]{2,1,0:T(8,128)(2,1)S(1)} %get-tuple-element.45), channel_id=1, source_target_pairs={{0,1},{1,2},{2,3},{3,4},{4,5},{5,6},{6,7},{8,9},{9,10},{10,11},{11... | collective-permute-start | bytes 110600 | tf_op jit(solution)/shard_map/ppermute | solution.py:283
  17.3 1.3 collective-permute-start.1
  19.9 0.1 shard_map.163.gain
  20.0 2.0 %copy-done.1 = bf16[768,2304]{1,0:T(8,128)(2,1)S(1)} copy-done((bf16[768,2304]{1,0:T(8,128)(2,1)S(1)}, bf16[768,2304]{1,0:T(8,128)(2,1)}, u32[]{:S(2)}) %copy-start.1) | copy-done | bytes 3538968
  22.0 1.3 shard_map.164
  23.4 3.4 %collective-permute-done.left = bf16[3,8,768]{2,1,0:T(8,128)(2,1)S(1)} collective-permute-done((bf16[3,8,768]{2,1,0:T(8,128)(2,1)S(1)}, bf16[3,8,768]{2,1,0:T(8,128)(2,1)S(1)}, u32[]{:S(2)}, u32[]{:S(2)}) %collective-permute-start) | collective-permute-done | bytes 36896 | tf_op jit(solution)/shard_map/ppermute | solution.py:283
  26.7 1.9 %collective-permute-done.1.right = bf16[3,8,768]{2,1,0:T(8,128)(2,1)S(1)} collective-permute-done((bf16[3,8,768]{2,1,0:T(8,128)(2,1)S(1)}, bf16[3,8,768]{2,1,0:T(8,128)(2,1)S(1)}, u32[]{:S(2)}, u32[]{:S(2)}) %collective-permute-start.1) | collective-permute-done | bytes 36896 | tf_op jit(solution)/shard_map/ppermute | solution.py:283
  28.6 0.1 fusion.1
  28.7 1.3 collective-permute-start.2
  30.0 1.3 collective-permute-start.3
  31.3 0.1 pad_add_fusion.start
  31.4 3.5 %collective-permute-done.3.down = bf16[18,3,768]{2,1,0:T(4,128)(2,1)S(1)} collective-permute-done((bf16[18,3,768]{2,1,0:T(4,128)(2,1)S(1)}, bf16[18,3,768]{2,1,0:T(4,128)(2,1)S(1)}, u32[]{:S(2)}, u32[]{:S(2)}) %collective-permute-start.3) | collective-permute-done | bytes 82976 | tf_op jit(solution)/shard_map/ppermute | solution.py:283
  34.9 4.0 %shard_map.165.p0.stream = bf16[4,24,768]{2,1,0:T(8,128)(2,1)S(1)} custom-call(s32[4]{0:T(128)S(1)} %pad_add_fusion.start, s32[12]{0:T(128)S(1)} %copy-done.8, f32[12]{0:T(128)S(1)} %copy-done.9, bf16[12,8,768]{2,1,0:T(8,128)(2,1)S(1)} %bitcast.46, bf16[3,8,768]{2,1,0:T(8,128)(2,1)S(1)} %collective-permute-done.left, ...), custom_call_target="tpu_custom_call" | custom-call | flops 905969664 | bytes 5242880 | tf_op jit(solution)/shard_map/pallas_call | solution.py:89
  38.9 3.4 %collective-permute-start.7 = (bf16[64,24,384]{2,1,0:T(8,128)(2,1)}, bf16[64,24,384]{2,1,0:T(8,128)(2,1)S(1)}, u32[]{:S(2)}, u32[]{:S(2)}) collective-permute-start(bf16[64,24,384]{2,1,0:T(8,128)(2,1)} %all-to-all-done.mine), channel_id=1, source_target_pairs={{0,8},{8,0},{1,9},{9,1},{2,10},{10,2},{3,11},{11,3},{4,12},{12,4},... | collective-permute-start | bytes 3538952 | tf_op jit(solution)/shard_map/ppermute | solution.py:301
  42.4 1.5 %collective-permute-start.4 = (bf16[4,24,768]{2,1,0:T(8,128)(2,1)S(1)}, bf16[4,24,768]{2,1,0:T(8,128)(2,1)S(1)}, u32[]{:S(2)}, u32[]{:S(2)}) collective-permute-start(bf16[4,24,768]{2,1,0:T(8,128)(2,1)S(1)} %shard_map.165.p0.stream), channel_id=1, source_target_pairs={{0,32},{32,64},{64,96},{96,0},{1,33},{33,65},{65,97},{97,1},{2,34}... | collective-permute-start | bytes 442376 | tf_op jit(solution)/shard_map/ppermute | solution.py:288
  43.9 2.9 %collective-permute-start.5 = (bf16[4,24,768]{2,1,0:T(8,128)(2,1)S(1)}, bf16[4,24,768]{2,1,0:T(8,128)(2,1)S(1)}, u32[]{:S(2)}, u32[]{:S(2)}) collective-permute-start(bf16[4,24,768]{2,1,0:T(8,128)(2,1)S(1)} %shard_map.165.p0.stream), channel_id=1, source_target_pairs={{0,64},{32,96},{64,0},{96,32},{1,65},{33,97},{65,1},{97,33},{2,66}... | collective-permute-start | bytes 442376 | tf_op jit(solution)/shard_map/ppermute | solution.py:288
  46.8 1.4 %collective-permute-start.6 = (bf16[4,24,768]{2,1,0:T(8,128)(2,1)S(1)}, bf16[4,24,768]{2,1,0:T(8,128)(2,1)S(1)}, u32[]{:S(2)}, u32[]{:S(2)}) collective-permute-start(bf16[4,24,768]{2,1,0:T(8,128)(2,1)S(1)} %shard_map.165.p0.stream), channel_id=1, source_target_pairs={{0,96},{32,0},{64,32},{96,64},{1,97},{33,1},{65,33},{97,65},{2,98}... | collective-permute-start | bytes 442376 | tf_op jit(solution)/shard_map/ppermute | solution.py:288
  48.1 0.1 pad.11.clone
  48.2 0.1 stack.77.place
  48.3 1.1 collective-permute-done.4.p1
  49.4 4.3 %collective-permute-done.5.p2 = bf16[4,24,768]{2,1,0:T(8,128)(2,1)S(1)} collective-permute-done((bf16[4,24,768]{2,1,0:T(8,128)(2,1)S(1)}, bf16[4,24,768]{2,1,0:T(8,128)(2,1)S(1)}, u32[]{:S(2)}, u32[]{:S(2)}) %collective-permute-start.5) | collective-permute-done | bytes 147488 | tf_op jit(solution)/shard_map/ppermute | solution.py:288
  53.7 2.0 %shard_map.166.p0 = bf16[4,24,384]{2,1,0:T(8,128)(2,1)S(1)} custom-call(s32[5]{0:T(128)S(1)} %stack.77.place, bf16[4,24,768]{2,1,0:T(8,128)(2,1)S(1)} %shard_map.165.p0.stream, bf16[4,24,768]{2,1,0:T(8,128)(2,1)S(1)} %collective-permute-done.4.p1, bf16[4,24,768]{2,1,0:T(8,128)(2,1)S(1)} %collective-permute-done.5.p2, ...), custom_call_target="tpu_custom_call" | custom-call | flops 226492416 | bytes 3145728 | tf_op jit(solution)/shard_map/pallas_call | solution.py:89
  55.8 1.3 collective-permute-start.8
  57.1 2.4 %collective-permute-start.9 = (bf16[4,24,384]{2,1,0:T(8,128)(2,1)S(1)}, bf16[4,24,384]{2,1,0:T(8,128)(2,1)S(1)}, u32[]{:S(2)}, u32[]{:S(2)}) collective-permute-start(bf16[4,24,384]{2,1,0:T(8,128)(2,1)S(1)} %shard_map.166.p0), channel_id=1, source_target_pairs={{0,64},{32,96},{64,0},{96,32},{1,65},{33,97},{65,1},{97,33},{2,66}... | collective-permute-start | bytes 221192 | tf_op jit(solution)/shard_map/ppermute | solution.py:288
  59.5 1.6 %collective-permute-start.10 = (bf16[4,24,384]{2,1,0:T(8,128)(2,1)S(1)}, bf16[4,24,384]{2,1,0:T(8,128)(2,1)S(1)}, u32[]{:S(2)}, u32[]{:S(2)}) collective-permute-start(bf16[4,24,384]{2,1,0:T(8,128)(2,1)S(1)} %shard_map.166.p0), channel_id=1, source_target_pairs={{0,96},{32,0},{64,32},{96,64},{1,97},{33,1},{65,33},{97,65},{2,98}... | collective-permute-start | bytes 221192 | tf_op jit(solution)/shard_map/ppermute | solution.py:288
  61.1 3.2 %constant_dynamic-slice_fusion.2 = (bf16[1536,192]{1,0:T(8,128)(2,1)S(1)}, bf16[1536,192]{1,0:T(8,128)(2,1)S(1)}, bf16[1536,192]{1,0:T(8,128)(2,1)S(1)}) fusion(bf16[1536,2304]{1,0:T(8,128)(2,1)} %param.27, s32[]{:T(128)S(6)} %select_n.45, s32[]{:T(128)S(6)} %select_n.47, s32[]{:T(128)S(6)} %select_n.46), kind=kLoop, calls=%fused_computation.15 | loop fusion | bytes 3538956 | tf_op jit(solution)/shard_map/dynamic_slice | solution.py:417
  64.3 0.8 maximum_maximum_fusion.weight
  65.1 2.3 %shard_map.167 = (bf16[96,1536]{1,0:T(8,128)(2,1)S(1)}, f32[96,256]{1,0:T(8,128)S(1)}, bf16[16,96,384]{2,1,0:T(8,128)(2,1)}) custom-call(s32[5]{0:T(128)S(1)} %stack.77.place, bf16[4,24,384]{2,1,0:T(8,128)(2,1)S(1)} %shard_map.166.p0, bf16[4,24,384]{2,1,0:T(8,128)(2,1)S(1)} %collective-permute-done.8.p1, bf16[4,24,384]{2,1,0:T(8,128)(2,1)S(1)} %collective-permute-done.9.p2, ...), custom_call_target="tpu_custom_call" | custom-call | flops 188743680 | bytes 4194304 | tf_op jit(solution)/shard_map/pallas_call | solution.py:89
  67.5 7.2 %all-to-all-start.1 = ((bf16[16,96,384]{2,1,0:T(8,128)(2,1)}), bf16[16,96,384]{2,1,0:T(8,128)(2,1)}, u32[]{:S(2)}, u32[]{:S(2)}) async-start(bf16[16,96,384]{2,1,0:T(8,128)(2,1)} %get-tuple-element.26), calls=%async_computation.1 | async-start | bytes 2359296 | tf_op jit(solution)/shard_map/all_to_all | solution.py:433
  74.7 3.2 %collective-permute-start.17 = (bf16[24,1536]{1,0:T(8,128)(2,1)S(1)}, bf16[24,1536]{1,0:T(8,128)(2,1)S(1)}, u32[]{:S(2)}, u32[]{:S(2)}) collective-permute-start(bf16[24,1536]{1,0:T(8,128)(2,1)S(1)} %bitcast.51), channel_id=1, source_target_pairs={{0,3},{1,0},{2,1},{3,2},{4,7},{5,4},{6,5},{7,6},{8,11},{9,8},{10,9... | collective-permute-start | bytes 221192 | tf_op jit(solution)/shard_map/ppermute | solution.py:318
  77.8 0.9 collective-permute-start.16
  78.7 0.9 collective-permute-start.15
  79.6 10.7 %collective-permute-done.17 = bf16[24,1536]{1,0:T(8,128)(2,1)S(1)} collective-permute-done((bf16[24,1536]{1,0:T(8,128)(2,1)S(1)}, bf16[24,1536]{1,0:T(8,128)(2,1)S(1)}, u32[]{:S(2)}, u32[]{:S(2)}) %collective-permute-start.17) | collective-permute-done | bytes 73760 | tf_op jit(solution)/shard_map/ppermute | solution.py:318
  90.2 1.6 %collective-permute-done.16 = bf16[24,1536]{1,0:T(8,128)(2,1)S(1)} collective-permute-done((bf16[24,1536]{1,0:T(8,128)(2,1)S(1)}, bf16[24,1536]{1,0:T(8,128)(2,1)S(1)}, u32[]{:S(2)}, u32[]{:S(2)}) %collective-permute-start.16) | collective-permute-done | bytes 73760 | tf_op jit(solution)/shard_map/ppermute | solution.py:318
  91.8 0.4 collective-permute-done.15
  92.2 0.8 fusion
  93.0 2.7 %collective-permute-start.20 = (bf16[4,24,1536]{2,1,0:T(8,128)(2,1)S(1)}, bf16[4,24,1536]{2,1,0:T(8,128)(2,1)S(1)}, u32[]{:S(2)}, u32[]{:S(2)}) collective-permute-start(bf16[4,24,1536]{2,1,0:T(8,128)(2,1)S(1)} %get-tuple-element.37), channel_id=1, source_target_pairs={{0,20},{4,16},{16,4},{20,0},{1,21},{5,17},{17,5},{21,1},{2,22},{6,... | collective-permute-start | bytes 884744 | tf_op jit(solution)/shard_map/ppermute | solution.py:324
  95.6 0.2 collective-permute-start.19
  95.9 1.8 %collective-permute-start.18 = (bf16[4,24,1536]{2,1,0:T(8,128)(2,1)S(1)}, bf16[4,24,1536]{2,1,0:T(8,128)(2,1)S(1)}, u32[]{:S(2)}, u32[]{:S(2)}) collective-permute-start(bf16[4,24,1536]{2,1,0:T(8,128)(2,1)S(1)} %get-tuple-element.37), channel_id=1, source_target_pairs={{0,4},{4,0},{16,20},{20,16},{1,5},{5,1},{17,21},{21,17},{2,6},{6,2... | collective-permute-start | bytes 884744 | tf_op jit(solution)/shard_map/ppermute | solution.py:324
  97.7 5.5 %collective-permute-done.20 = bf16[4,24,1536]{2,1,0:T(8,128)(2,1)S(1)} collective-permute-done((bf16[4,24,1536]{2,1,0:T(8,128)(2,1)S(1)}, bf16[4,24,1536]{2,1,0:T(8,128)(2,1)S(1)}, u32[]{:S(2)}, u32[]{:S(2)}) %collective-permute-start.20) | collective-permute-done | bytes 294944 | tf_op jit(solution)/shard_map/ppermute | solution.py:324
  103.2 2.0 %collective-permute-done.19 = bf16[4,24,1536]{2,1,0:T(8,128)(2,1)S(1)} collective-permute-done((bf16[4,24,1536]{2,1,0:T(8,128)(2,1)S(1)}, bf16[4,24,1536]{2,1,0:T(8,128)(2,1)S(1)}, u32[]{:S(2)}, u32[]{:S(2)}) %collective-permute-start.19) | collective-permute-done | bytes 294944 | tf_op jit(solution)/shard_map/ppermute | solution.py:324
  105.2 3.2 %collective-permute-done.18 = bf16[4,24,1536]{2,1,0:T(8,128)(2,1)S(1)} collective-permute-done((bf16[4,24,1536]{2,1,0:T(8,128)(2,1)S(1)}, bf16[4,24,1536]{2,1,0:T(8,128)(2,1)S(1)}, u32[]{:S(2)}, u32[]{:S(2)}) %collective-permute-start.18) | collective-permute-done | bytes 294944 | tf_op jit(solution)/shard_map/ppermute | solution.py:324
  108.4 0.7 copy-done.13
  109.1 1.4 %pad_maximum_fusion.mine = bf16[4,4,24,1536]{3,2,1,0:T(8,128)(2,1)S(1)} fusion(bf16[1,4,24,1536]{3,2,1,0:T(8,128)(2,1)} %bitcast.48, bf16[1,4,24,1536]{3,2,1,0:T(8,128)(2,1)} %bitcast.49, bf16[1,4,24,1536]{3,2,1,0:T(8,128)(2,1)} %bitcast.50, bf16[1,4,24,1536]{3,2,1,0:T(8,128)(2,1)} %get-tuple-element.36), kind=kLoop, calls=%fused_computation.1 | loop fusion | flops 1769472 | bytes 2359296 | tf_op jit(solution)/shard_map/stack | solution.py:455
  110.5 0.1 collective-permute-start.21
  110.6 2.9 %shard_map.168 = (f32[288,1]{1,0:T(8,128)S(1)}, f32[288,1]{1,0:T(8,128)S(1)}, f32[288,256]{1,0:T(8,128)S(1)}) custom-call(f32[12]{0:T(128)S(1)} %copy-done.10, s32[5]{0:T(128)S(1)} %stack.77.place, f32[96,256]{1,0:T(8,128)S(1)} %get-tuple-element.25.query, bf16[1536,384]{1,0:T(8,128)(2,1)} %bitcast.15.near), custom_call_target="tpu_custom_call" | custom-call | flops 679477248 | bytes 2097152 | tf_op jit(solution)/shard_map/pallas_call | solution.py:89
  113.5 2.2 %shard_map.169.p0 = bf16[96,192]{1,0:T(8,128)(2,1)S(1)} custom-call(f32[12]{0:T(128)S(1)} %copy-done.10, s32[5]{0:T(128)S(1)} %stack.77.place, f32[96,256]{1,0:T(8,128)S(1)} %get-tuple-element.25.query, bf16[1536,384]{1,0:T(8,128)(2,1)S(1)} %collective-permute-done.11.far, f32[288,1]{1,0:T(8,128)S(1)} %get-tuple-element.27.near_highest, ...), custom_call_target="tpu_custom_call" | custom-call | flops 679477248 | bytes 2097152 | tf_op jit(solution)/shard_map/pallas_call | solution.py:89
  115.7 1.5 %collective-permute-start.12 = (bf16[96,192]{1,0:T(8,128)(2,1)S(1)}, bf16[96,192]{1,0:T(8,128)(2,1)S(1)}, u32[]{:S(2)}, u32[]{:S(2)}) collective-permute-start(bf16[96,192]{1,0:T(8,128)(2,1)S(1)} %shard_map.169.p0), channel_id=1, source_target_pairs={{0,32},{32,64},{64,96},{96,0},{1,33},{33,65},{65,97},{97,1},{2,34}... | collective-permute-start | bytes 110600 | tf_op jit(solution)/shard_map/ppermute | solution.py:288
  117.2 0.9 collective-permute-start.13
  118.1 1.9 %collective-permute-start.14 = (bf16[96,192]{1,0:T(8,128)(2,1)S(1)}, bf16[96,192]{1,0:T(8,128)(2,1)S(1)}, u32[]{:S(2)}, u32[]{:S(2)}) collective-permute-start(bf16[96,192]{1,0:T(8,128)(2,1)S(1)} %shard_map.169.p0), channel_id=1, source_target_pairs={{0,96},{32,0},{64,32},{96,64},{1,97},{33,1},{65,33},{97,65},{2,98}... | collective-permute-start | bytes 110600 | tf_op jit(solution)/shard_map/ppermute | solution.py:288
  120.0 1.6 %shard_map.170 = bf16[32,24,1536]{2,1,0:T(8,128)(2,1)S(1)} custom-call(s32[5]{0:T(128)S(1)} %stack.77.place, bf16[4,4,24,1536]{3,2,1,0:T(8,128)(2,1)S(1)} %pad_maximum_fusion.mine, bf16[4,4,24,1536]{3,2,1,0:T(8,128)(2,1)} %collective-permute-done.21.other), custom_call_target="tpu_custom_call" | custom-call | tf_op jit(solution)/shard_map/pallas_call | solution.py:89
  121.6 1.2 collective-permute-done.13.p2
  122.8 1.7 %shard_map.171 = bf16[4,24,768]{2,1,0:T(8,128)(2,1)S(1)} custom-call(s32[5]{0:T(128)S(1)} %stack.77.place, bf16[96,192]{1,0:T(8,128)(2,1)S(1)} %shard_map.169.p0, bf16[96,192]{1,0:T(8,128)(2,1)S(1)} %collective-permute-done.12.p1, bf16[96,192]{1,0:T(8,128)(2,1)S(1)} %collective-permute-done.13.p2, bf16[96,192]{1,0:T(8,128)(2,1)S(1)} %collective-permute-done.14.p3, ...), custom_call_target="tpu_custom_call" | custom-call | flops 452984832 | bytes 5242880 | tf_op jit(solution)/shard_map/pallas_call | solution.py:89
  124.5 1.2 collective-permute-start.22
  125.8 3.0 %collective-permute-start.23 = (bf16[24,768]{1,0:T(8,128)(2,1)S(1)}, bf16[24,768]{1,0:T(8,128)(2,1)S(1)}, u32[]{:S(2)}, u32[]{:S(2)}) collective-permute-start(bf16[24,768]{1,0:T(8,128)(2,1)S(1)} %get-tuple-element.41), channel_id=1, source_target_pairs={{0,64},{32,96},{64,0},{96,32},{1,65},{33,97},{65,1},{97,33},{2,66}... | collective-permute-start | bytes 110600 | tf_op jit(solution)/shard_map/ppermute | solution.py:296
  128.8 0.4 collective-permute-start.24
  129.3 0.9 collective-permute-done.22.u1
  130.2 1.1 collective-permute-done.23.u2
  131.3 1.5 %collective-permute-done.24.u3 = bf16[24,768]{1,0:T(8,128)(2,1)S(1)} collective-permute-done((bf16[24,768]{1,0:T(8,128)(2,1)S(1)}, bf16[24,768]{1,0:T(8,128)(2,1)S(1)}, u32[]{:S(2)}, u32[]{:S(2)}) %collective-permute-start.24) | collective-permute-done | bytes 36896 | tf_op jit(solution)/shard_map/ppermute | solution.py:296
  132.8 1.4 %shard_map.172 = bf16[12,8,768]{2,1,0:T(8,128)(2,1)} custom-call(s32[5]{0:T(128)S(1)} %stack.77.place, bf16[4,24,768]{2,1,0:T(8,128)(2,1)S(1)} %shard_map.165.p0.stream, bf16[24,768]{1,0:T(8,128)(2,1)S(1)} %get-tuple-element.43.u0, bf16[24,768]{1,0:T(8,128)(2,1)S(1)} %collective-permute-done.22.u1, bf16[24,768]{1,0:T(8,128)(2,1)S(1)} %collective-permute-done.23.u2, ...), custom_call_target="tpu_custom_call" | custom-call | flops 18874368 | bytes 1048576 | tf_op jit(solution)/shard_map/pallas_call | solution.py:89
  (49 shorter events, 0.2 us)
Async XLA Ops:
  0.0 19.2 %copy-start = (bf16[1000,768]{1,0:T(8,128)(2,1)S(1)}, bf16[1000,768]{1,0:T(8,128)(2,1)}, u32[]{:S(2)}) copy-start(bf16[1000,768]{1,0:T(8,128)(2,1)} %param.18) | copy-start | bytes 4608004
  0.0 13.8 %copy-start.4 = (bf16[8,12,768]{2,0,1:T(8,128)(2,1)S(1)}, bf16[8,12,768]{2,0,1:T(8,128)(2,1)}, u32[]{:S(2)}) copy-start(bf16[8,12,768]{2,0,1:T(8,128)(2,1)} %param.17) | copy-start | bytes 442372
  0.9 19.0 %copy-start.7 = (f32[1,384]{1,0:T(1,128)S(1)}, f32[1,384]{1,0:T(1,128)}, u32[]{:S(2)}) copy-start(f32[1,384]{1,0:T(1,128)} %constant.91.clone.freqs) | copy-start | bytes 4612
  0.9 19.1 %copy-start.2 = (bf16[768,768]{1,0:T(8,128)(2,1)S(1)}, bf16[768,768]{1,0:T(8,128)(2,1)}, u32[]{:S(2)}) copy-start(bf16[768,768]{1,0:T(8,128)(2,1)} %out_w.4) | copy-start | bytes 3538948
  2.1 36.8 %all-to-all-start = ((bf16[64,24,384]{2,1,0:T(8,128)(2,1)}), bf16[64,24,384]{2,1,0:T(8,128)(2,1)}, u32[]{:S(2)}, u32[]{:S(2)}) async-start(bf16[64,24,384]{2,1,0:T(8,128)(2,1)} %bitcast.47), calls=%async_computation | async-start | bytes 2359296 | tf_op jit(solution)/shard_map/all_to_all | solution.py:313
  13.9 12.8 %collective-permute-start = (bf16[3,8,768]{2,1,0:T(8,128)(2,1)S(1)}, bf16[3,8,768]{2,1,0:T(8,128)(2,1)S(1)}, u32[]{:S(2)}, u32[]{:S(2)}) collective-permute-start(bf16[3,8,768]{2,1,0:T(8,128)(2,1)S(1)} %get-tuple-element.45), channel_id=1, source_target_pairs={{0,1},{1,2},{2,3},{3,4},{4,5},{5,6},{6,7},{8,9},{9,10},{10,11},{11... | collective-permute-start | bytes 110600 | tf_op jit(solution)/shard_map/ppermute | solution.py:283
  17.3 11.3 %collective-permute-start.1 = (bf16[3,8,768]{2,1,0:T(8,128)(2,1)S(1)}, bf16[3,8,768]{2,1,0:T(8,128)(2,1)S(1)}, u32[]{:S(2)}, u32[]{:S(2)}) collective-permute-start(bf16[3,8,768]{2,1,0:T(8,128)(2,1)S(1)} %get-tuple-element.44), channel_id=1, source_target_pairs={{1,0},{2,1},{3,2},{4,3},{5,4},{6,5},{7,6},{9,8},{10,9},{11,10},{12... | collective-permute-start | bytes 110600 | tf_op jit(solution)/shard_map/ppermute | solution.py:283
  20.0 2.0 %copy-start.1 = (bf16[768,2304]{1,0:T(8,128)(2,1)S(1)}, bf16[768,2304]{1,0:T(8,128)(2,1)}, u32[]{:S(2)}) copy-start(bf16[768,2304]{1,0:T(8,128)(2,1)} %qkv.3) | copy-start | bytes 10616836
  22.0 12.9 %copy-start.5 = (s32[96,2]{1,0:T(8,128)S(1)}, s32[96,2]{1,0:T(8,128)}, u32[]{:S(2)}) copy-start(s32[96,2]{1,0:T(8,128)} %constant.93.clone.query_place) | copy-start | bytes 2308
  22.0 12.9 %copy-start.6 = (s32[2,256]{1,0:T(2,128)S(1)}, s32[2,256]{1,0:T(2,128)}, u32[]{:S(2)}) copy-start(s32[2,256]{1,0:T(2,128)} %constant.92.clone.key_place) | copy-start | bytes 6148
  22.0 12.9 %copy-start.8 = (s32[12]{0:T(128)S(1)}, s32[12]{0:T(128)}, u32[]{:S(2)}) copy-start(s32[12]{0:T(128)} %windows.1) | copy-start | bytes 148
  22.0 12.9 %copy-start.9 = (f32[12]{0:T(128)S(1)}, f32[12]{0:T(128)}, u32[]{:S(2)}) copy-start(f32[12]{0:T(128)} %scales.3) | copy-start | bytes 148
  28.7 2.7 %collective-permute-start.2 = (bf16[18,3,768]{2,1,0:T(4,128)(2,1)S(1)}, bf16[18,3,768]{2,1,0:T(4,128)(2,1)S(1)}, u32[]{:S(2)}, u32[]{:S(2)}) collective-permute-start(bf16[18,3,768]{2,1,0:T(4,128)(2,1)S(1)} %get-tuple-element.39), channel_id=1, source_target_pairs={{0,8},{8,16},{16,24},{24,32},{32,40},{40,48},{48,56},{56,64},{64,7... | collective-permute-start | bytes 248840 | tf_op jit(solution)/shard_map/ppermute | solution.py:283
  30.0 4.9 %collective-permute-start.3 = (bf16[18,3,768]{2,1,0:T(4,128)(2,1)S(1)}, bf16[18,3,768]{2,1,0:T(4,128)(2,1)S(1)}, u32[]{:S(2)}, u32[]{:S(2)}) collective-permute-start(bf16[18,3,768]{2,1,0:T(4,128)(2,1)S(1)} %get-tuple-element.38), channel_id=1, source_target_pairs={{8,0},{16,8},{24,16},{32,24},{40,32},{48,40},{56,48},{64,56},{72,6... | collective-permute-start | bytes 248840 | tf_op jit(solution)/shard_map/ppermute | solution.py:283
  38.9 14.8 %collective-permute-start.7 = (bf16[64,24,384]{2,1,0:T(8,128)(2,1)}, bf16[64,24,384]{2,1,0:T(8,128)(2,1)S(1)}, u32[]{:S(2)}, u32[]{:S(2)}) collective-permute-start(bf16[64,24,384]{2,1,0:T(8,128)(2,1)} %all-to-all-done.mine), channel_id=1, source_target_pairs={{0,8},{8,0},{1,9},{9,1},{2,10},{10,2},{3,11},{11,3},{4,12},{12,4},... | collective-permute-start | bytes 3538952 | tf_op jit(solution)/shard_map/ppermute | solution.py:301
  42.4 7.0 %collective-permute-start.4 = (bf16[4,24,768]{2,1,0:T(8,128)(2,1)S(1)}, bf16[4,24,768]{2,1,0:T(8,128)(2,1)S(1)}, u32[]{:S(2)}, u32[]{:S(2)}) collective-permute-start(bf16[4,24,768]{2,1,0:T(8,128)(2,1)S(1)} %shard_map.165.p0.stream), channel_id=1, source_target_pairs={{0,32},{32,64},{64,96},{96,0},{1,33},{33,65},{65,97},{97,1},{2,34}... | collective-permute-start | bytes 442376 | tf_op jit(solution)/shard_map/ppermute | solution.py:288
  43.9 9.9 %collective-permute-start.5 = (bf16[4,24,768]{2,1,0:T(8,128)(2,1)S(1)}, bf16[4,24,768]{2,1,0:T(8,128)(2,1)S(1)}, u32[]{:S(2)}, u32[]{:S(2)}) collective-permute-start(bf16[4,24,768]{2,1,0:T(8,128)(2,1)S(1)} %shard_map.165.p0.stream), channel_id=1, source_target_pairs={{0,64},{32,96},{64,0},{96,32},{1,65},{33,97},{65,1},{97,33},{2,66}... | collective-permute-start | bytes 442376 | tf_op jit(solution)/shard_map/ppermute | solution.py:288
  46.8 7.0 %collective-permute-start.6 = (bf16[4,24,768]{2,1,0:T(8,128)(2,1)S(1)}, bf16[4,24,768]{2,1,0:T(8,128)(2,1)S(1)}, u32[]{:S(2)}, u32[]{:S(2)}) collective-permute-start(bf16[4,24,768]{2,1,0:T(8,128)(2,1)S(1)} %shard_map.165.p0.stream), channel_id=1, source_target_pairs={{0,96},{32,0},{64,32},{96,64},{1,97},{33,1},{65,33},{97,65},{2,98}... | collective-permute-start | bytes 442376 | tf_op jit(solution)/shard_map/ppermute | solution.py:288
  55.8 9.3 %collective-permute-start.8 = (bf16[4,24,384]{2,1,0:T(8,128)(2,1)S(1)}, bf16[4,24,384]{2,1,0:T(8,128)(2,1)S(1)}, u32[]{:S(2)}, u32[]{:S(2)}) collective-permute-start(bf16[4,24,384]{2,1,0:T(8,128)(2,1)S(1)} %shard_map.166.p0), channel_id=1, source_target_pairs={{0,32},{32,64},{64,96},{96,0},{1,33},{33,65},{65,97},{97,1},{2,34}... | collective-permute-start | bytes 221192 | tf_op jit(solution)/shard_map/ppermute | solution.py:288
  57.1 8.0 %collective-permute-start.9 = (bf16[4,24,384]{2,1,0:T(8,128)(2,1)S(1)}, bf16[4,24,384]{2,1,0:T(8,128)(2,1)S(1)}, u32[]{:S(2)}, u32[]{:S(2)}) collective-permute-start(bf16[4,24,384]{2,1,0:T(8,128)(2,1)S(1)} %shard_map.166.p0), channel_id=1, source_target_pairs={{0,64},{32,96},{64,0},{96,32},{1,65},{33,97},{65,1},{97,33},{2,66}... | collective-permute-start | bytes 221192 | tf_op jit(solution)/shard_map/ppermute | solution.py:288
  59.5 5.6 %collective-permute-start.10 = (bf16[4,24,384]{2,1,0:T(8,128)(2,1)S(1)}, bf16[4,24,384]{2,1,0:T(8,128)(2,1)S(1)}, u32[]{:S(2)}, u32[]{:S(2)}) collective-permute-start(bf16[4,24,384]{2,1,0:T(8,128)(2,1)S(1)} %shard_map.166.p0), channel_id=1, source_target_pairs={{0,96},{32,0},{64,32},{96,64},{1,97},{33,1},{65,33},{97,65},{2,98}... | collective-permute-start | bytes 221192 | tf_op jit(solution)/shard_map/ppermute | solution.py:288
  65.1 9.6 %copy-start.14 = (bf16[1536,24]{0,1:T(8,128)(2,1)S(1)}, bf16[1536,24]{0,1:T(8,128)(2,1)}, u32[]{:S(2)}) copy-start(bf16[1536,24]{0,1:T(8,128)(2,1)} %param.29) | copy-start | bytes 221188
  67.5 30.2 %all-to-all-start.1 = ((bf16[16,96,384]{2,1,0:T(8,128)(2,1)}), bf16[16,96,384]{2,1,0:T(8,128)(2,1)}, u32[]{:S(2)}, u32[]{:S(2)}) async-start(bf16[16,96,384]{2,1,0:T(8,128)(2,1)} %get-tuple-element.26), calls=%async_computation.1 | async-start | bytes 2359296 | tf_op jit(solution)/shard_map/all_to_all | solution.py:433
  74.7 35.9 %copy-start.10 = (f32[12]{0:T(128)S(1)}, f32[12]{0:T(128)}, u32[]{:S(2)}) copy-start(f32[12]{0:T(128)} %scales.5) | copy-start | bytes 148
  74.7 15.5 %collective-permute-start.17 = (bf16[24,1536]{1,0:T(8,128)(2,1)S(1)}, bf16[24,1536]{1,0:T(8,128)(2,1)S(1)}, u32[]{:S(2)}, u32[]{:S(2)}) collective-permute-start(bf16[24,1536]{1,0:T(8,128)(2,1)S(1)} %bitcast.51), channel_id=1, source_target_pairs={{0,3},{1,0},{2,1},{3,2},{4,7},{5,4},{6,5},{7,6},{8,11},{9,8},{10,9... | collective-permute-start | bytes 221192 | tf_op jit(solution)/shard_map/ppermute | solution.py:318
  77.8 14.0 %collective-permute-start.16 = (bf16[24,1536]{1,0:T(8,128)(2,1)S(1)}, bf16[24,1536]{1,0:T(8,128)(2,1)S(1)}, u32[]{:S(2)}, u32[]{:S(2)}) collective-permute-start(bf16[24,1536]{1,0:T(8,128)(2,1)S(1)} %bitcast.52), channel_id=1, source_target_pairs={{0,2},{1,3},{2,0},{3,1},{4,6},{5,7},{6,4},{7,5},{8,10},{9,11},{10,... | collective-permute-start | bytes 221192 | tf_op jit(solution)/shard_map/ppermute | solution.py:318
  78.7 13.5 %collective-permute-start.15 = (bf16[24,1536]{1,0:T(8,128)(2,1)S(1)}, bf16[24,1536]{1,0:T(8,128)(2,1)S(1)}, u32[]{:S(2)}, u32[]{:S(2)}) collective-permute-start(bf16[24,1536]{1,0:T(8,128)(2,1)S(1)} %bitcast.53), channel_id=1, source_target_pairs={{0,1},{1,2},{2,3},{3,0},{4,5},{5,6},{6,7},{7,4},{8,9},{9,10},{10,1... | collective-permute-start | bytes 221192 | tf_op jit(solution)/shard_map/ppermute | solution.py:318
  93.0 10.3 %collective-permute-start.20 = (bf16[4,24,1536]{2,1,0:T(8,128)(2,1)S(1)}, bf16[4,24,1536]{2,1,0:T(8,128)(2,1)S(1)}, u32[]{:S(2)}, u32[]{:S(2)}) collective-permute-start(bf16[4,24,1536]{2,1,0:T(8,128)(2,1)S(1)} %get-tuple-element.37), channel_id=1, source_target_pairs={{0,20},{4,16},{16,4},{20,0},{1,21},{5,17},{17,5},{21,1},{2,22},{6,... | collective-permute-start | bytes 884744 | tf_op jit(solution)/shard_map/ppermute | solution.py:324
  95.6 9.6 %collective-permute-start.19 = (bf16[4,24,1536]{2,1,0:T(8,128)(2,1)S(1)}, bf16[4,24,1536]{2,1,0:T(8,128)(2,1)S(1)}, u32[]{:S(2)}, u32[]{:S(2)}) collective-permute-start(bf16[4,24,1536]{2,1,0:T(8,128)(2,1)S(1)} %get-tuple-element.37), channel_id=1, source_target_pairs={{0,16},{4,20},{16,0},{20,4},{1,17},{5,21},{17,1},{21,5},{2,18},{6,... | collective-permute-start | bytes 884744 | tf_op jit(solution)/shard_map/ppermute | solution.py:324
  95.9 12.5 %collective-permute-start.18 = (bf16[4,24,1536]{2,1,0:T(8,128)(2,1)S(1)}, bf16[4,24,1536]{2,1,0:T(8,128)(2,1)S(1)}, u32[]{:S(2)}, u32[]{:S(2)}) collective-permute-start(bf16[4,24,1536]{2,1,0:T(8,128)(2,1)S(1)} %get-tuple-element.37), channel_id=1, source_target_pairs={{0,4},{4,0},{16,20},{20,16},{1,5},{5,1},{17,21},{21,17},{2,6},{6,2... | collective-permute-start | bytes 884744 | tf_op jit(solution)/shard_map/ppermute | solution.py:324
  97.7 15.9 %collective-permute-start.11 = (bf16[1536,384]{1,0:T(8,128)(2,1)}, bf16[1536,384]{1,0:T(8,128)(2,1)S(1)}, u32[]{:S(2)}, u32[]{:S(2)}) collective-permute-start(bf16[1536,384]{1,0:T(8,128)(2,1)} %bitcast.15.near), channel_id=1, source_target_pairs={{0,8},{8,0},{1,9},{9,1},{2,10},{10,2},{3,11},{11,3},{4,12},{12,4},... | collective-permute-start | bytes 3538952 | tf_op jit(solution)/shard_map/ppermute | solution.py:301
  103.2 5.2 %copy-start.11 = (bf16[4,24,1536]{2,1,0:T(8,128)(2,1)}, bf16[4,24,1536]{2,1,0:T(8,128)(2,1)S(1)}, u32[]{:S(2)}) copy-start(bf16[4,24,1536]{2,1,0:T(8,128)(2,1)S(1)} %collective-permute-done.20) | copy-start | bytes 884740
  105.2 3.2 %copy-start.12 = (bf16[4,24,1536]{2,1,0:T(8,128)(2,1)}, bf16[4,24,1536]{2,1,0:T(8,128)(2,1)S(1)}, u32[]{:S(2)}) copy-start(bf16[4,24,1536]{2,1,0:T(8,128)(2,1)S(1)} %collective-permute-done.19) | copy-start | bytes 884740
  108.4 0.7 copy-start.13
  110.5 9.5 %collective-permute-start.21 = (bf16[4,4,24,1536]{3,2,1,0:T(8,128)(2,1)S(1)}, bf16[4,4,24,1536]{3,2,1,0:T(8,128)(2,1)}, u32[]{:S(2)}, u32[]{:S(2)}) collective-permute-start(bf16[4,4,24,1536]{3,2,1,0:T(8,128)(2,1)S(1)} %pad_maximum_fusion.mine), channel_id=1, source_target_pairs={{0,8},{8,0},{1,9},{9,1},{2,10},{10,2},{3,11},{11,3},{4,12},{12,4},... | collective-permute-start | bytes 3538952 | tf_op jit(solution)/shard_map/ppermute | solution.py:301
  115.7 5.9 %collective-permute-start.12 = (bf16[96,192]{1,0:T(8,128)(2,1)S(1)}, bf16[96,192]{1,0:T(8,128)(2,1)S(1)}, u32[]{:S(2)}, u32[]{:S(2)}) collective-permute-start(bf16[96,192]{1,0:T(8,128)(2,1)S(1)} %shard_map.169.p0), channel_id=1, source_target_pairs={{0,32},{32,64},{64,96},{96,0},{1,33},{33,65},{65,97},{97,1},{2,34}... | collective-permute-start | bytes 110600 | tf_op jit(solution)/shard_map/ppermute | solution.py:288
  117.2 5.6 %collective-permute-start.13 = (bf16[96,192]{1,0:T(8,128)(2,1)S(1)}, bf16[96,192]{1,0:T(8,128)(2,1)S(1)}, u32[]{:S(2)}, u32[]{:S(2)}) collective-permute-start(bf16[96,192]{1,0:T(8,128)(2,1)S(1)} %shard_map.169.p0), channel_id=1, source_target_pairs={{0,64},{32,96},{64,0},{96,32},{1,65},{33,97},{65,1},{97,33},{2,66}... | collective-permute-start | bytes 110600 | tf_op jit(solution)/shard_map/ppermute | solution.py:288
  118.1 4.7 %collective-permute-start.14 = (bf16[96,192]{1,0:T(8,128)(2,1)S(1)}, bf16[96,192]{1,0:T(8,128)(2,1)S(1)}, u32[]{:S(2)}, u32[]{:S(2)}) collective-permute-start(bf16[96,192]{1,0:T(8,128)(2,1)S(1)} %shard_map.169.p0), channel_id=1, source_target_pairs={{0,96},{32,0},{64,32},{96,64},{1,97},{33,1},{65,33},{97,65},{2,98}... | collective-permute-start | bytes 110600 | tf_op jit(solution)/shard_map/ppermute | solution.py:288
  120.0 2.8 %copy-start.3 = (bf16[768,1536]{1,0:T(8,128)(2,1)S(1)}, bf16[768,1536]{1,0:T(8,128)(2,1)}, u32[]{:S(2)}) copy-start(bf16[768,1536]{1,0:T(8,128)(2,1)} %out_w.5) | copy-start | bytes 7077892
  122.8 6.4 %copy-start.15 = (f32[768]{0:T(1024)S(1)}, f32[768]{0:T(1024)}, u32[]{:S(2)}) copy-start(f32[768]{0:T(1024)} %param.30) | copy-start | bytes 9220
  124.5 5.6 %collective-permute-start.22 = (bf16[24,768]{1,0:T(8,128)(2,1)S(1)}, bf16[24,768]{1,0:T(8,128)(2,1)S(1)}, u32[]{:S(2)}, u32[]{:S(2)}) collective-permute-start(bf16[24,768]{1,0:T(8,128)(2,1)S(1)} %get-tuple-element.42), channel_id=1, source_target_pairs={{0,32},{32,64},{64,96},{96,0},{1,33},{33,65},{65,97},{97,1},{2,34}... | collective-permute-start | bytes 110600 | tf_op jit(solution)/shard_map/ppermute | solution.py:296
  125.8 5.5 %collective-permute-start.23 = (bf16[24,768]{1,0:T(8,128)(2,1)S(1)}, bf16[24,768]{1,0:T(8,128)(2,1)S(1)}, u32[]{:S(2)}, u32[]{:S(2)}) collective-permute-start(bf16[24,768]{1,0:T(8,128)(2,1)S(1)} %get-tuple-element.41), channel_id=1, source_target_pairs={{0,64},{32,96},{64,0},{96,32},{1,65},{33,97},{65,1},{97,33},{2,66}... | collective-permute-start | bytes 110600 | tf_op jit(solution)/shard_map/ppermute | solution.py:296
  128.8 4.0 %collective-permute-start.24 = (bf16[24,768]{1,0:T(8,128)(2,1)S(1)}, bf16[24,768]{1,0:T(8,128)(2,1)S(1)}, u32[]{:S(2)}, u32[]{:S(2)}) collective-permute-start(bf16[24,768]{1,0:T(8,128)(2,1)S(1)} %get-tuple-element.40), channel_id=1, source_target_pairs={{0,96},{32,0},{64,32},{96,64},{1,97},{33,1},{65,33},{97,65},{2,98}... | collective-permute-start | bytes 110600 | tf_op jit(solution)/shard_map/ppermute | solution.py:296
